TPU v7x, 512 devices: a whole 4x8x8 slice. The times are simulated.
512 devices in a mesh: dp: 32 (over z, x), tensor: 16 (over y, core).
Axes of the slice: x: 4, y: 8, z: 8, core: 2. Of those that a mesh axis runs over, the one named last changes fastest.
Arguments:
- grads_out: bfloat16 [1024, 28672], P('dp'), may hold values from -6 to 6
- inputs: bfloat16 [1024, 8192], P('dp'), may hold values from -6 to 6
- basis_out: bfloat16 [28672, 14336], P('dp', 'tensor'), may hold values from -0.03125 to 0.03125
- basis_in: bfloat16 [8192, 4096], P('tensor', 'dp'), may hold values from -0.0625 to 0.0625
- lengths: int32 [32], P('dp'), may hold values from 1 to 32, as said below
Outputs:
- corrections: float32 [14336, 4096], P('tensor', 'dp')
Inputs may be any that keep to these rules, and one draw needn't show every extreme that they name: `lengths`: every sequence has at least one live token, and some sequence has all 32 slots live.
All inputs are finite; a program needn't handle non-finite values.
Results may differ from a plain program's by a relative error of at most 0.0026.
Values may be sent and summed in bfloat16 or wider, within the bound.
No kernel may reach another device: no remote copies, remote signals or barrier semaphores. Data moves between devices by JAX's collectives and lax.ppermute only.
A program may use at most 64 MiB of HBM per device.

v0:
```python
import jax
import jax.numpy as jnp
from jax import lax
from jax.sharding import PartitionSpec as P


def per_device(grads_out, inputs, basis_out, basis_in, lengths):
    seq_len = grads_out.shape[0]
    positions = jnp.arange(seq_len)
    live = positions[:, None] < lengths[0]
    masked = jnp.where(live, grads_out, jnp.zeros_like(grads_out))
    gathered = lax.all_to_all(masked, "dp", split_axis=1, concat_axis=0, tiled=True)
    partial_sum = jnp.dot(gathered, basis_out, preferred_element_type=jnp.float32)
    rotated = lax.psum(partial_sum, "dp").astype(jnp.bfloat16)
    width_in = inputs.shape[1] // lax.axis_size("tensor")
    column_slab = lax.dynamic_slice_in_dim(inputs, lax.axis_index("tensor") * width_in, width_in, 1)
    partial_in = jnp.dot(
        lax.all_gather(column_slab, "dp", axis=0, tiled=True),
        basis_in,
        preferred_element_type=jnp.float32,
    )
    panel = lax.psum(partial_in, "tensor").astype(jnp.bfloat16)
    row_total = rotated.shape[0]
    sequences = row_total // seq_len
    group_size = 4
    number_of_blocks = sequences // group_size
    rotated_blocks = rotated.reshape(number_of_blocks, group_size, seq_len, rotated.shape[1])
    panel_block_list = panel.reshape(number_of_blocks, group_size, seq_len, panel.shape[1])

    def accumulate(total, pair):
        left_factor, right_factor = pair
        sample_case = jnp.einsum(
            "qjt,qjr->qtr", left_factor, right_factor, preferred_element_type=jnp.float32
        )
        return (total + jnp.sum(sample_case * sample_case, axis=0), None)

    initial_total = jnp.zeros((rotated.shape[1], panel.shape[1]), jnp.float32)
    total, unused = lax.scan(accumulate, initial_total, (rotated_blocks, panel_block_list))
    return total / row_total


def solution(mesh):
    placed = (P("dp", None), P("dp", None), P("dp", "tensor"), P("tensor", "dp"), P("dp"))
    return jax.shard_map(
        per_device, mesh=mesh, in_specs=placed, out_specs=P("tensor", "dp"), check_vma=False
    )
```

profile of v0, /device:TPU:56, one launch (start us, length us, event | category | flops | bytes accessed | tf_op | source)
XLA Modules:
  0.0 363.0 jit_solution(3044291850052730541)
XLA Ops:
  7.3 1.7 broadcast_select_fusion
  9.0 1.4 copy.10
  10.4 13.4 %all-to-all-start = ((bf16[32,32,896]{2,0,1:T(8,128)(2,1)}), bf16[32,32,896]{2,0,1:T(8,128)(2,1)}, u32[]{:S(2)}, u32[]{:S(2)}) async-start(bf16[32,32,896]{2,0,1:T(8,128)(2,1)} %bitcast.19), calls=%async_computation | async-start | bytes 3670016 | tf_op jit(solution)/shard_map/all_to_all | solution.py:12
  23.9 1.4 constant_dynamic-slice_fusion
  25.3 87.8 %all-gather.2.cloned.1.call-done = bf16[1024,512]{1,0:T(8,128)(2,1)} async-done(((bf16[32,512]{1,0:T(8,128)(2,1)}), bf16[1024,512]{1,0:T(8,128)(2,1)}) %all-gather.2.cloned.1.call-update) | async-done | bytes 1048592 | tf_op jit(solution)/shard_map/all_gather | solution.py:18
  113.1 1.7 fusion.6
  114.7 47.8 %all-reduce.3 = bf16[1024,128]{1,0:T(8,128)(2,1)S(1)} all-reduce(f32[1024,128]{1,0:T(8,128)S(1)} %fusion.6), channel_id=1, replica_groups=mesh['dp'=32,'tensor'=16] {'tensor'}, use_global_device_ids=true, to_apply=%region_1.2 | all-reduce | flops 131072 | bytes 786432 | tf_op jit(solution)/shard_map/psum | solution.py:22
  162.6 5.5 %fusion.5 = f32[1024,896]{1,0:T(8,128)} fusion(bf16[1024,896]{1,0:T(8,128)(2,1)} %bitcast.2, bf16[896,896]{1,0:T(8,128)(2,1)S(1)} %copy-done), kind=kOutput, calls=%fused_computation.12 | convolution fusion | flops 1644167168 | bytes 7110656 | tf_op jit(solution)/shard_map/dot_general | solution.py:13
  168.1 174.5 %all-reduce.2 = bf16[1024,896]{1,0:T(8,128)(2,1)} all-reduce(f32[1024,896]{1,0:T(8,128)} %fusion.5), channel_id=1, replica_groups=mesh['dp'=32,'tensor'=16] {'dp'}, use_global_device_ids=true, to_apply=%region_0.1 | all-reduce | flops 917504 | bytes 5505024 | tf_op jit(solution)/shard_map/psum | solution.py:14
  342.6 12.8 %while.11 = (s32[]{:T(128)}, f32[896,128]{1,0:T(8,128)S(1)}, bf16[8,4,32,896]{3,2,1,0:T(8,128)(2,1)}, bf16[8,4,32,128]{3,2,1,0:T(8,128)(2,1)S(1)}, s32[]{:T(128)}, /*index=5*/s32[]{:T(128)}) while((s32[]{:T(128)}, f32[896,128]{1,0:T(8,128)S(1)}, bf16[8,4,32,896]{3,2,1,0:T(8,128)(2,1)}, bf16[8,4,32,128]{3,2,1,0:T(8,128)(2,1)S(1)}, ...), condition=%wide.region_4.5_spmd.clone, body=%wide.region_2.4_spmd.clone.sunk | while | flops 30392320 | bytes 2098263 | solution.py:38
  342.6 1.4 multiply_reduce_fusion.2
  344.0 0.1 select_add_fusion.2
  344.2 1.4 multiply_reduce_fusion.2
  345.6 0.1 select_add_fusion.2
  345.8 1.4 multiply_reduce_fusion.2
  347.2 0.1 select_add_fusion.2
  347.4 1.4 multiply_reduce_fusion.2
  348.8 0.1 select_add_fusion.2
  349.0 1.4 multiply_reduce_fusion.2
  350.4 0.1 select_add_fusion.2
  350.6 1.4 multiply_reduce_fusion.2
  352.2 1.4 multiply_reduce_fusion.2
  353.8 1.4 multiply_reduce_fusion.2
  355.4 0.8 broadcast_multiply_fusion
  (12 shorter events, 0.4 us)
Async XLA Ops:
  6.5 156.0 %copy-start = (bf16[896,896]{1,0:T(8,128)(2,1)S(1)}, bf16[896,896]{1,0:T(8,128)(2,1)}, u32[]{:S(2)}) copy-start(bf16[896,896]{1,0:T(8,128)(2,1)} %param.9) | copy-start | bytes 4816900
  10.4 102.7 %copy-start.1 = (bf16[512,128]{1,0:T(8,128)(2,1)S(1)}, bf16[512,128]{1,0:T(8,128)(2,1)}, u32[]{:S(2)}) copy-start(bf16[512,128]{1,0:T(8,128)(2,1)} %param.10) | copy-start | bytes 393220
  10.4 152.1 %all-to-all-start = ((bf16[32,32,896]{2,0,1:T(8,128)(2,1)}), bf16[32,32,896]{2,0,1:T(8,128)(2,1)}, u32[]{:S(2)}, u32[]{:S(2)}) async-start(bf16[32,32,896]{2,0,1:T(8,128)(2,1)} %bitcast.19), calls=%async_computation | async-start | bytes 3670016 | tf_op jit(solution)/shard_map/all_to_all | solution.py:12
  23.8 89.2 %all-gather.2.cloned.1.call-start = ((), (), s32[]{:S(2)}) async-start(), calls=%async_computation.1 | async-start | bytes 1081344 | tf_op jit(solution)/shard_map/all_gather | solution.py:18
Sparse Core Ops, SparseCore 0:
  27.9 85.1 all-gather.1
where the time goes:
time: 367 us; the launch traced here: 363 us
  blocking collectives  222 us (60%)
  waiting for transfers between devices  87.8 us (24%)
  matrix products  18.8 us (5%)
  between operations  14.2 us (4%)
  starting transfers between devices  13.5 us (4%)
    psum x1, blocking collectives, per_device(): rotated = lax.psum(partial_sum, 'dp').astype(jnp.bfloat16)  174 us
    all_gather x1, waiting for transfers between devices, per_device(): lax.all_gather(column_slab, 'dp', axis=0, tiled=True)  87.8 us
    psum x1, blocking collectives, per_device(): panel = lax.psum(partial_in, 'tensor').astype(jnp.bfloat16)  47.8 us
    all_to_all x1, starting transfers between devices, per_device(): lax.all_to_all(masked, 'dp', split_axis=1, concat_axis=0, tiled=True)  13.4 us
    dot_general x8, matrix products, accumulate(): jnp.einsum('qjt,qjr->qtr', left_factor, right_factor, preferred_element_t...  11.6 us
  transfers between devices with their start and end apart: 2, of which 1 were waited for; matrix products, arithmetic and copies ran while one was open for 1% of the time, Pallas kernels for 0%

commit v1 on v0

v1 whole, which is shorter than its diff:
```python
import functools

import jax
import jax.numpy as jnp
from jax import lax
from jax.experimental import pallas as pl
from jax.experimental.pallas import tpu as pltpu
from jax.sharding import Mesh, PartitionSpec as P

BF = jnp.bfloat16
F32 = jnp.float32
DP = ("z", "x")
TN = ("y", "c")


def exchange(blocks, axis):
    return lax.all_to_all(blocks, axis, split_axis=0, concat_axis=0, tiled=True)


def gather(block, axis):
    count = lax.axis_size(axis)
    return exchange(jnp.broadcast_to(block[None], (count,) + block.shape), axis)


def example_kernel(groups, scale, left_ref, own_ref, other_ref, out_ref):
    rows = left_ref.shape[1]
    lanes = left_ref.shape[2]
    columns = own_ref.shape[-1]
    per_group = lanes // 16
    slot = lax.broadcasted_iota(jnp.int32, (rows, 2 * lanes), 1)
    owner = (slot % lanes) // 16
    total = jnp.zeros((rows, columns), F32)
    for k in range(groups):
        left = jnp.concatenate([left_ref[k], left_ref[groups + k]], axis=1)
        right = jnp.concatenate([own_ref[k], other_ref[k]], axis=0)
        for j in range(per_group):
            picked = jnp.where(owner == j, left, jnp.zeros_like(left))
            one = jnp.dot(picked, right, preferred_element_type=F32)
            total = total + one * one
    total = total * scale
    for q in range(out_ref.shape[0]):
        out_ref[q] = total[:, q * out_ref.shape[2] : (q + 1) * out_ref.shape[2]]


def examples(left, own, other, parts, scale):
    blocks, rows, lanes = left.shape
    columns = own.shape[-1]
    groups = blocks // 2
    return pl.pallas_call(
        functools.partial(example_kernel, groups, scale),
        out_shape=jax.ShapeDtypeStruct((parts, rows, columns // parts), F32),
        compiler_params=pltpu.CompilerParams(vmem_limit_bytes=40 * 1024 * 1024),
        cost_estimate=pl.CostEstimate(
            flops=2 * 32 * 32 * rows * columns, bytes_accessed=2_000_000, transcendentals=0
        ),
    )(left, own, other)


def per_device(grads_out, inputs, basis_out, basis_in, lengths):
    nz, nx, ny, nc = (lax.axis_size(a) for a in ("z", "x", "y", "c"))
    ndp, nt = nz * nx, ny * nc
    core = lax.axis_index("c")
    tensor = lax.axis_index("y") * nc + core
    slots = grads_out.shape[0]
    half = slots // nc
    wide = basis_out.shape[0]
    cols = basis_out.shape[1]

    width_in = basis_in.shape[0]
    slab = lax.dynamic_slice_in_dim(inputs, tensor * width_in, width_in, 1)
    with jax.named_scope("slab_z"):
        slab_z = gather(slab, "z").reshape(nz * slots, width_in)
    with jax.named_scope("basis_x"):
        basis_x = gather(basis_in, "x")

    rows = lax.dynamic_slice_in_dim(grads_out, core * half, half, 0)
    live = (core * half + jnp.arange(half))[:, None] < lengths[0]
    rows = jnp.where(live, rows, jnp.zeros_like(rows))
    blocks = rows.reshape(half, ndp, wide).transpose(1, 0, 2)
    with jax.named_scope("rows_dp"):
        own = exchange(blocks, DP).reshape(ndp * half, wide)
    with jax.named_scope("rows_c"):
        other = lax.ppermute(own, "c", [(0, 1), (1, 0)])

    def rotate(tokens):
        part = lax.dot_general(
            basis_out, tokens, (((0,), (1,)), ((), ())), preferred_element_type=F32
        ).astype(BF)
        part = part.reshape(nx, cols // nx, nz // 2, 128)
        return part.transpose(2, 0, 1, 3)

    parts = jnp.concatenate([rotate(own), rotate(other)], axis=0)
    parts = parts.reshape(ndp, cols // nx, 128)
    with jax.named_scope("sum_dp"):
        parts = exchange(parts, DP)
    rotated = jnp.sum(parts.astype(F32), axis=0).astype(BF)
    with jax.named_scope("rotated_z"):
        rotated = gather(rotated, "z")

    partial_in = lax.dot_general(
        slab_z, basis_x, (((1,), (1,)), ((), ())), preferred_element_type=F32
    ).astype(BF)
    columns = nx * basis_in.shape[1]
    partial_in = partial_in.reshape(nt, nz * slots // nt, columns)
    with jax.named_scope("panel_sum"):
        partial_in = exchange(partial_in, TN)
    piece = jnp.sum(partial_in.astype(F32), axis=0).astype(BF)
    with jax.named_scope("panel_x"):
        piece = gather(piece, "x")
    with jax.named_scope("panel_T"):
        panel = gather(piece, TN)
    panel = panel.reshape(nz, 2, nx, half, columns).transpose(1, 0, 2, 3, 4)
    panel = panel.reshape(2, nz // 2, 128, columns)
    first = lax.dynamic_index_in_dim(panel, core, 0, keepdims=False)
    second = lax.dynamic_index_in_dim(panel, 1 - core, 0, keepdims=False)

    result = examples(rotated, first, second, nx, 1.0 / (ndp * slots))
    with jax.named_scope("out_x"):
        result = exchange(result, "x")
    return result.reshape(cols, result.shape[2])


def solution(mesh):
    fine = Mesh(mesh.devices.reshape(8, 4, 8, 2), ("z", "x", "y", "c"))
    placed = (P(DP, None), P(DP, None), P(DP, TN), P(TN, DP), P(DP))
    return jax.shard_map(
        per_device, mesh=fine, in_specs=placed, out_specs=P(TN, DP), check_vma=False
    )
```

time: 367 us -> 230 us (0.63)
  the two profiles are of different devices: /device:TPU:56 before, /device:TPU:1 now
where the time goes in v1:
time: 230 us; the launch traced here: 229 us
  blocking collectives  84.2 us (37%)
  waiting for transfers between devices  71.2 us (31%)
  starting transfers between devices  40 us (17%)
  local copies, waits for them, and re-layouts  19.9 us (9%)
  matrix products  6.95 us (3%)
  other arithmetic  4.12 us (2%)
    all_to_all x3, blocking collectives, exchange(): return lax.all_to_all(blocks, axis, split_axis=0, concat_axis=0, tiled=True)  84.2 us
    all_to_all x6, waiting for transfers between devices, exchange(): return lax.all_to_all(blocks, axis, split_axis=0, concat_axis=0, tiled=True)  71.2 us
    all_to_all x6, starting transfers between devices, exchange(): return lax.all_to_all(blocks, axis, split_axis=0, concat_axis=0, tiled=True)  34.2 us
    reshape x4, local copies, waits for them, and re-layouts, rotate(): part = part.reshape(nx, cols // nx, nz // 2, 128)  9.77 us
    dot_general x2, matrix products, rotate(): lax.dot_general(basis_out, tokens, (((0,), (1,)), ((), ())), preferred_el...  6.65 us
    ppermute x1, starting transfers between devices, per_device(): other = lax.ppermute(own, 'c', [(0, 1), (1, 0)])  5.82 us
    broadcast_in_dim x5, local copies, waits for them, and re-layouts, gather(): return exchange(jnp.broadcast_to(block[None], (count,) + block.shape), axis)  5.18 us
  transfers between devices with their start and end apart: 7, of which 5 were waited for; matrix products, arithmetic and copies ran while one was open for 11% of the time, Pallas kernels for 0%

profile of v1, /device:TPU:1, one launch (start us, length us, event | category | flops | bytes accessed | tf_op | source)
XLA Modules:
  0.0 229.3 jit_solution(13940364691141457660)
XLA Ops:
  0.0 1.9 broadcast_in_dim.24
  1.9 4.8 %all-to-all-start.4 = ((bf16[4,512,128]{2,1,0:T(8,128)(2,1)}), bf16[4,512,128]{2,1,0:T(8,128)(2,1)S(1)}, u32[]{:S(2)}, u32[]{:S(2)}) async-start(bf16[4,512,128]{2,1,0:T(8,128)(2,1)} %broadcast_in_dim.24), calls=%async_computation.4 | async-start | bytes 1048576 | tf_op jit(solution)/shard_map/basis_x/all_to_all | solution.py:17
  10.2 3.5 %all-to-all-done.4 = bf16[4,512,128]{2,1,0:T(8,128)(2,1)S(1)} async-done(((bf16[4,512,128]{2,1,0:T(8,128)(2,1)}), bf16[4,512,128]{2,1,0:T(8,128)(2,1)S(1)}, u32[]{:S(2)}, u32[]{:S(2)}) %all-to-all-start.4) | async-done | bytes 524320 | tf_op jit(solution)/shard_map/basis_x/all_to_all | solution.py:17
  13.7 12.5 %all-to-all-start = ((bf16[32,16,896]{2,1,0:T(8,128)(2,1)}), bf16[32,16,896]{2,1,0:T(8,128)(2,1)}, u32[]{:S(2)}, u32[]{:S(2)}) async-start(bf16[32,16,896]{2,1,0:T(8,128)(2,1)} %copy.16), calls=%async_computation | async-start | bytes 1835008 | tf_op jit(solution)/shard_map/rows_dp/all_to_all | solution.py:17
  26.9 21.4 %all-to-all-done = bf16[32,16,896]{2,1,0:T(8,128)(2,1)} async-done(((bf16[32,16,896]{2,1,0:T(8,128)(2,1)}), bf16[32,16,896]{2,1,0:T(8,128)(2,1)}, u32[]{:S(2)}, u32[]{:S(2)}) %all-to-all-start) | async-done | bytes 917536 | tf_op jit(solution)/shard_map/rows_dp/all_to_all | solution.py:17
  49.1 4.2 %all-to-all-start.3 = ((bf16[8,32,512]{2,1,0:T(8,128)(2,1)}), bf16[8,32,512]{2,1,0:T(8,128)(2,1)S(1)}, u32[]{:S(2)}, u32[]{:S(2)}) async-start(bf16[8,32,512]{2,1,0:T(8,128)(2,1)} %broadcast_in_dim.23), calls=%async_computation.3 | async-start | bytes 524288 | tf_op jit(solution)/shard_map/slab_z/all_to_all | solution.py:17
  53.3 5.8 %collective-permute-start = (bf16[512,896]{1,0:T(8,128)(2,1)}, bf16[512,896]{1,0:T(8,128)(2,1)}, u32[]{:S(2)}, u32[]{:S(2)}) collective-permute-start(bf16[512,896]{1,0:T(8,128)(2,1)} %bitcast.2), channel_id=1, source_target_pairs={{0,1},{1,0},{2,3},{3,2},{4,5},{5,4},{6,7},{7,6},{8,9},{9,8},{10,11... | collective-permute-start | bytes 2752520 | tf_op jit(solution)/shard_map/rows_c/ppermute | solution.py:83
  59.1 3.6 %all-to-all-done.3 = bf16[8,32,512]{2,1,0:T(8,128)(2,1)S(1)} async-done(((bf16[8,32,512]{2,1,0:T(8,128)(2,1)}), bf16[8,32,512]{2,1,0:T(8,128)(2,1)S(1)}, u32[]{:S(2)}, u32[]{:S(2)}) %all-to-all-start.3) | async-done | bytes 262176 | tf_op jit(solution)/shard_map/slab_z/all_to_all | solution.py:17
  63.4 23.6 %all_to_all.45 = bf16[16,16,512]{2,1,0:T(8,128)(2,1)S(1)} all-to-all(bf16[16,16,512]{2,1,0:T(8,128)(2,1)S(1)} %reshape.47), channel_id=1, replica_groups=mesh['z'=8,'x'=4,'y'=8,'c'=2] {'y','c'}, dimensions={0} | all-to-all | bytes 524288 | tf_op jit(solution)/shard_map/panel_sum/all_to_all | solution.py:17
  87.6 3.5 %all-to-all-start.6 = ((bf16[4,16,512]{2,1,0:T(8,128)(2,1)}), bf16[4,16,512]{2,1,0:T(8,128)(2,1)S(1)}, u32[]{:S(2)}, u32[]{:S(2)}) async-start(bf16[4,16,512]{2,1,0:T(8,128)(2,1)} %broadcast_in_dim.25), calls=%async_computation.6 | async-start | bytes 131072 | tf_op jit(solution)/shard_map/panel_x/all_to_all | solution.py:17
  91.1 3.3 %fusion = bf16[896,512]{0,1:T(8,128)(2,1)} fusion(bf16[512,896]{1,0:T(8,128)(2,1)} %bitcast.2, bf16[896,896]{1,0:T(8,128)(2,1)S(1)} %copy-done), kind=kOutput, calls=%fused_computation.3 | convolution fusion | flops 822542336 | bytes 3440640 | tf_op jit(solution)/shard_map/dot_general | solution.py:86
  94.4 3.0 %reshape.52 = bf16[4,224,4,128]{1,0,3,2:T(4,128)(2,1)S(1)} reshape(bf16[896,512]{0,1:T(8,128)(2,1)} %fusion) | data formatting | bytes 1835008 | tf_op jit(solution)/shard_map/reshape | solution.py:89
  97.5 1.9 copy.22
  99.3 3.3 %fusion.1 = bf16[896,512]{0,1:T(8,128)(2,1)} fusion(bf16[512,896]{1,0:T(8,128)(2,1)} %collective-permute-done, bf16[896,896]{1,0:T(8,128)(2,1)S(1)} %copy-done), kind=kOutput, calls=%fused_computation.4 | convolution fusion | flops 822542336 | bytes 3440640 | tf_op jit(solution)/shard_map/dot_general | solution.py:86
  102.7 3.0 %reshape.53 = bf16[4,224,4,128]{1,0,3,2:T(4,128)(2,1)S(1)} reshape(bf16[896,512]{0,1:T(8,128)(2,1)} %fusion.1) | data formatting | bytes 1835008 | tf_op jit(solution)/shard_map/reshape | solution.py:89
  105.7 1.8 copy.23
  107.6 2.4 %pad_maximum_fusion = bf16[8,4,224,128]{3,0,2,1:T(8,128)(2,1)S(1)} fusion(bf16[4,4,224,128]{3,0,2,1:T(4,128)(2,1)} %bitcast.40, bf16[4,4,224,128]{3,0,2,1:T(4,128)(2,1)} %bitcast.38), kind=kLoop, calls=%fused_computation | loop fusion | flops 3670016 | bytes 3670016 | tf_op jit(solution)/shard_map/concatenate | solution.py:92
  110.3 49.1 %all_to_all.46 = bf16[32,224,128]{2,1,0:T(8,128)(2,1)} all-to-all(bf16[32,224,128]{2,1,0:T(8,128)(2,1)S(1)} %bitcast.36), channel_id=1, replica_groups=mesh['z'=8,'x'=4,'y'=8,'c'=2] {'z','x'}, dimensions={0} | all-to-all | bytes 3670016 | tf_op jit(solution)/shard_map/sum_dp/all_to_all | solution.py:17
  160.5 5.5 %all-to-all-start.7 = ((bf16[16,4,16,512]{3,2,1,0:T(8,128)(2,1)}), bf16[16,4,16,512]{3,2,1,0:T(8,128)(2,1)}, u32[]{:S(2)}, u32[]{:S(2)}) async-start(bf16[16,4,16,512]{3,2,1,0:T(8,128)(2,1)} %broadcast_in_dim.26), calls=%async_computation.7 | async-start | bytes 2097152 | tf_op jit(solution)/shard_map/panel_T/all_to_all | solution.py:17
  166.2 27.8 %all-to-all-done.7 = bf16[16,4,16,512]{3,2,1,0:T(8,128)(2,1)} async-done(((bf16[16,4,16,512]{3,2,1,0:T(8,128)(2,1)}), bf16[16,4,16,512]{3,2,1,0:T(8,128)(2,1)}, u32[]{:S(2)}, u32[]{:S(2)}) %all-to-all-start.7) | async-done | bytes 1048608 | tf_op jit(solution)/shard_map/panel_T/all_to_all | solution.py:17
  194.9 3.7 %all-to-all-start.2 = ((bf16[8,224,128]{2,1,0:T(8,128)(2,1)}), bf16[8,224,128]{2,1,0:T(8,128)(2,1)S(1)}, u32[]{:S(2)}, u32[]{:S(2)}) async-start(bf16[8,224,128]{2,1,0:T(8,128)(2,1)} %broadcast_in_dim.22), calls=%async_computation.2 | async-start | bytes 917504 | tf_op jit(solution)/shard_map/rotated_z/all_to_all | solution.py:17
  200.0 14.8 %all-to-all-done.2.left_ref = bf16[8,224,128]{2,1,0:T(8,128)(2,1)S(1)} async-done(((bf16[8,224,128]{2,1,0:T(8,128)(2,1)}), bf16[8,224,128]{2,1,0:T(8,128)(2,1)S(1)}, u32[]{:S(2)}, u32[]{:S(2)}) %all-to-all-start.2) | async-done | bytes 458784 | tf_op jit(solution)/shard_map/rotated_z/all_to_all | solution.py:17
  214.8 2.1 shard_map.55
  216.9 11.6 %all_to_all.47 = f32[4,224,128]{2,1,0:T(8,128)S(1)} all-to-all(f32[4,224,128]{2,1,0:T(8,128)S(1)} %shard_map.55), channel_id=1, replica_groups=mesh['z'=8,'x'=4,'y'=8,'c'=2] {'x'}, dimensions={0} | all-to-all | bytes 917504 | tf_op jit(solution)/shard_map/out_x/all_to_all | solution.py:17
  (24 shorter events, 10.2 us)
Async XLA Ops:
  0.0 91.1 %copy-start = (bf16[896,896]{1,0:T(8,128)(2,1)S(1)}, bf16[896,896]{1,0:T(8,128)(2,1)}, u32[]{:S(2)}) copy-start(bf16[896,896]{1,0:T(8,128)(2,1)} %param.7) | copy-start | bytes 4816900
  1.9 11.8 %all-to-all-start.4 = ((bf16[4,512,128]{2,1,0:T(8,128)(2,1)}), bf16[4,512,128]{2,1,0:T(8,128)(2,1)S(1)}, u32[]{:S(2)}, u32[]{:S(2)}) async-start(bf16[4,512,128]{2,1,0:T(8,128)(2,1)} %broadcast_in_dim.24), calls=%async_computation.4 | async-start | bytes 1048576 | tf_op jit(solution)/shard_map/basis_x/all_to_all | solution.py:17
  13.7 34.7 %all-to-all-start = ((bf16[32,16,896]{2,1,0:T(8,128)(2,1)}), bf16[32,16,896]{2,1,0:T(8,128)(2,1)}, u32[]{:S(2)}, u32[]{:S(2)}) async-start(bf16[32,16,896]{2,1,0:T(8,128)(2,1)} %copy.16), calls=%async_computation | async-start | bytes 1835008 | tf_op jit(solution)/shard_map/rows_dp/all_to_all | solution.py:17
  49.1 13.7 %all-to-all-start.3 = ((bf16[8,32,512]{2,1,0:T(8,128)(2,1)}), bf16[8,32,512]{2,1,0:T(8,128)(2,1)S(1)}, u32[]{:S(2)}, u32[]{:S(2)}) async-start(bf16[8,32,512]{2,1,0:T(8,128)(2,1)} %broadcast_in_dim.23), calls=%async_computation.3 | async-start | bytes 524288 | tf_op jit(solution)/shard_map/slab_z/all_to_all | solution.py:17
  53.3 46.1 %collective-permute-start = (bf16[512,896]{1,0:T(8,128)(2,1)}, bf16[512,896]{1,0:T(8,128)(2,1)}, u32[]{:S(2)}, u32[]{:S(2)}) collective-permute-start(bf16[512,896]{1,0:T(8,128)(2,1)} %bitcast.2), channel_id=1, source_target_pairs={{0,1},{1,0},{2,3},{3,2},{4,5},{5,4},{6,7},{7,6},{8,9},{9,8},{10,11... | collective-permute-start | bytes 2752520 | tf_op jit(solution)/shard_map/rows_c/ppermute | solution.py:83
  87.6 22.6 %all-to-all-start.6 = ((bf16[4,16,512]{2,1,0:T(8,128)(2,1)}), bf16[4,16,512]{2,1,0:T(8,128)(2,1)S(1)}, u32[]{:S(2)}, u32[]{:S(2)}) async-start(bf16[4,16,512]{2,1,0:T(8,128)(2,1)} %broadcast_in_dim.25), calls=%async_computation.6 | async-start | bytes 131072 | tf_op jit(solution)/shard_map/panel_x/all_to_all | solution.py:17
  159.4 6.6 %copy-start.1 = (bf16[32,224,128]{2,1,0:T(8,128)(2,1)S(1)}, bf16[32,224,128]{2,1,0:T(8,128)(2,1)}, u32[]{:S(2)}) copy-start(bf16[32,224,128]{2,1,0:T(8,128)(2,1)} %all_to_all.46) | copy-start | bytes 5505028
  160.5 33.5 %all-to-all-start.7 = ((bf16[16,4,16,512]{3,2,1,0:T(8,128)(2,1)}), bf16[16,4,16,512]{3,2,1,0:T(8,128)(2,1)}, u32[]{:S(2)}, u32[]{:S(2)}) async-start(bf16[16,4,16,512]{3,2,1,0:T(8,128)(2,1)} %broadcast_in_dim.26), calls=%async_computation.7 | async-start | bytes 2097152 | tf_op jit(solution)/shard_map/panel_T/all_to_all | solution.py:17
  194.9 19.9 %all-to-all-start.2 = ((bf16[8,224,128]{2,1,0:T(8,128)(2,1)}), bf16[8,224,128]{2,1,0:T(8,128)(2,1)S(1)}, u32[]{:S(2)}, u32[]{:S(2)}) async-start(bf16[8,224,128]{2,1,0:T(8,128)(2,1)} %broadcast_in_dim.22), calls=%async_computation.2 | async-start | bytes 917504 | tf_op jit(solution)/shard_map/rotated_z/all_to_all | solution.py:17

commit v2 on v1

v2 whole, which is shorter than its diff:
```python
import functools

import jax
import jax.numpy as jnp
from jax import lax
from jax.experimental import pallas as pl
from jax.experimental.pallas import tpu as pltpu
from jax.sharding import Mesh, PartitionSpec as P

BF = jnp.bfloat16
F32 = jnp.float32
DP = ("z", "x")
TN = ("y", "c")
MIB = 1024 * 1024
PARAMS = pltpu.CompilerParams(vmem_limit_bytes=40 * MIB)
SMEM = pltpu.SMEM
VMEM = pltpu.VMEM


def exchange(blocks, axis):
    return lax.all_to_all(blocks, axis, split_axis=0, concat_axis=0, tiled=True)


def swap(block, axis, bit):
    count = lax.axis_size(axis)
    return lax.ppermute(block, axis, [(i, i ^ bit) for i in range(count)])


def bits(axis):
    count = lax.axis_size(axis)
    return [1 << k for k in range(count.bit_length() - 1)]


def double(block, axis):
    for bit in bits(axis):
        block = jnp.concatenate([block, swap(block, axis, bit)], axis=0)
    return block


def halve(block, axis):
    index = lax.axis_index(axis)
    for bit in reversed(bits(axis)):
        upper = (index // bit) % 2
        kept = lax.dynamic_slice_in_dim(block, upper * bit, bit, 0)
        sent = lax.dynamic_slice_in_dim(block, (1 - upper) * bit, bit, 0)
        block = kept + swap(sent, axis, bit)
    return block


def cost(flops, moved):
    return pl.CostEstimate(flops=flops, bytes_accessed=moved, transcendentals=0)


def split_kernel(half, at_ref, grads_ref, out_ref):
    parts, _, wide = out_ref.shape
    slot = at_ref[0] * half + lax.broadcasted_iota(jnp.int32, (half, wide), 0)
    live = slot < at_ref[1]
    for q in range(parts):
        piece = grads_ref[:, q * wide : (q + 1) * wide]
        out_ref[q] = jnp.where(live, piece, jnp.zeros_like(piece))


def split_rows(grads, at, half, parts, steps=4):
    wide = grads.shape[1] // parts
    each = parts // steps
    return pl.pallas_call(
        functools.partial(split_kernel, half),
        out_shape=jax.ShapeDtypeStruct((parts, half, wide), grads.dtype),
        grid_spec=pltpu.PrefetchScalarGridSpec(
            num_scalar_prefetch=1,
            grid=(steps,),
            in_specs=[pl.BlockSpec((half, each * wide), lambda i, at: (at[0], i))],
            out_specs=pl.BlockSpec((each, half, wide), lambda i, at: (i, 0, 0)),
        ),
        compiler_params=PARAMS,
        cost_estimate=cost(0, 4 * half * grads.shape[1]),
    )(at, grads)


def rotate_kernel(tokens_ref, basis_ref, *rest):
    out_ref = rest[-1]
    product = jnp.dot(tokens_ref[...], basis_ref[...], preferred_element_type=F32)
    lanes = out_ref.shape[2]
    rows = out_ref.shape[1]
    groups = product.shape[0] // lanes
    pieces = product.shape[1] // rows
    for g in range(groups):
        turned = product[g * lanes : (g + 1) * lanes].T.astype(BF)
        for q in range(pieces):
            out_ref[g * pieces + q] = turned[q * rows : (q + 1) * rows]


def rotate(tokens, basis, place, pieces, before=None):
    count, wide = tokens.shape
    columns = basis.shape[1]
    rows = columns // pieces
    blocks = pieces * count // 128
    in_specs = [
        pl.BlockSpec((count, wide), lambda i: (0, 0)),
        pl.BlockSpec((wide, columns), lambda i: (0, 0)),
    ]
    args = [tokens, basis]
    aliases = {}
    if before is not None:
        in_specs.append(pl.BlockSpec(memory_space=pl.ANY))
        args.append(before)
        aliases = {2: 0}
    return pl.pallas_call(
        rotate_kernel,
        out_shape=jax.ShapeDtypeStruct((2 * blocks, rows, 128), BF),
        grid=(1,),
        in_specs=in_specs,
        out_specs=pl.BlockSpec((blocks, rows, 128), lambda i: (place, 0, 0)),
        input_output_aliases=aliases,
        compiler_params=PARAMS,
        cost_estimate=cost(2 * count * wide * columns, 2 * count * (wide + columns)),
    )(*args)


def sum_kernel(parts_ref, out_ref):
    total = parts_ref[0].astype(F32)
    for q in range(1, parts_ref.shape[0]):
        total = total + parts_ref[q].astype(F32)
    total = total.astype(BF)
    for q in range(out_ref.shape[0]):
        out_ref[q] = total


def sum_parts(parts, copies, steps=2):
    count, rows, lanes = parts.shape
    return pl.pallas_call(
        sum_kernel,
        out_shape=jax.ShapeDtypeStruct((copies, rows, lanes), BF),
        grid=(steps,),
        in_specs=[pl.BlockSpec((count, rows // steps, lanes), lambda i: (0, i, 0))],
        out_specs=pl.BlockSpec((copies, rows // steps, lanes), lambda i: (0, i, 0)),
        compiler_params=PARAMS,
        cost_estimate=cost(parts.size, 2 * parts.size),
    )(parts)


def panel_kernel(at_ref, slab_ref, basis_ref, out_ref):
    cores, count, slots, deep = slab_ref.shape
    for q in range(basis_ref.shape[1]):
        total = jnp.zeros((count * slots, basis_ref.shape[3]), F32)
        for r in range(cores):
            left = slab_ref[r].reshape(count * slots, deep)
            right = basis_ref[r, q ^ at_ref[0]]
            total = total + jnp.dot(left, right, preferred_element_type=F32)
        lanes = total.shape[1]
        out_ref[:, :, q * lanes : (q + 1) * lanes] = total.reshape(count, slots, lanes)


def panel_part(at, slab, basis):
    cores, count, slots, deep = slab.shape
    columns = basis.shape[1] * basis.shape[3]
    return pl.pallas_call(
        panel_kernel,
        out_shape=jax.ShapeDtypeStruct((count, slots, columns), F32),
        in_specs=[pl.BlockSpec(memory_space=SMEM)] + [pl.BlockSpec(memory_space=VMEM)] * 2,
        out_specs=pl.BlockSpec(memory_space=VMEM),
        compiler_params=PARAMS,
        cost_estimate=cost(2 * count * slots * columns * deep * cores, 2 * basis.size),
    )(at, slab, basis)


def example_kernel(nx, scale, at_ref, left_ref, own_ref, other_ref, out_ref):
    blocks, rows, lanes = left_ref.shape
    slots, columns = own_ref.shape[2:]
    groups = blocks // 2
    per_group = lanes // slots
    slot = lax.broadcasted_iota(jnp.int32, (rows, 2 * lanes), 1)
    owner = (slot % lanes) // slots
    total = jnp.zeros((rows, columns), F32)
    for k in range(groups):
        left = jnp.concatenate([left_ref[k], left_ref[groups + k]], axis=1)
        places = [divmod(k * per_group + j, nx) for j in range(per_group)]
        places = [(xp ^ at_ref[0], zp ^ at_ref[1]) for zp, xp in places]
        right = jnp.concatenate(
            [own_ref[a, b] for a, b in places] + [other_ref[a, b] for a, b in places], axis=0
        )
        for j in range(per_group):
            picked = jnp.where(owner == j, left, jnp.zeros_like(left))
            one = jnp.dot(picked, right, preferred_element_type=F32)
            total = total + one * one
    total = total * scale
    wide = out_ref.shape[2]
    for q in range(out_ref.shape[0]):
        out_ref[q] = total[:, q * wide : (q + 1) * wide]


def examples(at, left, own, other, nx, scale):
    blocks, rows, lanes = left.shape
    columns = own.shape[-1]
    return pl.pallas_call(
        functools.partial(example_kernel, nx, scale),
        out_shape=jax.ShapeDtypeStruct((nx, rows, columns // nx), F32),
        in_specs=[pl.BlockSpec(memory_space=SMEM)] + [pl.BlockSpec(memory_space=VMEM)] * 3,
        out_specs=pl.BlockSpec(memory_space=VMEM),
        compiler_params=PARAMS,
        cost_estimate=cost(2 * blocks * lanes * rows * columns, 4 * own.size),
    )(at, left, own, other)


def per_device(grads_out, inputs, basis_out, basis_in, lengths):
    nz, nx, ny, nc = (lax.axis_size(a) for a in ("z", "x", "y", "c"))
    iz, ix, iy, ic = (lax.axis_index(a) for a in ("z", "x", "y", "c"))
    slots = grads_out.shape[0]
    half = slots // nc
    wide, columns = basis_out.shape
    deep = basis_in.shape[0]
    at = jnp.stack([ix, iz ^ iy]).astype(jnp.int32)

    blocks = split_rows(grads_out, jnp.stack([ic.astype(jnp.int32), lengths[0]]), half, nz * nx)
    with jax.named_scope("rows_dp"):
        own = exchange(blocks, DP).reshape(nz * nx * half, wide)

    with jax.named_scope("slab_z"):
        mine = lax.dynamic_slice(inputs, (ic * half, (iy * nc + ic) * deep), (half, deep))
        theirs = lax.dynamic_slice(inputs, (ic * half, (iy * nc + 1 - ic) * deep), (half, deep))
        slab = jnp.stack([mine, theirs])[:, None]
        for bit in bits("z"):
            slab = jnp.concatenate([slab, swap(slab, "z", bit)], axis=1)
    with jax.named_scope("basis_xc"):
        basis_x = double(basis_in[None], "x")
        basis_x = jnp.stack([basis_x, swap(basis_x, "c", 1)])
    own, slab, basis_x = lax.optimization_barrier((own, slab, basis_x))
    part_in = panel_part(at, slab, basis_x)
    with jax.named_scope("panel_sum"):
        piece = halve(part_in, "y").astype(BF)
    with jax.named_scope("panel_y"):
        piece = double(piece, "y")
    with jax.named_scope("panel_x"):
        piece = double(piece[None], "x")
    with jax.named_scope("panel_c"):
        piece_other = swap(piece, "c", 1)

    with jax.named_scope("rows_c"):
        other = swap(own, "c", 1)
    parts = rotate(own, basis_out, 0, nx)
    parts = rotate(other, basis_out, 1, nx, parts)
    with jax.named_scope("sum_dp"):
        parts = exchange(parts, DP)
    rotated = sum_parts(parts, nz)
    with jax.named_scope("rotated_z"):
        rotated = exchange(rotated, "z")

    result = examples(at, rotated, piece, piece_other, nx, 1.0 / (nz * nx * slots))
    with jax.named_scope("out_x"):
        result = exchange(result, "x")
    return result.reshape(columns, result.shape[2])


def solution(mesh):
    fine = Mesh(mesh.devices.reshape(8, 4, 8, 2), ("z", "x", "y", "c"))
    placed = (P(DP, None), P(DP, None), P(DP, TN), P(TN, DP), P(DP))
    return jax.shard_map(
        per_device, mesh=fine, in_specs=placed, out_specs=P(TN, DP), check_vma=False
    )
```

time: 230 us -> 182 us (0.79)
  the two profiles are of different devices: /device:TPU:1 before, /device:TPU:56 now
where the time goes in v2:
time: 182 us; the launch traced here: 179 us
  starting transfers between devices  88.9 us (49%)
  waiting for transfers between devices  62.6 us (34%)
  Pallas kernels  12.6 us (7%)
  blocking collectives  10.1 us (6%)
  local copies, waits for them, and re-layouts  3.07 us (2%)
    ppermute x16, starting transfers between devices, swap(): return lax.ppermute(block, axis, [(i, i ^ bit) for i in range(count)])  62.7 us
    ppermute x16, waiting for transfers between devices, swap(): return lax.ppermute(block, axis, [(i, i ^ bit) for i in range(count)])  53.9 us
    all_to_all x3, starting transfers between devices, exchange(): return lax.all_to_all(blocks, axis, split_axis=0, concat_axis=0, tiled=True)  26.2 us
    all_to_all x1, blocking collectives, exchange(): return lax.all_to_all(blocks, axis, split_axis=0, concat_axis=0, tiled=True)  10.1 us
    all_to_all x3, waiting for transfers between devices, exchange(): return lax.all_to_all(blocks, axis, split_axis=0, concat_axis=0, tiled=True)  8.72 us
    pallas_call x2, Pallas kernels, rotate(): pl.pallas_call(rotate_kernel, out_shape=jax.ShapeDtypeStruct((2 * blocks,...  5.74 us
  transfers between devices with their start and end apart: 19, of which 13 were waited for; matrix products, arithmetic and copies ran while one was open for 1% of the time, Pallas kernels for 3%

profile of v2, /device:TPU:56, one launch (start us, length us, event | category | flops | bytes accessed | tf_op | source)
XLA Modules:
  0.0 178.9 jit_solution(3858643795487505410)
XLA Ops:
  4.4 13.3 %all-to-all-start = ((bf16[32,16,896]{2,1,0:T(8,128)(2,1)}), bf16[32,16,896]{2,1,0:T(8,128)(2,1)}, u32[]{:S(2)}, u32[]{:S(2)}) async-start(bf16[32,16,896]{2,1,0:T(8,128)(2,1)} %shard_map.55), calls=%async_computation | async-start | bytes 1835008 | tf_op jit(solution)/shard_map/rows_dp/all_to_all | solution.py:21
  17.7 3.6 %collective-permute-start.3 = (bf16[1,512,128]{2,1,0:T(8,128)(2,1)S(1)}, bf16[1,512,128]{2,1,0:T(8,128)(2,1)S(1)}, u32[]{:S(2)}, u32[]{:S(2)}) collective-permute-start(bf16[1,512,128]{2,1,0:T(8,128)(2,1)S(1)} %bitcast.18), channel_id=1, source_target_pairs={{0,16},{16,0},{32,48},{48,32},{1,17},{17,1},{33,49},{49,33},{2,18}... | collective-permute-start | bytes 393224 | tf_op jit(solution)/shard_map/basis_xc/ppermute | solution.py:26
  21.3 6.5 %collective-permute-done.3 = bf16[1,512,128]{2,1,0:T(8,128)(2,1)S(1)} collective-permute-done((bf16[1,512,128]{2,1,0:T(8,128)(2,1)S(1)}, bf16[1,512,128]{2,1,0:T(8,128)(2,1)S(1)}, u32[]{:S(2)}, u32[]{:S(2)}) %collective-permute-start.3) | collective-permute-done | bytes 131104 | tf_op jit(solution)/shard_map/basis_xc/ppermute | solution.py:26
  27.8 4.4 %collective-permute-start.4 = (bf16[2,512,128]{2,1,0:T(8,128)(2,1)S(1)}, bf16[2,512,128]{2,1,0:T(8,128)(2,1)S(1)}, u32[]{:S(2)}, u32[]{:S(2)}) collective-permute-start(bf16[2,512,128]{2,1,0:T(8,128)(2,1)S(1)} %pad_maximum_fusion.4), channel_id=1, source_target_pairs={{0,32},{16,48},{32,0},{48,16},{1,33},{17,49},{33,1},{49,17},{2,34}... | collective-permute-start | bytes 786440 | tf_op jit(solution)/shard_map/basis_xc/ppermute | solution.py:26
  33.0 4.3 %collective-permute-start = (bf16[2,1,16,512]{3,2,1,0:T(8,128)(2,1)S(1)}, bf16[2,1,16,512]{3,2,1,0:T(8,128)(2,1)S(1)}, u32[]{:S(2)}, u32[]{:S(2)}) collective-permute-start(bf16[2,1,16,512]{3,2,1,0:T(8,128)(2,1)S(1)} %maximum_bitcast_fusion.1), channel_id=1, source_target_pairs={{0,64},{64,0},{128,192},{192,128},{256,320},{320,256},{384,448},{4... | collective-permute-start | bytes 98312 | tf_op jit(solution)/shard_map/slab_z/ppermute | solution.py:26
  37.3 6.1 %collective-permute-done.4 = bf16[2,512,128]{2,1,0:T(8,128)(2,1)S(1)} collective-permute-done((bf16[2,512,128]{2,1,0:T(8,128)(2,1)S(1)}, bf16[2,512,128]{2,1,0:T(8,128)(2,1)S(1)}, u32[]{:S(2)}, u32[]{:S(2)}) %collective-permute-start.4) | collective-permute-done | bytes 262176 | tf_op jit(solution)/shard_map/basis_xc/ppermute | solution.py:26
  45.6 4.6 %collective-permute-start.1 = (bf16[2,2,16,512]{3,2,1,0:T(8,128)(2,1)S(1)}, bf16[2,2,16,512]{3,2,1,0:T(8,128)(2,1)S(1)}, u32[]{:S(2)}, u32[]{:S(2)}) collective-permute-start(bf16[2,2,16,512]{3,2,1,0:T(8,128)(2,1)S(1)} %pad_maximum_fusion.7), channel_id=1, source_target_pairs={{0,128},{64,192},{128,0},{192,64},{256,384},{320,448},{384,256},{4... | collective-permute-start | bytes 196616 | tf_op jit(solution)/shard_map/slab_z/ppermute | solution.py:26
  50.2 3.6 %collective-permute-done.1 = bf16[2,2,16,512]{3,2,1,0:T(8,128)(2,1)S(1)} collective-permute-done((bf16[2,2,16,512]{3,2,1,0:T(8,128)(2,1)S(1)}, bf16[2,2,16,512]{3,2,1,0:T(8,128)(2,1)S(1)}, u32[]{:S(2)}, u32[]{:S(2)}) %collective-permute-start.1) | collective-permute-done | bytes 65568 | tf_op jit(solution)/shard_map/slab_z/ppermute | solution.py:26
  53.8 7.4 %collective-permute-start.2 = (bf16[2,4,16,512]{3,2,1,0:T(8,128)(2,1)S(1)}, bf16[2,4,16,512]{3,2,1,0:T(8,128)(2,1)S(1)}, u32[]{:S(2)}, u32[]{:S(2)}) collective-permute-start(bf16[2,4,16,512]{3,2,1,0:T(8,128)(2,1)S(1)} %pad_maximum_fusion.6), channel_id=1, source_target_pairs={{0,256},{64,320},{128,384},{192,448},{256,0},{320,64},{384,128},{4... | collective-permute-start | bytes 393224 | tf_op jit(solution)/shard_map/slab_z/ppermute | solution.py:26
  61.2 6.7 %collective-permute-done.2 = bf16[2,4,16,512]{3,2,1,0:T(8,128)(2,1)S(1)} collective-permute-done((bf16[2,4,16,512]{3,2,1,0:T(8,128)(2,1)S(1)}, bf16[2,4,16,512]{3,2,1,0:T(8,128)(2,1)S(1)}, u32[]{:S(2)}, u32[]{:S(2)}) %collective-permute-start.2) | collective-permute-done | bytes 131104 | tf_op jit(solution)/shard_map/slab_z/ppermute | solution.py:26
  70.0 3.4 %shard_map.56.rest_0_ = bf16[32,224,128]{2,1,0:T(8,128)(2,1)} custom-call(bf16[512,896]{1,0:T(8,128)(2,1)} %bitcast.3.tokens_ref, bf16[896,896]{1,0:T(8,128)(2,1)S(1)} %copy-done), custom_call_target="tpu_custom_call" | custom-call | flops 822083584 | bytes 1835008 | tf_op jit(solution)/shard_map/pallas_call | solution.py:108
  75.8 6.2 %all-to-all-start.1 = ((bf16[32,224,128]{2,1,0:T(8,128)(2,1)}), bf16[32,224,128]{2,1,0:T(8,128)(2,1)S(1)}, u32[]{:S(2)}, u32[]{:S(2)}) async-start(bf16[32,224,128]{2,1,0:T(8,128)(2,1)} %shard_map.57), calls=%async_computation.1 | async-start | bytes 3670016 | tf_op jit(solution)/shard_map/sum_dp/all_to_all | solution.py:21
  83.1 4.7 %collective-permute-start.7 = (f32[4,16,512]{2,1,0:T(8,128)S(1)}, f32[4,16,512]{2,1,0:T(8,128)S(1)}, u32[]{:S(2)}, u32[]{:S(2)}) collective-permute-start(f32[4,16,512]{2,1,0:T(8,128)S(1)} %constant_dynamic-slice_fusion.2), channel_id=1, source_target_pairs={{0,8},{2,10},{4,12},{6,14},{8,0},{10,2},{12,4},{14,6},{1,9},{3,11}... | collective-permute-start | bytes 393224 | tf_op jit(solution)/shard_map/panel_sum/ppermute | solution.py:26
  87.9 9.1 %collective-permute-done.7 = f32[4,16,512]{2,1,0:T(8,128)S(1)} collective-permute-done((f32[4,16,512]{2,1,0:T(8,128)S(1)}, f32[4,16,512]{2,1,0:T(8,128)S(1)}, u32[]{:S(2)}, u32[]{:S(2)}) %collective-permute-start.7) | collective-permute-done | bytes 131104 | tf_op jit(solution)/shard_map/panel_sum/ppermute | solution.py:26
  97.0 4.4 %collective-permute-start.8 = (f32[2,16,512]{2,1,0:T(8,128)S(1)}, f32[2,16,512]{2,1,0:T(8,128)S(1)}, u32[]{:S(2)}, u32[]{:S(2)}) collective-permute-start(f32[2,16,512]{2,1,0:T(8,128)S(1)} %constant_dynamic-slice_fusion.1), channel_id=1, source_target_pairs={{0,4},{2,6},{4,0},{6,2},{8,12},{10,14},{12,8},{14,10},{1,5},{3,7},... | collective-permute-start | bytes 196616 | tf_op jit(solution)/shard_map/panel_sum/ppermute | solution.py:26
  104.3 3.3 %collective-permute-start.9 = (f32[1,16,512]{2,1,0:T(8,128)S(1)}, f32[1,16,512]{2,1,0:T(8,128)S(1)}, u32[]{:S(2)}, u32[]{:S(2)}) collective-permute-start(f32[1,16,512]{2,1,0:T(8,128)S(1)} %constant_dynamic-slice_fusion), channel_id=1, source_target_pairs={{0,2},{2,0},{4,6},{6,4},{8,10},{10,8},{12,14},{14,12},{1,3},{3,1},... | collective-permute-start | bytes 98312 | tf_op jit(solution)/shard_map/panel_sum/ppermute | solution.py:26
  115.7 4.4 %collective-permute-start.11 = (bf16[2,16,512]{2,1,0:T(8,128)(2,1)S(1)}, bf16[2,16,512]{2,1,0:T(8,128)(2,1)S(1)}, u32[]{:S(2)}, u32[]{:S(2)}) collective-permute-start(bf16[2,16,512]{2,1,0:T(8,128)(2,1)S(1)} %pad_maximum_fusion.9), channel_id=1, source_target_pairs={{0,4},{2,6},{4,0},{6,2},{8,12},{10,14},{12,8},{14,10},{1,5},{3,7},... | collective-permute-start | bytes 98312 | tf_op jit(solution)/shard_map/panel_y/ppermute | solution.py:26
  122.4 5.3 %collective-permute-start.12 = (bf16[4,16,512]{2,1,0:T(8,128)(2,1)S(1)}, bf16[4,16,512]{2,1,0:T(8,128)(2,1)S(1)}, u32[]{:S(2)}, u32[]{:S(2)}) collective-permute-start(bf16[4,16,512]{2,1,0:T(8,128)(2,1)S(1)} %pad_maximum_fusion.8), channel_id=1, source_target_pairs={{0,8},{2,10},{4,12},{6,14},{8,0},{10,2},{12,4},{14,6},{1,9},{3,11}... | collective-permute-start | bytes 196616 | tf_op jit(solution)/shard_map/panel_y/ppermute | solution.py:26
  127.8 5.4 %collective-permute-done.12 = bf16[4,16,512]{2,1,0:T(8,128)(2,1)S(1)} collective-permute-done((bf16[4,16,512]{2,1,0:T(8,128)(2,1)S(1)}, bf16[4,16,512]{2,1,0:T(8,128)(2,1)S(1)}, u32[]{:S(2)}, u32[]{:S(2)}) %collective-permute-start.12) | collective-permute-done | bytes 65568 | tf_op jit(solution)/shard_map/panel_y/ppermute | solution.py:26
  135.9 4.8 %collective-permute-done.13 = bf16[1,8,16,512]{3,2,1,0:T(8,128)(2,1)S(1)} collective-permute-done((bf16[1,8,16,512]{3,2,1,0:T(8,128)(2,1)S(1)}, bf16[1,8,16,512]{3,2,1,0:T(8,128)(2,1)S(1)}, u32[]{:S(2)}, u32[]{:S(2)}) %collective-permute-start.13) | collective-permute-done | bytes 131104 | tf_op jit(solution)/shard_map/panel_x/ppermute | solution.py:26
  140.7 4.3 %collective-permute-start.14 = (bf16[2,8,16,512]{3,2,1,0:T(8,128)(2,1)S(1)}, bf16[2,8,16,512]{3,2,1,0:T(8,128)(2,1)S(1)}, u32[]{:S(2)}, u32[]{:S(2)}) collective-permute-start(bf16[2,8,16,512]{3,2,1,0:T(8,128)(2,1)S(1)} %pad_maximum_fusion.5), channel_id=1, source_target_pairs={{0,32},{16,48},{32,0},{48,16},{1,33},{17,49},{33,1},{49,17},{2,34}... | collective-permute-start | bytes 786440 | tf_op jit(solution)/shard_map/panel_x/ppermute | solution.py:26
  146.2 6.7 %all-to-all-start.2 = ((bf16[8,224,128]{2,1,0:T(8,128)(2,1)}), bf16[8,224,128]{2,1,0:T(8,128)(2,1)S(1)}, u32[]{:S(2)}, u32[]{:S(2)}) async-start(bf16[8,224,128]{2,1,0:T(8,128)(2,1)} %shard_map.58), calls=%async_computation.2 | async-start | bytes 917504 | tf_op jit(solution)/shard_map/rotated_z/all_to_all | solution.py:21
  156.7 8.7 %all-to-all-done.2.left_ref = bf16[8,224,128]{2,1,0:T(8,128)(2,1)S(1)} async-done(((bf16[8,224,128]{2,1,0:T(8,128)(2,1)}), bf16[8,224,128]{2,1,0:T(8,128)(2,1)S(1)}, u32[]{:S(2)}, u32[]{:S(2)}) %all-to-all-start.2) | async-done | bytes 458784 | tf_op jit(solution)/shard_map/rotated_z/all_to_all | solution.py:21
  168.1 10.1 %all_to_all.20 = f32[4,224,128]{2,1,0:T(8,128)S(1)} all-to-all(f32[4,224,128]{2,1,0:T(8,128)S(1)} %shard_map.60), channel_id=1, replica_groups=mesh['z'=8,'x'=4,'y'=8,'c'=2] {'x'}, dimensions={0} | all-to-all | bytes 917504 | tf_op jit(solution)/shard_map/out_x/all_to_all | solution.py:21
  (49 shorter events, 36.4 us)
Async XLA Ops:
  0.7 1.5 copy-start.1
  2.2 15.4 %copy-start.2 = (bf16[512,128]{1,0:T(8,128)(2,1)S(1)}, bf16[512,128]{1,0:T(8,128)(2,1)}, u32[]{:S(2)}) copy-start(bf16[512,128]{1,0:T(8,128)(2,1)} %param.8) | copy-start | bytes 393220
  4.4 63.7 %all-to-all-start = ((bf16[32,16,896]{2,1,0:T(8,128)(2,1)}), bf16[32,16,896]{2,1,0:T(8,128)(2,1)}, u32[]{:S(2)}, u32[]{:S(2)}) async-start(bf16[32,16,896]{2,1,0:T(8,128)(2,1)} %shard_map.55), calls=%async_computation | async-start | bytes 1835008 | tf_op jit(solution)/shard_map/rows_dp/all_to_all | solution.py:21
  17.7 10.1 %collective-permute-start.3 = (bf16[1,512,128]{2,1,0:T(8,128)(2,1)S(1)}, bf16[1,512,128]{2,1,0:T(8,128)(2,1)S(1)}, u32[]{:S(2)}, u32[]{:S(2)}) collective-permute-start(bf16[1,512,128]{2,1,0:T(8,128)(2,1)S(1)} %bitcast.18), channel_id=1, source_target_pairs={{0,16},{16,0},{32,48},{48,32},{1,17},{17,1},{33,49},{49,33},{2,18}... | collective-permute-start | bytes 393224 | tf_op jit(solution)/shard_map/basis_xc/ppermute | solution.py:26
  27.8 15.6 %collective-permute-start.4 = (bf16[2,512,128]{2,1,0:T(8,128)(2,1)S(1)}, bf16[2,512,128]{2,1,0:T(8,128)(2,1)S(1)}, u32[]{:S(2)}, u32[]{:S(2)}) collective-permute-start(bf16[2,512,128]{2,1,0:T(8,128)(2,1)S(1)} %pad_maximum_fusion.4), channel_id=1, source_target_pairs={{0,32},{16,48},{32,0},{48,16},{1,33},{17,49},{33,1},{49,17},{2,34}... | collective-permute-start | bytes 786440 | tf_op jit(solution)/shard_map/basis_xc/ppermute | solution.py:26
  33.0 12.6 %collective-permute-start = (bf16[2,1,16,512]{3,2,1,0:T(8,128)(2,1)S(1)}, bf16[2,1,16,512]{3,2,1,0:T(8,128)(2,1)S(1)}, u32[]{:S(2)}, u32[]{:S(2)}) collective-permute-start(bf16[2,1,16,512]{3,2,1,0:T(8,128)(2,1)S(1)} %maximum_bitcast_fusion.1), channel_id=1, source_target_pairs={{0,64},{64,0},{128,192},{192,128},{256,320},{320,256},{384,448},{4... | collective-permute-start | bytes 98312 | tf_op jit(solution)/shard_map/slab_z/ppermute | solution.py:26
  43.5 26.6 %copy-start = (bf16[896,896]{1,0:T(8,128)(2,1)S(1)}, bf16[896,896]{1,0:T(8,128)(2,1)}, u32[]{:S(2)}) copy-start(bf16[896,896]{1,0:T(8,128)(2,1)} %basis_ref.3) | copy-start | bytes 4816900
  43.5 24.5 %collective-permute-start.5 = (bf16[4,512,128]{2,1,0:T(8,128)(2,1)S(1)}, bf16[4,512,128]{2,1,0:T(8,128)(2,1)S(1)}, u32[]{:S(2)}, u32[]{:S(2)}) collective-permute-start(bf16[4,512,128]{2,1,0:T(8,128)(2,1)S(1)} %get-tuple-element.12), channel_id=1, source_target_pairs={{0,1},{1,0},{2,3},{3,2},{4,5},{5,4},{6,7},{7,6},{8,9},{9,8},{10,11... | collective-permute-start | bytes 1572872 | tf_op jit(solution)/shard_map/basis_xc/ppermute | solution.py:26
  45.6 8.2 %collective-permute-start.1 = (bf16[2,2,16,512]{3,2,1,0:T(8,128)(2,1)S(1)}, bf16[2,2,16,512]{3,2,1,0:T(8,128)(2,1)S(1)}, u32[]{:S(2)}, u32[]{:S(2)}) collective-permute-start(bf16[2,2,16,512]{3,2,1,0:T(8,128)(2,1)S(1)} %pad_maximum_fusion.7), channel_id=1, source_target_pairs={{0,128},{64,192},{128,0},{192,64},{256,384},{320,448},{384,256},{4... | collective-permute-start | bytes 196616 | tf_op jit(solution)/shard_map/slab_z/ppermute | solution.py:26
  53.8 14.1 %collective-permute-start.2 = (bf16[2,4,16,512]{3,2,1,0:T(8,128)(2,1)S(1)}, bf16[2,4,16,512]{3,2,1,0:T(8,128)(2,1)S(1)}, u32[]{:S(2)}, u32[]{:S(2)}) collective-permute-start(bf16[2,4,16,512]{3,2,1,0:T(8,128)(2,1)S(1)} %pad_maximum_fusion.6), channel_id=1, source_target_pairs={{0,256},{64,320},{128,384},{192,448},{256,0},{320,64},{384,128},{4... | collective-permute-start | bytes 393224 | tf_op jit(solution)/shard_map/slab_z/ppermute | solution.py:26
  68.1 5.4 %collective-permute-start.6 = (bf16[512,896]{1,0:T(8,128)(2,1)}, bf16[512,896]{1,0:T(8,128)(2,1)S(1)}, u32[]{:S(2)}, u32[]{:S(2)}) collective-permute-start(bf16[512,896]{1,0:T(8,128)(2,1)} %bitcast.3.tokens_ref), channel_id=1, source_target_pairs={{0,1},{1,0},{2,3},{3,2},{4,5},{5,4},{6,7},{7,6},{8,9},{9,8},{10,11... | collective-permute-start | bytes 2752520 | tf_op jit(solution)/shard_map/rows_c/ppermute | solution.py:26
  75.8 69.3 %all-to-all-start.1 = ((bf16[32,224,128]{2,1,0:T(8,128)(2,1)}), bf16[32,224,128]{2,1,0:T(8,128)(2,1)S(1)}, u32[]{:S(2)}, u32[]{:S(2)}) async-start(bf16[32,224,128]{2,1,0:T(8,128)(2,1)} %shard_map.57), calls=%async_computation.1 | async-start | bytes 3670016 | tf_op jit(solution)/shard_map/sum_dp/all_to_all | solution.py:21
  83.1 13.9 %collective-permute-start.7 = (f32[4,16,512]{2,1,0:T(8,128)S(1)}, f32[4,16,512]{2,1,0:T(8,128)S(1)}, u32[]{:S(2)}, u32[]{:S(2)}) collective-permute-start(f32[4,16,512]{2,1,0:T(8,128)S(1)} %constant_dynamic-slice_fusion.2), channel_id=1, source_target_pairs={{0,8},{2,10},{4,12},{6,14},{8,0},{10,2},{12,4},{14,6},{1,9},{3,11}... | collective-permute-start | bytes 393224 | tf_op jit(solution)/shard_map/panel_sum/ppermute | solution.py:26
  97.0 7.2 %collective-permute-start.8 = (f32[2,16,512]{2,1,0:T(8,128)S(1)}, f32[2,16,512]{2,1,0:T(8,128)S(1)}, u32[]{:S(2)}, u32[]{:S(2)}) collective-permute-start(f32[2,16,512]{2,1,0:T(8,128)S(1)} %constant_dynamic-slice_fusion.1), channel_id=1, source_target_pairs={{0,4},{2,6},{4,0},{6,2},{8,12},{10,14},{12,8},{14,10},{1,5},{3,7},... | collective-permute-start | bytes 196616 | tf_op jit(solution)/shard_map/panel_sum/ppermute | solution.py:26
  104.3 5.8 %collective-permute-start.9 = (f32[1,16,512]{2,1,0:T(8,128)S(1)}, f32[1,16,512]{2,1,0:T(8,128)S(1)}, u32[]{:S(2)}, u32[]{:S(2)}) collective-permute-start(f32[1,16,512]{2,1,0:T(8,128)S(1)} %constant_dynamic-slice_fusion), channel_id=1, source_target_pairs={{0,2},{2,0},{4,6},{6,4},{8,10},{10,8},{12,14},{14,12},{1,3},{3,1},... | collective-permute-start | bytes 98312 | tf_op jit(solution)/shard_map/panel_sum/ppermute | solution.py:26
  110.1 5.6 %collective-permute-start.10 = (bf16[1,16,512]{2,1,0:T(8,128)(2,1)S(1)}, bf16[1,16,512]{2,1,0:T(8,128)(2,1)S(1)}, u32[]{:S(2)}, u32[]{:S(2)}) collective-permute-start(bf16[1,16,512]{2,1,0:T(8,128)(2,1)S(1)} %add_convert_fusion), channel_id=1, source_target_pairs={{0,2},{2,0},{4,6},{6,4},{8,10},{10,8},{12,14},{14,12},{1,3},{3,1},... | collective-permute-start | bytes 49160 | tf_op jit(solution)/shard_map/panel_y/ppermute | solution.py:26
  115.7 6.7 %collective-permute-start.11 = (bf16[2,16,512]{2,1,0:T(8,128)(2,1)S(1)}, bf16[2,16,512]{2,1,0:T(8,128)(2,1)S(1)}, u32[]{:S(2)}, u32[]{:S(2)}) collective-permute-start(bf16[2,16,512]{2,1,0:T(8,128)(2,1)S(1)} %pad_maximum_fusion.9), channel_id=1, source_target_pairs={{0,4},{2,6},{4,0},{6,2},{8,12},{10,14},{12,8},{14,10},{1,5},{3,7},... | collective-permute-start | bytes 98312 | tf_op jit(solution)/shard_map/panel_y/ppermute | solution.py:26
  122.4 10.8 %collective-permute-start.12 = (bf16[4,16,512]{2,1,0:T(8,128)(2,1)S(1)}, bf16[4,16,512]{2,1,0:T(8,128)(2,1)S(1)}, u32[]{:S(2)}, u32[]{:S(2)}) collective-permute-start(bf16[4,16,512]{2,1,0:T(8,128)(2,1)S(1)} %pad_maximum_fusion.8), channel_id=1, source_target_pairs={{0,8},{2,10},{4,12},{6,14},{8,0},{10,2},{12,4},{14,6},{1,9},{3,11}... | collective-permute-start | bytes 196616 | tf_op jit(solution)/shard_map/panel_y/ppermute | solution.py:26
  133.2 7.4 %collective-permute-start.13 = (bf16[1,8,16,512]{3,2,1,0:T(8,128)(2,1)S(1)}, bf16[1,8,16,512]{3,2,1,0:T(8,128)(2,1)S(1)}, u32[]{:S(2)}, u32[]{:S(2)}) collective-permute-start(bf16[1,8,16,512]{3,2,1,0:T(8,128)(2,1)S(1)} %maximum_bitcast_fusion), channel_id=1, source_target_pairs={{0,16},{16,0},{32,48},{48,32},{1,17},{17,1},{33,49},{49,33},{2,18}... | collective-permute-start | bytes 393224 | tf_op jit(solution)/shard_map/panel_x/ppermute | solution.py:26
  140.7 12.1 %collective-permute-start.14 = (bf16[2,8,16,512]{3,2,1,0:T(8,128)(2,1)S(1)}, bf16[2,8,16,512]{3,2,1,0:T(8,128)(2,1)S(1)}, u32[]{:S(2)}, u32[]{:S(2)}) collective-permute-start(bf16[2,8,16,512]{3,2,1,0:T(8,128)(2,1)S(1)} %pad_maximum_fusion.5), channel_id=1, source_target_pairs={{0,32},{16,48},{32,0},{48,16},{1,33},{17,49},{33,1},{49,17},{2,34}... | collective-permute-start | bytes 786440 | tf_op jit(solution)/shard_map/panel_x/ppermute | solution.py:26
  146.2 19.2 %all-to-all-start.2 = ((bf16[8,224,128]{2,1,0:T(8,128)(2,1)}), bf16[8,224,128]{2,1,0:T(8,128)(2,1)S(1)}, u32[]{:S(2)}, u32[]{:S(2)}) async-start(bf16[8,224,128]{2,1,0:T(8,128)(2,1)} %shard_map.58), calls=%async_computation.2 | async-start | bytes 917504 | tf_op jit(solution)/shard_map/rotated_z/all_to_all | solution.py:21
  152.9 3.8 %collective-permute-start.15 = (bf16[4,8,16,512]{3,2,1,0:T(8,128)(2,1)S(1)}, bf16[4,8,16,512]{3,2,1,0:T(8,128)(2,1)S(1)}, u32[]{:S(2)}, u32[]{:S(2)}) collective-permute-start(bf16[4,8,16,512]{3,2,1,0:T(8,128)(2,1)S(1)} %pad_maximum_fusion.2.own_ref), channel_id=1, source_target_pairs={{0,1},{1,0},{2,3},{3,2},{4,5},{5,4},{6,7},{7,6},{8,9},{9,8},{10,11... | collective-permute-start | bytes 1572872 | tf_op jit(solution)/shard_map/panel_c/ppermute | solution.py:26

commit v3 on v2

--- a/solution.py
+++ b/solution.py
@@ -28,7 +28,14 @@
 
 def bits(axis):
     count = lax.axis_size(axis)
-    return [1 << k for k in range(count.bit_length() - 1)]
+    return [1 << k for k in reversed(range(count.bit_length() - 1))]
+
+
+def reverse(index, width):
+    result = 0
+    for k in range(width):
+        result = result | (((index >> k) & 1) << (width - 1 - k))
+    return result
 
 
 def double(block, axis):
@@ -37,13 +44,9 @@
     return block
 
 
-def halve(block, axis):
-    index = lax.axis_index(axis)
+def total_over(block, axis):
     for bit in reversed(bits(axis)):
-        upper = (index // bit) % 2
-        kept = lax.dynamic_slice_in_dim(block, upper * bit, bit, 0)
-        sent = lax.dynamic_slice_in_dim(block, (1 - upper) * bit, bit, 0)
-        block = kept + swap(sent, axis, bit)
+        block = block + swap(block.astype(BF), axis, bit).astype(F32)
     return block
 
 
@@ -72,7 +75,7 @@
             in_specs=[pl.BlockSpec((half, each * wide), lambda i, at: (at[0], i))],
             out_specs=pl.BlockSpec((each, half, wide), lambda i, at: (i, 0, 0)),
         ),
-        compiler_params=PARAMS,
+        compiler_params=pltpu.CompilerParams(vmem_limit_bytes=58 * MIB),
         cost_estimate=cost(0, 4 * half * grads.shape[1]),
     )(at, grads)
 
@@ -145,7 +148,7 @@
         total = jnp.zeros((count * slots, basis_ref.shape[3]), F32)
         for r in range(cores):
             left = slab_ref[r].reshape(count * slots, deep)
-            right = basis_ref[r, q ^ at_ref[0]]
+            right = basis_ref[r, reverse(q ^ at_ref[0], 2)]
             total = total + jnp.dot(left, right, preferred_element_type=F32)
         lanes = total.shape[1]
         out_ref[:, :, q * lanes : (q + 1) * lanes] = total.reshape(count, slots, lanes)
@@ -175,7 +178,7 @@
     for k in range(groups):
         left = jnp.concatenate([left_ref[k], left_ref[groups + k]], axis=1)
         places = [divmod(k * per_group + j, nx) for j in range(per_group)]
-        places = [(xp ^ at_ref[0], zp ^ at_ref[1]) for zp, xp in places]
+        places = [(reverse(xp ^ at_ref[0], 2), reverse(zp ^ at_ref[1], 3)) for zp, xp in places]
         right = jnp.concatenate(
             [own_ref[a, b] for a, b in places] + [other_ref[a, b] for a, b in places], axis=0
         )
@@ -209,27 +212,33 @@
     half = slots // nc
     wide, columns = basis_out.shape
     deep = basis_in.shape[0]
-    at = jnp.stack([ix, iz ^ iy]).astype(jnp.int32)
+    at = jnp.stack([ix, iz]).astype(jnp.int32)
 
     blocks = split_rows(grads_out, jnp.stack([ic.astype(jnp.int32), lengths[0]]), half, nz * nx)
     with jax.named_scope("rows_dp"):
         own = exchange(blocks, DP).reshape(nz * nx * half, wide)
 
-    with jax.named_scope("slab_z"):
-        mine = lax.dynamic_slice(inputs, (ic * half, (iy * nc + ic) * deep), (half, deep))
-        theirs = lax.dynamic_slice(inputs, (ic * half, (iy * nc + 1 - ic) * deep), (half, deep))
-        slab = jnp.stack([mine, theirs])[:, None]
+    mine = lax.dynamic_slice(inputs, (ic * half, (iy * nc + ic) * deep), (half, deep))
+    theirs = lax.dynamic_slice(inputs, (ic * half, (iy * nc + 1 - ic) * deep), (half, deep))
+    slab = jnp.stack([mine, theirs])[:, None]
+    basis_x = basis_in[None]
+    with jax.named_scope("panel_gather"):
         for bit in bits("z"):
-            slab = jnp.concatenate([slab, swap(slab, "z", bit)], axis=1)
-    with jax.named_scope("basis_xc"):
-        basis_x = double(basis_in[None], "x")
-        basis_x = jnp.stack([basis_x, swap(basis_x, "c", 1)])
+            more_slab = swap(slab, "z", bit)
+            if bit > 1:
+                more_basis = swap(basis_x, "x", bit // 2)
+            else:
+                more_basis = swap(basis_x, "c", 1)
+            more_slab, more_basis = lax.optimization_barrier((more_slab, more_basis))
+            slab = jnp.concatenate([slab, more_slab], axis=1)
+            if bit > 1:
+                basis_x = jnp.concatenate([basis_x, more_basis], axis=0)
+            else:
+                basis_x = jnp.stack([basis_x, more_basis])
     own, slab, basis_x = lax.optimization_barrier((own, slab, basis_x))
     part_in = panel_part(at, slab, basis_x)
     with jax.named_scope("panel_sum"):
-        piece = halve(part_in, "y").astype(BF)
-    with jax.named_scope("panel_y"):
-        piece = double(piece, "y")
+        piece = total_over(part_in, "y").astype(BF)
     with jax.named_scope("panel_x"):
         piece = double(piece[None], "x")
     with jax.named_scope("panel_c"):

time: 182 us -> 163 us (0.90); the launches traced: 179 us -> 162 us
  starting transfers between devices: 88.9 us -> 68.5 us
  Pallas kernels: 12.6 us -> 14.6 us
    ppermute x16 -> x13, starting transfers between devices: 62.7 us -> 44.8 us  [swap(): return lax.ppermute(block, axis, [(i, i ^ bit) for i in range(count)])]
    all_to_all x3, waiting for transfers between devices: 8.72 us -> 11.7 us  [exchange(): return lax.all_to_all(blocks, axis, split_axis=0, concat_axis=0, tiled=True)]
    all_to_all x3, starting transfers between devices: 26.2 us -> 23.7 us  [exchange(): return lax.all_to_all(blocks, axis, split_axis=0, concat_axis=0, tiled=True)]
    pallas_call x1, Pallas kernels: 2.15 us -> 4.15 us  [split_rows(): pl.pallas_call(functools.partial(split_kernel, half), out_shape=jax.Shape...]
    ppermute x16 -> x13, waiting for transfers between devices: 53.9 us -> 52.8 us  [swap(): return lax.ppermute(block, axis, [(i, i ^ bit) for i in range(count)])]
  transfers between devices with their start and end apart: 19 -> 16, of which waited for: 13 -> 9; matrix products, arithmetic and copies ran while one was open for 1% -> 1% of each run, Pallas kernels for 3% -> 3%
where the time goes in v3:
time: 163 us; the launch traced here: 162 us
  starting transfers between devices  68.5 us (42%)
  waiting for transfers between devices  64.4 us (40%)
  Pallas kernels  14.6 us (9%)
  blocking collectives  11.1 us (7%)
    ppermute x13, waiting for transfers between devices, swap(): return lax.ppermute(block, axis, [(i, i ^ bit) for i in range(count)])  52.8 us
    ppermute x13, starting transfers between devices, swap(): return lax.ppermute(block, axis, [(i, i ^ bit) for i in range(count)])  44.8 us
    all_to_all x3, starting transfers between devices, exchange(): return lax.all_to_all(blocks, axis, split_axis=0, concat_axis=0, tiled=True)  23.7 us
    all_to_all x3, waiting for transfers between devices, exchange(): return lax.all_to_all(blocks, axis, split_axis=0, concat_axis=0, tiled=True)  11.7 us
    all_to_all x1, blocking collectives, exchange(): return lax.all_to_all(blocks, axis, split_axis=0, concat_axis=0, tiled=True)  11.1 us
    pallas_call x2, Pallas kernels, rotate(): pl.pallas_call(rotate_kernel, out_shape=jax.ShapeDtypeStruct((2 * blocks,...  5.76 us
    pallas_call x1, Pallas kernels, split_rows(): pl.pallas_call(functools.partial(split_kernel, half), out_shape=jax.Shape...  4.15 us
  transfers between devices with their start and end apart: 16, of which 9 were waited for; matrix products, arithmetic and copies ran while one was open for 1% of the time, Pallas kernels for 3%

profile of v3, /device:TPU:56, one launch (start us, length us, event | category | flops | bytes accessed | tf_op | source)
XLA Modules:
  0.0 162.4 jit_solution(5454745286937568185)
XLA Ops:
  1.3 4.1 %shard_map.55 = bf16[32,16,896]{2,1,0:T(8,128)(2,1)} custom-call(s32[2]{0:T(128)} %pad_add_fusion.1.at_ref, bf16[32,28672]{1,0:T(8,128)(2,1)} %grads_ref.1), custom_call_target="tpu_custom_call" | custom-call | bytes 1835008 | tf_op jit(solution)/shard_map/pallas_call | solution.py:69
  5.5 13.3 %all-to-all-start = ((bf16[32,16,896]{2,1,0:T(8,128)(2,1)}), bf16[32,16,896]{2,1,0:T(8,128)(2,1)}, u32[]{:S(2)}, u32[]{:S(2)}) async-start(bf16[32,16,896]{2,1,0:T(8,128)(2,1)} %shard_map.55), calls=%async_computation | async-start | bytes 1835008 | tf_op jit(solution)/shard_map/rows_dp/all_to_all | solution.py:21
  18.8 5.1 %collective-permute-start.1 = (bf16[1,512,128]{2,1,0:T(8,128)(2,1)S(1)}, bf16[1,512,128]{2,1,0:T(8,128)(2,1)S(1)}, u32[]{:S(2)}, u32[]{:S(2)}) collective-permute-start(bf16[1,512,128]{2,1,0:T(8,128)(2,1)S(1)} %bitcast.18), channel_id=1, source_target_pairs={{0,32},{16,48},{32,0},{48,16},{1,33},{17,49},{33,1},{49,17},{2,34}... | collective-permute-start | bytes 393224 | tf_op jit(solution)/shard_map/panel_gather/ppermute | solution.py:26
  24.7 7.3 %collective-permute-start = (bf16[2,1,16,512]{3,2,1,0:T(8,128)(2,1)S(1)}, bf16[2,1,16,512]{3,2,1,0:T(8,128)(2,1)S(1)}, u32[]{:S(2)}, u32[]{:S(2)}) collective-permute-start(bf16[2,1,16,512]{3,2,1,0:T(8,128)(2,1)S(1)} %maximum_bitcast_fusion), channel_id=1, source_target_pairs={{0,256},{64,320},{128,384},{192,448},{256,0},{320,64},{384,128},{4... | collective-permute-start | bytes 98312 | tf_op jit(solution)/shard_map/panel_gather/ppermute | solution.py:26
  32.0 12.9 %collective-permute-done = bf16[2,1,16,512]{3,2,1,0:T(8,128)(2,1)S(1)} collective-permute-done((bf16[2,1,16,512]{3,2,1,0:T(8,128)(2,1)S(1)}, bf16[2,1,16,512]{3,2,1,0:T(8,128)(2,1)S(1)}, u32[]{:S(2)}, u32[]{:S(2)}) %collective-permute-start) | collective-permute-done | bytes 32800 | tf_op jit(solution)/shard_map/panel_gather/ppermute | solution.py:26
  44.9 4.1 %collective-permute-start.3 = (bf16[2,512,128]{2,1,0:T(8,128)(2,1)S(1)}, bf16[2,512,128]{2,1,0:T(8,128)(2,1)S(1)}, u32[]{:S(2)}, u32[]{:S(2)}) collective-permute-start(bf16[2,512,128]{2,1,0:T(8,128)(2,1)S(1)} %pad_maximum_fusion.3), channel_id=1, source_target_pairs={{0,16},{16,0},{32,48},{48,32},{1,17},{17,1},{33,49},{49,33},{2,18}... | collective-permute-start | bytes 786440 | tf_op jit(solution)/shard_map/panel_gather/ppermute | solution.py:26
  51.0 5.8 %collective-permute-done.2 = bf16[2,2,16,512]{3,2,1,0:T(8,128)(2,1)S(1)} collective-permute-done((bf16[2,2,16,512]{3,2,1,0:T(8,128)(2,1)S(1)}, bf16[2,2,16,512]{3,2,1,0:T(8,128)(2,1)S(1)}, u32[]{:S(2)}, u32[]{:S(2)}) %collective-permute-start.2) | collective-permute-done | bytes 65568 | tf_op jit(solution)/shard_map/panel_gather/ppermute | solution.py:26
  60.9 5.9 %collective-permute-done.4 = bf16[2,4,16,512]{3,2,1,0:T(8,128)(2,1)S(1)} collective-permute-done((bf16[2,4,16,512]{3,2,1,0:T(8,128)(2,1)S(1)}, bf16[2,4,16,512]{3,2,1,0:T(8,128)(2,1)S(1)}, u32[]{:S(2)}, u32[]{:S(2)}) %collective-permute-start.4) | collective-permute-done | bytes 131104 | tf_op jit(solution)/shard_map/panel_gather/ppermute | solution.py:26
  68.9 3.5 %shard_map.56.rest_0_ = bf16[32,224,128]{2,1,0:T(8,128)(2,1)} custom-call(bf16[512,896]{1,0:T(8,128)(2,1)} %bitcast.3.tokens_ref, bf16[896,896]{1,0:T(8,128)(2,1)S(1)} %copy-done), custom_call_target="tpu_custom_call" | custom-call | flops 822083584 | bytes 1835008 | tf_op jit(solution)/shard_map/pallas_call | solution.py:111
  72.3 2.3 %shard_map.57 = bf16[32,224,128]{2,1,0:T(8,128)(2,1)} custom-call(bf16[512,896]{1,0:T(8,128)(2,1)S(1)} %collective-permute-done.6.tokens_ref, bf16[896,896]{1,0:T(8,128)(2,1)S(1)} %copy-done, bf16[32,224,128]{2,1,0:T(8,128)(2,1)} %shard_map.56.rest_0_), custom_call_target="tpu_custom_call", output_to_operand_aliasing={{}: (2, {})} | custom-call | flops 822083584 | bytes 1835008 | tf_op jit(solution)/shard_map/pallas_call | solution.py:111
  74.7 4.3 %all-to-all-start.1 = ((bf16[32,224,128]{2,1,0:T(8,128)(2,1)}), bf16[32,224,128]{2,1,0:T(8,128)(2,1)S(1)}, u32[]{:S(2)}, u32[]{:S(2)}) async-start(bf16[32,224,128]{2,1,0:T(8,128)(2,1)} %shard_map.57), calls=%async_computation.1 | async-start | bytes 3670016 | tf_op jit(solution)/shard_map/sum_dp/all_to_all | solution.py:21
  80.1 3.3 %collective-permute-start.7 = (bf16[8,16,512]{2,1,0:T(8,128)(2,1)S(1)}, bf16[8,16,512]{2,1,0:T(8,128)(2,1)S(1)}, u32[]{:S(2)}, u32[]{:S(2)}) collective-permute-start(bf16[8,16,512]{2,1,0:T(8,128)(2,1)S(1)} %convert_element_type.21), channel_id=1, source_target_pairs={{0,2},{2,0},{4,6},{6,4},{8,10},{10,8},{12,14},{14,12},{1,3},{3,1},... | collective-permute-start | bytes 393224 | tf_op jit(solution)/shard_map/panel_sum/ppermute | solution.py:26
  83.3 4.2 %collective-permute-done.7 = bf16[8,16,512]{2,1,0:T(8,128)(2,1)S(1)} collective-permute-done((bf16[8,16,512]{2,1,0:T(8,128)(2,1)S(1)}, bf16[8,16,512]{2,1,0:T(8,128)(2,1)S(1)}, u32[]{:S(2)}, u32[]{:S(2)}) %collective-permute-start.7) | collective-permute-done | bytes 131104 | tf_op jit(solution)/shard_map/panel_sum/ppermute | solution.py:26
  87.6 4.0 %collective-permute-start.8 = (bf16[8,16,512]{2,1,0:T(8,128)(2,1)S(1)}, bf16[8,16,512]{2,1,0:T(8,128)(2,1)S(1)}, u32[]{:S(2)}, u32[]{:S(2)}) collective-permute-start(bf16[8,16,512]{2,1,0:T(8,128)(2,1)S(1)} %fusion), channel_id=1, source_target_pairs={{0,4},{2,6},{4,0},{6,2},{8,12},{10,14},{12,8},{14,10},{1,5},{3,7},... | collective-permute-start | bytes 393224 | tf_op jit(solution)/shard_map/panel_sum/ppermute | solution.py:26
  91.7 6.3 %collective-permute-done.8 = bf16[8,16,512]{2,1,0:T(8,128)(2,1)S(1)} collective-permute-done((bf16[8,16,512]{2,1,0:T(8,128)(2,1)S(1)}, bf16[8,16,512]{2,1,0:T(8,128)(2,1)S(1)}, u32[]{:S(2)}, u32[]{:S(2)}) %collective-permute-start.8) | collective-permute-done | bytes 131104 | tf_op jit(solution)/shard_map/panel_sum/ppermute | solution.py:26
  98.1 4.6 %collective-permute-start.9 = (bf16[8,16,512]{2,1,0:T(8,128)(2,1)S(1)}, bf16[8,16,512]{2,1,0:T(8,128)(2,1)S(1)}, u32[]{:S(2)}, u32[]{:S(2)}) collective-permute-start(bf16[8,16,512]{2,1,0:T(8,128)(2,1)S(1)} %fusion.2), channel_id=1, source_target_pairs={{0,8},{2,10},{4,12},{6,14},{8,0},{10,2},{12,4},{14,6},{1,9},{3,11}... | collective-permute-start | bytes 393224 | tf_op jit(solution)/shard_map/panel_sum/ppermute | solution.py:26
  102.7 8.6 %collective-permute-done.9 = bf16[8,16,512]{2,1,0:T(8,128)(2,1)S(1)} collective-permute-done((bf16[8,16,512]{2,1,0:T(8,128)(2,1)S(1)}, bf16[8,16,512]{2,1,0:T(8,128)(2,1)S(1)}, u32[]{:S(2)}, u32[]{:S(2)}) %collective-permute-start.9) | collective-permute-done | bytes 131104 | tf_op jit(solution)/shard_map/panel_sum/ppermute | solution.py:26
  111.3 4.3 %collective-permute-start.10 = (bf16[1,8,16,512]{3,2,1,0:T(8,128)(2,1)S(1)}, bf16[1,8,16,512]{3,2,1,0:T(8,128)(2,1)S(1)}, u32[]{:S(2)}, u32[]{:S(2)}) collective-permute-start(bf16[1,8,16,512]{3,2,1,0:T(8,128)(2,1)S(1)} %fusion.1), channel_id=1, source_target_pairs={{0,32},{16,48},{32,0},{48,16},{1,33},{17,49},{33,1},{49,17},{2,34}... | collective-permute-start | bytes 393224 | tf_op jit(solution)/shard_map/panel_x/ppermute | solution.py:26
  115.6 7.1 %collective-permute-done.10 = bf16[1,8,16,512]{3,2,1,0:T(8,128)(2,1)S(1)} collective-permute-done((bf16[1,8,16,512]{3,2,1,0:T(8,128)(2,1)S(1)}, bf16[1,8,16,512]{3,2,1,0:T(8,128)(2,1)S(1)}, u32[]{:S(2)}, u32[]{:S(2)}) %collective-permute-start.10) | collective-permute-done | bytes 131104 | tf_op jit(solution)/shard_map/panel_x/ppermute | solution.py:26
  122.8 2.3 %collective-permute-start.11 = (bf16[2,8,16,512]{3,2,1,0:T(8,128)(2,1)S(1)}, bf16[2,8,16,512]{3,2,1,0:T(8,128)(2,1)S(1)}, u32[]{:S(2)}, u32[]{:S(2)}) collective-permute-start(bf16[2,8,16,512]{3,2,1,0:T(8,128)(2,1)S(1)} %pad_maximum_fusion.5), channel_id=1, source_target_pairs={{0,16},{16,0},{32,48},{48,32},{1,17},{17,1},{33,49},{49,33},{2,18}... | collective-permute-start | bytes 786440 | tf_op jit(solution)/shard_map/panel_x/ppermute | solution.py:26
  126.2 6.1 %all-to-all-start.2 = ((bf16[8,224,128]{2,1,0:T(8,128)(2,1)}), bf16[8,224,128]{2,1,0:T(8,128)(2,1)S(1)}, u32[]{:S(2)}, u32[]{:S(2)}) async-start(bf16[8,224,128]{2,1,0:T(8,128)(2,1)} %shard_map.58), calls=%async_computation.2 | async-start | bytes 917504 | tf_op jit(solution)/shard_map/rotated_z/all_to_all | solution.py:21
  136.2 11.7 %all-to-all-done.2.left_ref = bf16[8,224,128]{2,1,0:T(8,128)(2,1)S(1)} async-done(((bf16[8,224,128]{2,1,0:T(8,128)(2,1)}), bf16[8,224,128]{2,1,0:T(8,128)(2,1)S(1)}, u32[]{:S(2)}, u32[]{:S(2)}) %all-to-all-start.2) | async-done | bytes 458784 | tf_op jit(solution)/shard_map/rotated_z/all_to_all | solution.py:21
  147.9 2.6 %shard_map.60 = f32[4,224,128]{2,1,0:T(8,128)S(1)} custom-call(s32[2]{0:T(128)S(1)} %pad_add_fusion.at_ref, bf16[8,224,128]{2,1,0:T(8,128)(2,1)S(1)} %all-to-all-done.2.left_ref, bf16[4,8,16,512]{3,2,1,0:T(8,128)(2,1)S(1)} %pad_maximum_fusion.2.own_ref, bf16[4,8,16,512]{3,2,1,0:T(8,128)(2,1)S(1)} %collective-permute-done.12.other_ref), custom_call_target="tpu_custom_call" | custom-call | flops 234881024 | bytes 1048576 | tf_op jit(solution)/shard_map/pallas_call | solution.py:198
  150.5 11.1 %all_to_all.20 = f32[4,224,128]{2,1,0:T(8,128)S(1)} all-to-all(f32[4,224,128]{2,1,0:T(8,128)S(1)} %shard_map.60), channel_id=1, replica_groups=mesh['z'=8,'x'=4,'y'=8,'c'=2] {'x'}, dimensions={0} | all-to-all | bytes 917504 | tf_op jit(solution)/shard_map/out_x/all_to_all | solution.py:21
  (36 shorter events, 16.5 us)
Async XLA Ops:
  1.3 17.4 %copy-start.1 = (bf16[512,128]{1,0:T(8,128)(2,1)S(1)}, bf16[512,128]{1,0:T(8,128)(2,1)}, u32[]{:S(2)}) copy-start(bf16[512,128]{1,0:T(8,128)(2,1)} %param.8) | copy-start | bytes 393220
  5.5 61.5 %all-to-all-start = ((bf16[32,16,896]{2,1,0:T(8,128)(2,1)}), bf16[32,16,896]{2,1,0:T(8,128)(2,1)}, u32[]{:S(2)}, u32[]{:S(2)}) async-start(bf16[32,16,896]{2,1,0:T(8,128)(2,1)} %shard_map.55), calls=%async_computation | async-start | bytes 1835008 | tf_op jit(solution)/shard_map/rows_dp/all_to_all | solution.py:21
  18.8 26.1 %collective-permute-start.1 = (bf16[1,512,128]{2,1,0:T(8,128)(2,1)S(1)}, bf16[1,512,128]{2,1,0:T(8,128)(2,1)S(1)}, u32[]{:S(2)}, u32[]{:S(2)}) collective-permute-start(bf16[1,512,128]{2,1,0:T(8,128)(2,1)S(1)} %bitcast.18), channel_id=1, source_target_pairs={{0,32},{16,48},{32,0},{48,16},{1,33},{17,49},{33,1},{49,17},{2,34}... | collective-permute-start | bytes 393224 | tf_op jit(solution)/shard_map/panel_gather/ppermute | solution.py:26
  24.7 20.2 %collective-permute-start = (bf16[2,1,16,512]{3,2,1,0:T(8,128)(2,1)S(1)}, bf16[2,1,16,512]{3,2,1,0:T(8,128)(2,1)S(1)}, u32[]{:S(2)}, u32[]{:S(2)}) collective-permute-start(bf16[2,1,16,512]{3,2,1,0:T(8,128)(2,1)S(1)} %maximum_bitcast_fusion), channel_id=1, source_target_pairs={{0,256},{64,320},{128,384},{192,448},{256,0},{320,64},{384,128},{4... | collective-permute-start | bytes 98312 | tf_op jit(solution)/shard_map/panel_gather/ppermute | solution.py:26
  44.9 11.9 %collective-permute-start.3 = (bf16[2,512,128]{2,1,0:T(8,128)(2,1)S(1)}, bf16[2,512,128]{2,1,0:T(8,128)(2,1)S(1)}, u32[]{:S(2)}, u32[]{:S(2)}) collective-permute-start(bf16[2,512,128]{2,1,0:T(8,128)(2,1)S(1)} %pad_maximum_fusion.3), channel_id=1, source_target_pairs={{0,16},{16,0},{32,48},{48,32},{1,17},{17,1},{33,49},{49,33},{2,18}... | collective-permute-start | bytes 786440 | tf_op jit(solution)/shard_map/panel_gather/ppermute | solution.py:26
  49.1 7.8 %collective-permute-start.2 = (bf16[2,2,16,512]{3,2,1,0:T(8,128)(2,1)S(1)}, bf16[2,2,16,512]{3,2,1,0:T(8,128)(2,1)S(1)}, u32[]{:S(2)}, u32[]{:S(2)}) collective-permute-start(bf16[2,2,16,512]{3,2,1,0:T(8,128)(2,1)S(1)} %pad_maximum_fusion.7), channel_id=1, source_target_pairs={{0,128},{64,192},{128,0},{192,64},{256,384},{320,448},{384,256},{4... | collective-permute-start | bytes 196616 | tf_op jit(solution)/shard_map/panel_gather/ppermute | solution.py:26
  56.9 12.0 %copy-start = (bf16[896,896]{1,0:T(8,128)(2,1)S(1)}, bf16[896,896]{1,0:T(8,128)(2,1)}, u32[]{:S(2)}) copy-start(bf16[896,896]{1,0:T(8,128)(2,1)} %basis_ref.3) | copy-start | bytes 4816900
  56.9 9.9 %collective-permute-start.5 = (bf16[4,512,128]{2,1,0:T(8,128)(2,1)S(1)}, bf16[4,512,128]{2,1,0:T(8,128)(2,1)S(1)}, u32[]{:S(2)}, u32[]{:S(2)}) collective-permute-start(bf16[4,512,128]{2,1,0:T(8,128)(2,1)S(1)} %get-tuple-element.24), channel_id=1, source_target_pairs={{0,1},{1,0},{2,3},{3,2},{4,5},{5,4},{6,7},{7,6},{8,9},{9,8},{10,11... | collective-permute-start | bytes 1572872 | tf_op jit(solution)/shard_map/panel_gather/ppermute | solution.py:26
  59.0 7.8 %collective-permute-start.4 = (bf16[2,4,16,512]{3,2,1,0:T(8,128)(2,1)S(1)}, bf16[2,4,16,512]{3,2,1,0:T(8,128)(2,1)S(1)}, u32[]{:S(2)}, u32[]{:S(2)}) collective-permute-start(bf16[2,4,16,512]{3,2,1,0:T(8,128)(2,1)S(1)} %pad_maximum_fusion.6), channel_id=1, source_target_pairs={{0,64},{64,0},{128,192},{192,128},{256,320},{320,256},{384,448},{4... | collective-permute-start | bytes 393224 | tf_op jit(solution)/shard_map/panel_gather/ppermute | solution.py:26
  67.0 5.4 %collective-permute-start.6 = (bf16[512,896]{1,0:T(8,128)(2,1)}, bf16[512,896]{1,0:T(8,128)(2,1)S(1)}, u32[]{:S(2)}, u32[]{:S(2)}) collective-permute-start(bf16[512,896]{1,0:T(8,128)(2,1)} %bitcast.3.tokens_ref), channel_id=1, source_target_pairs={{0,1},{1,0},{2,3},{3,2},{4,5},{5,4},{6,7},{7,6},{8,9},{9,8},{10,11... | collective-permute-start | bytes 2752520 | tf_op jit(solution)/shard_map/rows_c/ppermute | solution.py:26
  74.7 50.5 %all-to-all-start.1 = ((bf16[32,224,128]{2,1,0:T(8,128)(2,1)}), bf16[32,224,128]{2,1,0:T(8,128)(2,1)S(1)}, u32[]{:S(2)}, u32[]{:S(2)}) async-start(bf16[32,224,128]{2,1,0:T(8,128)(2,1)} %shard_map.57), calls=%async_computation.1 | async-start | bytes 3670016 | tf_op jit(solution)/shard_map/sum_dp/all_to_all | solution.py:21
  80.1 7.5 %collective-permute-start.7 = (bf16[8,16,512]{2,1,0:T(8,128)(2,1)S(1)}, bf16[8,16,512]{2,1,0:T(8,128)(2,1)S(1)}, u32[]{:S(2)}, u32[]{:S(2)}) collective-permute-start(bf16[8,16,512]{2,1,0:T(8,128)(2,1)S(1)} %convert_element_type.21), channel_id=1, source_target_pairs={{0,2},{2,0},{4,6},{6,4},{8,10},{10,8},{12,14},{14,12},{1,3},{3,1},... | collective-permute-start | bytes 393224 | tf_op jit(solution)/shard_map/panel_sum/ppermute | solution.py:26
  87.6 10.4 %collective-permute-start.8 = (bf16[8,16,512]{2,1,0:T(8,128)(2,1)S(1)}, bf16[8,16,512]{2,1,0:T(8,128)(2,1)S(1)}, u32[]{:S(2)}, u32[]{:S(2)}) collective-permute-start(bf16[8,16,512]{2,1,0:T(8,128)(2,1)S(1)} %fusion), channel_id=1, source_target_pairs={{0,4},{2,6},{4,0},{6,2},{8,12},{10,14},{12,8},{14,10},{1,5},{3,7},... | collective-permute-start | bytes 393224 | tf_op jit(solution)/shard_map/panel_sum/ppermute | solution.py:26
  98.1 13.2 %collective-permute-start.9 = (bf16[8,16,512]{2,1,0:T(8,128)(2,1)S(1)}, bf16[8,16,512]{2,1,0:T(8,128)(2,1)S(1)}, u32[]{:S(2)}, u32[]{:S(2)}) collective-permute-start(bf16[8,16,512]{2,1,0:T(8,128)(2,1)S(1)} %fusion.2), channel_id=1, source_target_pairs={{0,8},{2,10},{4,12},{6,14},{8,0},{10,2},{12,4},{14,6},{1,9},{3,11}... | collective-permute-start | bytes 393224 | tf_op jit(solution)/shard_map/panel_sum/ppermute | solution.py:26
  111.3 11.4 %collective-permute-start.10 = (bf16[1,8,16,512]{3,2,1,0:T(8,128)(2,1)S(1)}, bf16[1,8,16,512]{3,2,1,0:T(8,128)(2,1)S(1)}, u32[]{:S(2)}, u32[]{:S(2)}) collective-permute-start(bf16[1,8,16,512]{3,2,1,0:T(8,128)(2,1)S(1)} %fusion.1), channel_id=1, source_target_pairs={{0,32},{16,48},{32,0},{48,16},{1,33},{17,49},{33,1},{49,17},{2,34}... | collective-permute-start | bytes 393224 | tf_op jit(solution)/shard_map/panel_x/ppermute | solution.py:26
  122.8 9.5 %collective-permute-start.11 = (bf16[2,8,16,512]{3,2,1,0:T(8,128)(2,1)S(1)}, bf16[2,8,16,512]{3,2,1,0:T(8,128)(2,1)S(1)}, u32[]{:S(2)}, u32[]{:S(2)}) collective-permute-start(bf16[2,8,16,512]{3,2,1,0:T(8,128)(2,1)S(1)} %pad_maximum_fusion.5), channel_id=1, source_target_pairs={{0,16},{16,0},{32,48},{48,32},{1,17},{17,1},{33,49},{49,33},{2,18}... | collective-permute-start | bytes 786440 | tf_op jit(solution)/shard_map/panel_x/ppermute | solution.py:26
  126.2 21.6 %all-to-all-start.2 = ((bf16[8,224,128]{2,1,0:T(8,128)(2,1)}), bf16[8,224,128]{2,1,0:T(8,128)(2,1)S(1)}, u32[]{:S(2)}, u32[]{:S(2)}) async-start(bf16[8,224,128]{2,1,0:T(8,128)(2,1)} %shard_map.58), calls=%async_computation.2 | async-start | bytes 917504 | tf_op jit(solution)/shard_map/rotated_z/all_to_all | solution.py:21
  132.4 3.8 %collective-permute-start.12 = (bf16[4,8,16,512]{3,2,1,0:T(8,128)(2,1)S(1)}, bf16[4,8,16,512]{3,2,1,0:T(8,128)(2,1)S(1)}, u32[]{:S(2)}, u32[]{:S(2)}) collective-permute-start(bf16[4,8,16,512]{3,2,1,0:T(8,128)(2,1)S(1)} %pad_maximum_fusion.2.own_ref), channel_id=1, source_target_pairs={{0,1},{1,0},{2,3},{3,2},{4,5},{5,4},{6,7},{7,6},{8,9},{9,8},{10,11... | collective-permute-start | bytes 1572872 | tf_op jit(solution)/shard_map/panel_c/ppermute | solution.py:26

commit v4 on v3

--- a/solution.py
+++ b/solution.py
@@ -44,60 +44,66 @@
     return block
 
 
-def total_over(block, axis):
-    for bit in reversed(bits(axis)):
-        block = block + swap(block.astype(BF), axis, bit).astype(F32)
-    return block
+def add_from(block, axis, bit):
+    return block + swap(block.astype(BF), axis, bit).astype(F32)
 
 
 def cost(flops, moved):
     return pl.CostEstimate(flops=flops, bytes_accessed=moved, transcendentals=0)
 
 
-def split_kernel(half, at_ref, grads_ref, out_ref):
-    parts, _, wide = out_ref.shape
-    slot = at_ref[0] * half + lax.broadcasted_iota(jnp.int32, (half, wide), 0)
-    live = slot < at_ref[1]
-    for q in range(parts):
-        piece = grads_ref[:, q * wide : (q + 1) * wide]
-        out_ref[q] = jnp.where(live, piece, jnp.zeros_like(piece))
-
-
-def split_rows(grads, at, half, parts, steps=4):
+def split_kernel(length_ref, grads_ref, out_ref, held, sems):
+    parts, half, wide = out_ref.shape
+    steps, _, chunk = held.shape
+    each = parts // steps
+    first = lax.axis_index("c") * half
+    copies = [
+        pltpu.make_async_copy(
+            grads_ref.at[pl.ds(first, half), pl.ds(k * chunk, chunk)], held.at[k], sems.at[k]
+        )
+        for k in range(steps)
+    ]
+    for copy in copies:
+        copy.start()
+    slot = first + lax.broadcasted_iota(jnp.int32, (half, wide), 0)
+    live = slot < length_ref[0]
+    for k in range(steps):
+        copies[k].wait()
+        for q in range(each):
+            piece = held[k, :, q * wide : (q + 1) * wide]
+            out_ref[k * each + q] = jnp.where(live, piece, jnp.zeros_like(piece))
+
+
+def split_rows(grads, length, half, parts, steps=4):
     wide = grads.shape[1] // parts
-    each = parts // steps
-    return pl.pallas_call(
-        functools.partial(split_kernel, half),
+    return pl.pallas_call(
+        split_kernel,
         out_shape=jax.ShapeDtypeStruct((parts, half, wide), grads.dtype),
-        grid_spec=pltpu.PrefetchScalarGridSpec(
-            num_scalar_prefetch=1,
-            grid=(steps,),
-            in_specs=[pl.BlockSpec((half, each * wide), lambda i, at: (at[0], i))],
-            out_specs=pl.BlockSpec((each, half, wide), lambda i, at: (i, 0, 0)),
-        ),
+        in_specs=[pl.BlockSpec(memory_space=SMEM), pl.BlockSpec(memory_space=pl.ANY)],
+        out_specs=pl.BlockSpec(memory_space=VMEM),
+        scratch_shapes=[
+            VMEM((steps, half, grads.shape[1] // steps), grads.dtype),
+            pltpu.SemaphoreType.DMA((steps,)),
+        ],
         compiler_params=pltpu.CompilerParams(vmem_limit_bytes=58 * MIB),
         cost_estimate=cost(0, 4 * half * grads.shape[1]),
-    )(at, grads)
+    )(length, grads)
 
 
 def rotate_kernel(tokens_ref, basis_ref, *rest):
     out_ref = rest[-1]
     product = jnp.dot(tokens_ref[...], basis_ref[...], preferred_element_type=F32)
-    lanes = out_ref.shape[2]
-    rows = out_ref.shape[1]
-    groups = product.shape[0] // lanes
-    pieces = product.shape[1] // rows
-    for g in range(groups):
-        turned = product[g * lanes : (g + 1) * lanes].T.astype(BF)
+    pieces, rows, count = out_ref.shape
+    for g in range(0, count, 128):
+        turned = product[g : g + 128].T.astype(BF)
         for q in range(pieces):
-            out_ref[g * pieces + q] = turned[q * rows : (q + 1) * rows]
+            out_ref[q, :, g : g + 128] = turned[q * rows : (q + 1) * rows]
 
 
 def rotate(tokens, basis, place, pieces, before=None):
     count, wide = tokens.shape
     columns = basis.shape[1]
     rows = columns // pieces
-    blocks = pieces * count // 128
     in_specs = [
         pl.BlockSpec((count, wide), lambda i: (0, 0)),
         pl.BlockSpec((wide, columns), lambda i: (0, 0)),
@@ -110,14 +116,37 @@
         aliases = {2: 0}
     return pl.pallas_call(
         rotate_kernel,
-        out_shape=jax.ShapeDtypeStruct((2 * blocks, rows, 128), BF),
+        out_shape=jax.ShapeDtypeStruct((pieces, rows, 2 * count), BF),
         grid=(1,),
         in_specs=in_specs,
-        out_specs=pl.BlockSpec((blocks, rows, 128), lambda i: (place, 0, 0)),
+        out_specs=pl.BlockSpec((pieces, rows, count), lambda i: (0, 0, place)),
         input_output_aliases=aliases,
         compiler_params=PARAMS,
         cost_estimate=cost(2 * count * wide * columns, 2 * count * (wide + columns)),
     )(*args)
+
+
+def sum_lanes_kernel(parts_ref, out_ref):
+    for g in range(out_ref.shape[0]):
+        lanes = slice(g * 128, (g + 1) * 128)
+        total = parts_ref[0, :, lanes].astype(F32)
+        for q in range(1, parts_ref.shape[0]):
+            total = total + parts_ref[q, :, lanes].astype(F32)
+        out_ref[g] = total.astype(BF)
+
+
+def sum_lanes(parts, steps=2):
+    count, rows, lanes = parts.shape
+    blocks = lanes // 128
+    return pl.pallas_call(
+        sum_lanes_kernel,
+        out_shape=jax.ShapeDtypeStruct((blocks, rows, 128), BF),
+        grid=(steps,),
+        in_specs=[pl.BlockSpec((count, rows, lanes // steps), lambda i: (0, 0, i))],
+        out_specs=pl.BlockSpec((blocks // steps, rows, 128), lambda i: (i, 0, 0)),
+        compiler_params=PARAMS,
+        cost_estimate=cost(parts.size, 2 * parts.size),
+    )(parts)
 
 
 def sum_kernel(parts_ref, out_ref):
@@ -178,7 +207,7 @@
     for k in range(groups):
         left = jnp.concatenate([left_ref[k], left_ref[groups + k]], axis=1)
         places = [divmod(k * per_group + j, nx) for j in range(per_group)]
-        places = [(reverse(xp ^ at_ref[0], 2), reverse(zp ^ at_ref[1], 3)) for zp, xp in places]
+        places = [(xp ^ at_ref[0], reverse(zp ^ at_ref[1], 3)) for zp, xp in places]
         right = jnp.concatenate(
             [own_ref[a, b] for a, b in places] + [other_ref[a, b] for a, b in places], axis=0
         )
@@ -213,8 +242,9 @@
     wide, columns = basis_out.shape
     deep = basis_in.shape[0]
     at = jnp.stack([ix, iz]).astype(jnp.int32)
-
-    blocks = split_rows(grads_out, jnp.stack([ic.astype(jnp.int32), lengths[0]]), half, nz * nx)
+    tie = lax.optimization_barrier
+
+    blocks = split_rows(grads_out, lengths, half, nz * nx)
     with jax.named_scope("rows_dp"):
         own = exchange(blocks, DP).reshape(nz * nx * half, wide)
 
@@ -223,36 +253,41 @@
     slab = jnp.stack([mine, theirs])[:, None]
     basis_x = basis_in[None]
     with jax.named_scope("panel_gather"):
-        for bit in bits("z"):
-            more_slab = swap(slab, "z", bit)
-            if bit > 1:
-                more_basis = swap(basis_x, "x", bit // 2)
-            else:
-                more_basis = swap(basis_x, "c", 1)
-            more_slab, more_basis = lax.optimization_barrier((more_slab, more_basis))
-            slab = jnp.concatenate([slab, more_slab], axis=1)
-            if bit > 1:
-                basis_x = jnp.concatenate([basis_x, more_basis], axis=0)
-            else:
-                basis_x = jnp.stack([basis_x, more_basis])
-    own, slab, basis_x = lax.optimization_barrier((own, slab, basis_x))
-    part_in = panel_part(at, slab, basis_x)
-    with jax.named_scope("panel_sum"):
-        piece = total_over(part_in, "y").astype(BF)
-    with jax.named_scope("panel_x"):
-        piece = double(piece[None], "x")
-    with jax.named_scope("panel_c"):
-        piece_other = swap(piece, "c", 1)
+        more_slab = swap(slab, "z", 4)
+        basis_x = double(basis_x, "x")
+        basis_x = jnp.stack([basis_x, swap(basis_x, "c", 1)])
+        own, more_slab, basis_x = tie((own, more_slab, basis_x))
+        slab = jnp.concatenate([slab, more_slab], axis=1)
+        more_slab = swap(slab, "z", 2)
 
     with jax.named_scope("rows_c"):
         other = swap(own, "c", 1)
     parts = rotate(own, basis_out, 0, nx)
+    other, more_slab = tie((other, more_slab))
     parts = rotate(other, basis_out, 1, nx, parts)
-    with jax.named_scope("sum_dp"):
-        parts = exchange(parts, DP)
+    with jax.named_scope("sum_x"):
+        parts = exchange(parts, "x")
+
+    with jax.named_scope("panel_gather"):
+        slab = jnp.concatenate([slab, more_slab], axis=1)
+        slab = jnp.concatenate([slab, swap(slab, "z", 1)], axis=1)
+    piece = panel_part(at, slab, basis_x)
+    with jax.named_scope("panel_sum"):
+        piece = add_from(piece, "y", 1)
+        piece = add_from(piece, "y", 2)
+    parts, piece = tie((parts, piece))
+    parts = sum_lanes(parts)
+    with jax.named_scope("sum_z"):
+        parts = exchange(parts, "z")
+    with jax.named_scope("panel_sum"):
+        piece = add_from(piece, "y", 4).astype(BF)
     rotated = sum_parts(parts, nz)
     with jax.named_scope("rotated_z"):
         rotated = exchange(rotated, "z")
+    with jax.named_scope("panel_x"):
+        piece = jnp.stack([piece] + [swap(piece, "x", k) for k in range(1, 4)])
+    with jax.named_scope("panel_c"):
+        piece_other = swap(piece, "c", 1)
 
     result = examples(at, rotated, piece, piece_other, nx, 1.0 / (nz * nx * slots))
     with jax.named_scope("out_x"):

time: 163 us -> 155 us (0.951)
  waiting for transfers between devices: 64.4 us -> 44.9 us
  starting transfers between devices: 68.5 us -> 77.3 us
    ppermute x13 -> x14, waiting for transfers between devices: 52.8 us -> 34.9 us  [swap(): return lax.ppermute(block, axis, [(i, i ^ bit) for i in range(count)])]
    ppermute x13 -> x14, starting transfers between devices: 44.8 us -> 49.8 us  [swap(): return lax.ppermute(block, axis, [(i, i ^ bit) for i in range(count)])]
    all_to_all x3 -> x4, starting transfers between devices: 23.7 us -> 27.5 us  [exchange(): return lax.all_to_all(blocks, axis, split_axis=0, concat_axis=0, tiled=True)]
    all_to_all x3 -> x4, waiting for transfers between devices: 11.7 us -> 9.99 us  [exchange(): return lax.all_to_all(blocks, axis, split_axis=0, concat_axis=0, tiled=True)]
    pallas_call x3 -> x4, Pallas kernels: 9.9 us -> 9.28 us  [the longest x2 5.88 us: rotate(): pl.pallas_call(rotate_kernel, out_shape=jax.ShapeDtypeStruct((pieces, row...]
  transfers between devices with their start and end apart: 16 -> 18, of which waited for: 9 -> 11; matrix products, arithmetic and copies ran while one was open for 1% -> 2% of each run, Pallas kernels for 3% -> 3%
where the time goes in v4:
time: 155 us; the launch traced here: 154 us
  starting transfers between devices  77.3 us (50%)
  waiting for transfers between devices  44.9 us (29%)
  Pallas kernels  13.9 us (9%)
  blocking collectives  12.7 us (8%)
  local copies, waits for them, and re-layouts  2.34 us (2%)
  other arithmetic  1.58 us (1%)
    ppermute x14, starting transfers between devices, swap(): return lax.ppermute(block, axis, [(i, i ^ bit) for i in range(count)])  49.8 us
    ppermute x14, waiting for transfers between devices, swap(): return lax.ppermute(block, axis, [(i, i ^ bit) for i in range(count)])  34.9 us
    all_to_all x4, starting transfers between devices, exchange(): return lax.all_to_all(blocks, axis, split_axis=0, concat_axis=0, tiled=True)  27.5 us
    all_to_all x1, blocking collectives, exchange(): return lax.all_to_all(blocks, axis, split_axis=0, concat_axis=0, tiled=True)  12.7 us
    all_to_all x4, waiting for transfers between devices, exchange(): return lax.all_to_all(blocks, axis, split_axis=0, concat_axis=0, tiled=True)  9.99 us
    pallas_call x2, Pallas kernels, rotate(): pl.pallas_call(rotate_kernel, out_shape=jax.ShapeDtypeStruct((pieces, row...  5.88 us
  transfers between devices with their start and end apart: 18, of which 11 were waited for; matrix products, arithmetic and copies ran while one was open for 2% of the time, Pallas kernels for 3%

profile of v4, /device:TPU:56, one launch (start us, length us, event | category | flops | bytes accessed | tf_op | source)
XLA Modules:
  0.0 153.7 jit_solution(18360157604400260563)
XLA Ops:
  3.0 13.3 %all-to-all-start = ((bf16[32,16,896]{2,1,0:T(8,128)(2,1)}), bf16[32,16,896]{2,1,0:T(8,128)(2,1)}, u32[]{:S(2)}, u32[]{:S(2)}) async-start(bf16[32,16,896]{2,1,0:T(8,128)(2,1)} %shard_map.55), calls=%async_computation | async-start | bytes 1835008 | tf_op jit(solution)/shard_map/rows_dp/all_to_all | solution.py:21
  16.3 5.1 %collective-permute-start.1 = (bf16[1,512,128]{2,1,0:T(8,128)(2,1)S(1)}, bf16[1,512,128]{2,1,0:T(8,128)(2,1)S(1)}, u32[]{:S(2)}, u32[]{:S(2)}) collective-permute-start(bf16[1,512,128]{2,1,0:T(8,128)(2,1)S(1)} %bitcast.19), channel_id=1, source_target_pairs={{0,32},{16,48},{32,0},{48,16},{1,33},{17,49},{33,1},{49,17},{2,34}... | collective-permute-start | bytes 393224 | tf_op jit(solution)/shard_map/panel_gather/ppermute | solution.py:26
  21.4 5.5 %collective-permute-done.1 = bf16[1,512,128]{2,1,0:T(8,128)(2,1)S(1)} collective-permute-done((bf16[1,512,128]{2,1,0:T(8,128)(2,1)S(1)}, bf16[1,512,128]{2,1,0:T(8,128)(2,1)S(1)}, u32[]{:S(2)}, u32[]{:S(2)}) %collective-permute-start.1) | collective-permute-done | bytes 131104 | tf_op jit(solution)/shard_map/panel_gather/ppermute | solution.py:26
  26.9 4.0 %collective-permute-start.2 = (bf16[2,512,128]{2,1,0:T(8,128)(2,1)S(1)}, bf16[2,512,128]{2,1,0:T(8,128)(2,1)S(1)}, u32[]{:S(2)}, u32[]{:S(2)}) collective-permute-start(bf16[2,512,128]{2,1,0:T(8,128)(2,1)S(1)} %pad_maximum_fusion.3), channel_id=1, source_target_pairs={{0,16},{16,0},{32,48},{48,32},{1,17},{17,1},{33,49},{49,33},{2,18}... | collective-permute-start | bytes 786440 | tf_op jit(solution)/shard_map/panel_gather/ppermute | solution.py:26
  31.0 8.5 %collective-permute-done.2 = bf16[2,512,128]{2,1,0:T(8,128)(2,1)S(1)} collective-permute-done((bf16[2,512,128]{2,1,0:T(8,128)(2,1)S(1)}, bf16[2,512,128]{2,1,0:T(8,128)(2,1)S(1)}, u32[]{:S(2)}, u32[]{:S(2)}) %collective-permute-start.2) | collective-permute-done | bytes 262176 | tf_op jit(solution)/shard_map/panel_gather/ppermute | solution.py:26
  42.2 6.5 %collective-permute-start = (bf16[2,1,16,512]{3,2,1,0:T(8,128)(2,1)S(1)}, bf16[2,1,16,512]{3,2,1,0:T(8,128)(2,1)S(1)}, u32[]{:S(2)}, u32[]{:S(2)}) collective-permute-start(bf16[2,1,16,512]{3,2,1,0:T(8,128)(2,1)S(1)} %maximum_bitcast_fusion), channel_id=1, source_target_pairs={{0,256},{64,320},{128,384},{192,448},{256,0},{320,64},{384,128},{4... | collective-permute-start | bytes 98312 | tf_op jit(solution)/shard_map/panel_gather/ppermute | solution.py:26
  53.8 4.8 %collective-permute-start.5 = (bf16[2,2,16,512]{3,2,1,0:T(8,128)(2,1)S(1)}, bf16[2,2,16,512]{3,2,1,0:T(8,128)(2,1)S(1)}, u32[]{:S(2)}, u32[]{:S(2)}) collective-permute-start(bf16[2,2,16,512]{3,2,1,0:T(8,128)(2,1)S(1)} %pad_maximum_fusion.6), channel_id=1, source_target_pairs={{0,128},{64,192},{128,0},{192,64},{256,384},{320,448},{384,256},{4... | collective-permute-start | bytes 196616 | tf_op jit(solution)/shard_map/panel_gather/ppermute | solution.py:26
  58.6 3.5 %shard_map.56.rest_0_ = bf16[4,224,1024]{2,1,0:T(8,128)(2,1)} custom-call(bf16[512,896]{1,0:T(8,128)(2,1)} %bitcast.2.tokens_ref, bf16[896,896]{1,0:T(8,128)(2,1)S(1)} %copy-done), custom_call_target="tpu_custom_call" | custom-call | flops 822083584 | bytes 1835008 | tf_op jit(solution)/shard_map/pallas_call | solution.py:117
  62.8 2.3 %shard_map.57 = bf16[4,224,1024]{2,1,0:T(8,128)(2,1)} custom-call(bf16[512,896]{1,0:T(8,128)(2,1)S(1)} %collective-permute-done.4.tokens_ref, bf16[896,896]{1,0:T(8,128)(2,1)S(1)} %copy-done, bf16[4,224,1024]{2,1,0:T(8,128)(2,1)} %shard_map.56.rest_0_), custom_call_target="tpu_custom_call", output_to_operand_aliasing={{}: (2, {})} | custom-call | flops 822083584 | bytes 1835008 | tf_op jit(solution)/shard_map/pallas_call | solution.py:117
  65.1 4.9 %all-to-all-start.1 = ((bf16[4,224,1024]{2,1,0:T(8,128)(2,1)}), bf16[4,224,1024]{2,1,0:T(8,128)(2,1)S(1)}, u32[]{:S(2)}, u32[]{:S(2)}) async-start(bf16[4,224,1024]{2,1,0:T(8,128)(2,1)} %shard_map.57), calls=%async_computation.1 | async-start | bytes 3670016 | tf_op jit(solution)/shard_map/sum_x/all_to_all | solution.py:21
  72.0 5.1 %collective-permute-done.6 = bf16[2,4,16,512]{3,2,1,0:T(8,128)(2,1)S(1)} collective-permute-done((bf16[2,4,16,512]{3,2,1,0:T(8,128)(2,1)S(1)}, bf16[2,4,16,512]{3,2,1,0:T(8,128)(2,1)S(1)}, u32[]{:S(2)}, u32[]{:S(2)}) %collective-permute-start.6) | collective-permute-done | bytes 131104 | tf_op jit(solution)/shard_map/panel_gather/ppermute | solution.py:26
  78.1 3.3 %collective-permute-start.7 = (bf16[8,16,512]{2,1,0:T(8,128)(2,1)S(1)}, bf16[8,16,512]{2,1,0:T(8,128)(2,1)S(1)}, u32[]{:S(2)}, u32[]{:S(2)}) collective-permute-start(bf16[8,16,512]{2,1,0:T(8,128)(2,1)S(1)} %convert_element_type.21), channel_id=1, source_target_pairs={{0,2},{2,0},{4,6},{6,4},{8,10},{10,8},{12,14},{14,12},{1,3},{3,1},... | collective-permute-start | bytes 393224 | tf_op jit(solution)/shard_map/panel_sum/ppermute | solution.py:26
  81.4 3.6 %collective-permute-done.7 = bf16[8,16,512]{2,1,0:T(8,128)(2,1)S(1)} collective-permute-done((bf16[8,16,512]{2,1,0:T(8,128)(2,1)S(1)}, bf16[8,16,512]{2,1,0:T(8,128)(2,1)S(1)}, u32[]{:S(2)}, u32[]{:S(2)}) %collective-permute-start.7) | collective-permute-done | bytes 131104 | tf_op jit(solution)/shard_map/panel_sum/ppermute | solution.py:26
  85.0 4.0 %collective-permute-start.8 = (bf16[8,16,512]{2,1,0:T(8,128)(2,1)S(1)}, bf16[8,16,512]{2,1,0:T(8,128)(2,1)S(1)}, u32[]{:S(2)}, u32[]{:S(2)}) collective-permute-start(bf16[8,16,512]{2,1,0:T(8,128)(2,1)S(1)} %fusion), channel_id=1, source_target_pairs={{0,4},{2,6},{4,0},{6,2},{8,12},{10,14},{12,8},{14,10},{1,5},{3,7},... | collective-permute-start | bytes 393224 | tf_op jit(solution)/shard_map/panel_sum/ppermute | solution.py:26
  89.0 5.1 %collective-permute-done.8 = bf16[8,16,512]{2,1,0:T(8,128)(2,1)S(1)} collective-permute-done((bf16[8,16,512]{2,1,0:T(8,128)(2,1)S(1)}, bf16[8,16,512]{2,1,0:T(8,128)(2,1)S(1)}, u32[]{:S(2)}, u32[]{:S(2)}) %collective-permute-start.8) | collective-permute-done | bytes 131104 | tf_op jit(solution)/shard_map/panel_sum/ppermute | solution.py:26
  95.3 5.9 %all-to-all-start.2 = ((bf16[8,224,128]{2,1,0:T(8,128)(2,1)}), bf16[8,224,128]{2,1,0:T(8,128)(2,1)S(1)}, u32[]{:S(2)}, u32[]{:S(2)}) async-start(bf16[8,224,128]{2,1,0:T(8,128)(2,1)} %shard_map.59), calls=%async_computation.2 | async-start | bytes 917504 | tf_op jit(solution)/shard_map/sum_z/all_to_all | solution.py:21
  101.2 4.6 %collective-permute-start.9 = (bf16[8,16,512]{2,1,0:T(8,128)(2,1)S(1)}, bf16[8,16,512]{2,1,0:T(8,128)(2,1)S(1)}, u32[]{:S(2)}, u32[]{:S(2)}) collective-permute-start(bf16[8,16,512]{2,1,0:T(8,128)(2,1)S(1)} %convert_element_type.25), channel_id=1, source_target_pairs={{0,8},{2,10},{4,12},{6,14},{8,0},{10,2},{12,4},{14,6},{1,9},{3,11}... | collective-permute-start | bytes 393224 | tf_op jit(solution)/shard_map/panel_sum/ppermute | solution.py:26
  105.8 10.0 %all-to-all-done.2.parts_ref = bf16[8,224,128]{2,1,0:T(8,128)(2,1)S(1)} async-done(((bf16[8,224,128]{2,1,0:T(8,128)(2,1)}), bf16[8,224,128]{2,1,0:T(8,128)(2,1)S(1)}, u32[]{:S(2)}, u32[]{:S(2)}) %all-to-all-start.2) | async-done | bytes 458784 | tf_op jit(solution)/shard_map/sum_z/all_to_all | solution.py:21
  116.6 3.5 %all-to-all-start.3 = ((bf16[8,224,128]{2,1,0:T(8,128)(2,1)}), bf16[8,224,128]{2,1,0:T(8,128)(2,1)S(1)}, u32[]{:S(2)}, u32[]{:S(2)}) async-start(bf16[8,224,128]{2,1,0:T(8,128)(2,1)} %shard_map.60), calls=%async_computation.3 | async-start | bytes 917504 | tf_op jit(solution)/shard_map/rotated_z/all_to_all | solution.py:21
  120.2 3.6 %collective-permute-start.12 = (bf16[8,16,512]{2,1,0:T(8,128)(2,1)S(1)}, bf16[8,16,512]{2,1,0:T(8,128)(2,1)S(1)}, u32[]{:S(2)}, u32[]{:S(2)}) collective-permute-start(bf16[8,16,512]{2,1,0:T(8,128)(2,1)S(1)} %add_convert_fusion), channel_id=1, source_target_pairs={{0,48},{16,32},{32,16},{48,0},{1,49},{17,33},{33,17},{49,1},{2,50}... | collective-permute-start | bytes 393224 | tf_op jit(solution)/shard_map/panel_x/ppermute | solution.py:26
  123.7 2.9 %collective-permute-start.11 = (bf16[8,16,512]{2,1,0:T(8,128)(2,1)S(1)}, bf16[8,16,512]{2,1,0:T(8,128)(2,1)S(1)}, u32[]{:S(2)}, u32[]{:S(2)}) collective-permute-start(bf16[8,16,512]{2,1,0:T(8,128)(2,1)S(1)} %add_convert_fusion), channel_id=1, source_target_pairs={{0,32},{16,48},{32,0},{48,16},{1,33},{17,49},{33,1},{49,17},{2,34}... | collective-permute-start | bytes 393224 | tf_op jit(solution)/shard_map/panel_x/ppermute | solution.py:26
  126.6 3.4 %collective-permute-start.10 = (bf16[8,16,512]{2,1,0:T(8,128)(2,1)S(1)}, bf16[8,16,512]{2,1,0:T(8,128)(2,1)S(1)}, u32[]{:S(2)}, u32[]{:S(2)}) collective-permute-start(bf16[8,16,512]{2,1,0:T(8,128)(2,1)S(1)} %add_convert_fusion), channel_id=1, source_target_pairs={{0,16},{16,0},{32,48},{48,32},{1,17},{17,1},{33,49},{49,33},{2,18}... | collective-permute-start | bytes 393224 | tf_op jit(solution)/shard_map/panel_x/ppermute | solution.py:26
  137.4 2.8 %shard_map.61 = f32[4,224,128]{2,1,0:T(8,128)S(1)} custom-call(s32[2]{0:T(128)S(1)} %pad_add_fusion.at_ref, bf16[8,224,128]{2,1,0:T(8,128)(2,1)S(1)} %all-to-all-done.3.left_ref, bf16[4,8,16,512]{3,2,1,0:T(8,128)(2,1)S(1)} %pad_maximum_fusion.2.own_ref, bf16[4,8,16,512]{3,2,1,0:T(8,128)(2,1)S(1)} %collective-permute-done.13.other_ref), custom_call_target="tpu_custom_call" | custom-call | flops 234881024 | bytes 1048576 | tf_op jit(solution)/shard_map/pallas_call | solution.py:227
  140.2 12.7 %all_to_all.25 = f32[4,224,128]{2,1,0:T(8,128)S(1)} all-to-all(f32[4,224,128]{2,1,0:T(8,128)S(1)} %shard_map.61), channel_id=1, replica_groups=mesh['z'=8,'x'=4,'y'=8,'c'=2] {'x'}, dimensions={0} | all-to-all | bytes 917504 | tf_op jit(solution)/shard_map/out_x/all_to_all | solution.py:21
  (42 shorter events, 24.0 us)
Async XLA Ops:
  0.7 15.6 %copy-start.1 = (bf16[512,128]{1,0:T(8,128)(2,1)S(1)}, bf16[512,128]{1,0:T(8,128)(2,1)}, u32[]{:S(2)}) copy-start(bf16[512,128]{1,0:T(8,128)(2,1)} %param.8) | copy-start | bytes 393220
  3.0 48.9 %all-to-all-start = ((bf16[32,16,896]{2,1,0:T(8,128)(2,1)}), bf16[32,16,896]{2,1,0:T(8,128)(2,1)}, u32[]{:S(2)}, u32[]{:S(2)}) async-start(bf16[32,16,896]{2,1,0:T(8,128)(2,1)} %shard_map.55), calls=%async_computation | async-start | bytes 1835008 | tf_op jit(solution)/shard_map/rows_dp/all_to_all | solution.py:21
  16.3 10.6 %collective-permute-start.1 = (bf16[1,512,128]{2,1,0:T(8,128)(2,1)S(1)}, bf16[1,512,128]{2,1,0:T(8,128)(2,1)S(1)}, u32[]{:S(2)}, u32[]{:S(2)}) collective-permute-start(bf16[1,512,128]{2,1,0:T(8,128)(2,1)S(1)} %bitcast.19), channel_id=1, source_target_pairs={{0,32},{16,48},{32,0},{48,16},{1,33},{17,49},{33,1},{49,17},{2,34}... | collective-permute-start | bytes 393224 | tf_op jit(solution)/shard_map/panel_gather/ppermute | solution.py:26
  26.9 31.7 %copy-start = (bf16[896,896]{1,0:T(8,128)(2,1)S(1)}, bf16[896,896]{1,0:T(8,128)(2,1)}, u32[]{:S(2)}) copy-start(bf16[896,896]{1,0:T(8,128)(2,1)} %basis_ref.3) | copy-start | bytes 4816900
  26.9 12.5 %collective-permute-start.2 = (bf16[2,512,128]{2,1,0:T(8,128)(2,1)S(1)}, bf16[2,512,128]{2,1,0:T(8,128)(2,1)S(1)}, u32[]{:S(2)}, u32[]{:S(2)}) collective-permute-start(bf16[2,512,128]{2,1,0:T(8,128)(2,1)S(1)} %pad_maximum_fusion.3), channel_id=1, source_target_pairs={{0,16},{16,0},{32,48},{48,32},{1,17},{17,1},{33,49},{49,33},{2,18}... | collective-permute-start | bytes 786440 | tf_op jit(solution)/shard_map/panel_gather/ppermute | solution.py:26
  39.5 9.2 %collective-permute-start.3 = (bf16[4,512,128]{2,1,0:T(8,128)(2,1)S(1)}, bf16[4,512,128]{2,1,0:T(8,128)(2,1)S(1)}, u32[]{:S(2)}, u32[]{:S(2)}) collective-permute-start(bf16[4,512,128]{2,1,0:T(8,128)(2,1)S(1)} %get-tuple-element.20), channel_id=1, source_target_pairs={{0,1},{1,0},{2,3},{3,2},{4,5},{5,4},{6,7},{7,6},{8,9},{9,8},{10,11... | collective-permute-start | bytes 1572872 | tf_op jit(solution)/shard_map/panel_gather/ppermute | solution.py:26
  42.2 9.7 %collective-permute-start = (bf16[2,1,16,512]{3,2,1,0:T(8,128)(2,1)S(1)}, bf16[2,1,16,512]{3,2,1,0:T(8,128)(2,1)S(1)}, u32[]{:S(2)}, u32[]{:S(2)}) collective-permute-start(bf16[2,1,16,512]{3,2,1,0:T(8,128)(2,1)S(1)} %maximum_bitcast_fusion), channel_id=1, source_target_pairs={{0,256},{64,320},{128,384},{192,448},{256,0},{320,64},{384,128},{4... | collective-permute-start | bytes 98312 | tf_op jit(solution)/shard_map/panel_gather/ppermute | solution.py:26
  48.7 0.8 copy-start.2
  51.9 10.8 %collective-permute-start.4 = (bf16[512,896]{1,0:T(8,128)(2,1)}, bf16[512,896]{1,0:T(8,128)(2,1)S(1)}, u32[]{:S(2)}, u32[]{:S(2)}) collective-permute-start(bf16[512,896]{1,0:T(8,128)(2,1)} %bitcast.2.tokens_ref), channel_id=1, source_target_pairs={{0,1},{1,0},{2,3},{3,2},{4,5},{5,4},{6,7},{7,6},{8,9},{9,8},{10,11... | collective-permute-start | bytes 2752520 | tf_op jit(solution)/shard_map/rows_c/ppermute | solution.py:26
  53.8 8.9 %collective-permute-start.5 = (bf16[2,2,16,512]{3,2,1,0:T(8,128)(2,1)S(1)}, bf16[2,2,16,512]{3,2,1,0:T(8,128)(2,1)S(1)}, u32[]{:S(2)}, u32[]{:S(2)}) collective-permute-start(bf16[2,2,16,512]{3,2,1,0:T(8,128)(2,1)S(1)} %pad_maximum_fusion.6), channel_id=1, source_target_pairs={{0,128},{64,192},{128,0},{192,64},{256,384},{320,448},{384,256},{4... | collective-permute-start | bytes 196616 | tf_op jit(solution)/shard_map/panel_gather/ppermute | solution.py:26
  65.1 29.1 %all-to-all-start.1 = ((bf16[4,224,1024]{2,1,0:T(8,128)(2,1)}), bf16[4,224,1024]{2,1,0:T(8,128)(2,1)S(1)}, u32[]{:S(2)}, u32[]{:S(2)}) async-start(bf16[4,224,1024]{2,1,0:T(8,128)(2,1)} %shard_map.57), calls=%async_computation.1 | async-start | bytes 3670016 | tf_op jit(solution)/shard_map/sum_x/all_to_all | solution.py:21
  70.0 7.1 %collective-permute-start.6 = (bf16[2,4,16,512]{3,2,1,0:T(8,128)(2,1)S(1)}, bf16[2,4,16,512]{3,2,1,0:T(8,128)(2,1)S(1)}, u32[]{:S(2)}, u32[]{:S(2)}) collective-permute-start(bf16[2,4,16,512]{3,2,1,0:T(8,128)(2,1)S(1)} %pad_maximum_fusion.5), channel_id=1, source_target_pairs={{0,64},{64,0},{128,192},{192,128},{256,320},{320,256},{384,448},{4... | collective-permute-start | bytes 393224 | tf_op jit(solution)/shard_map/panel_gather/ppermute | solution.py:26
  78.1 6.9 %collective-permute-start.7 = (bf16[8,16,512]{2,1,0:T(8,128)(2,1)S(1)}, bf16[8,16,512]{2,1,0:T(8,128)(2,1)S(1)}, u32[]{:S(2)}, u32[]{:S(2)}) collective-permute-start(bf16[8,16,512]{2,1,0:T(8,128)(2,1)S(1)} %convert_element_type.21), channel_id=1, source_target_pairs={{0,2},{2,0},{4,6},{6,4},{8,10},{10,8},{12,14},{14,12},{1,3},{3,1},... | collective-permute-start | bytes 393224 | tf_op jit(solution)/shard_map/panel_sum/ppermute | solution.py:26
  85.0 9.2 %collective-permute-start.8 = (bf16[8,16,512]{2,1,0:T(8,128)(2,1)S(1)}, bf16[8,16,512]{2,1,0:T(8,128)(2,1)S(1)}, u32[]{:S(2)}, u32[]{:S(2)}) collective-permute-start(bf16[8,16,512]{2,1,0:T(8,128)(2,1)S(1)} %fusion), channel_id=1, source_target_pairs={{0,4},{2,6},{4,0},{6,2},{8,12},{10,14},{12,8},{14,10},{1,5},{3,7},... | collective-permute-start | bytes 393224 | tf_op jit(solution)/shard_map/panel_sum/ppermute | solution.py:26
  95.3 20.5 %all-to-all-start.2 = ((bf16[8,224,128]{2,1,0:T(8,128)(2,1)}), bf16[8,224,128]{2,1,0:T(8,128)(2,1)S(1)}, u32[]{:S(2)}, u32[]{:S(2)}) async-start(bf16[8,224,128]{2,1,0:T(8,128)(2,1)} %shard_map.59), calls=%async_computation.2 | async-start | bytes 917504 | tf_op jit(solution)/shard_map/sum_z/all_to_all | solution.py:21
  101.2 18.9 %collective-permute-start.9 = (bf16[8,16,512]{2,1,0:T(8,128)(2,1)S(1)}, bf16[8,16,512]{2,1,0:T(8,128)(2,1)S(1)}, u32[]{:S(2)}, u32[]{:S(2)}) collective-permute-start(bf16[8,16,512]{2,1,0:T(8,128)(2,1)S(1)} %convert_element_type.25), channel_id=1, source_target_pairs={{0,8},{2,10},{4,12},{6,14},{8,0},{10,2},{12,4},{14,6},{1,9},{3,11}... | collective-permute-start | bytes 393224 | tf_op jit(solution)/shard_map/panel_sum/ppermute | solution.py:26
  116.6 20.7 %all-to-all-start.3 = ((bf16[8,224,128]{2,1,0:T(8,128)(2,1)}), bf16[8,224,128]{2,1,0:T(8,128)(2,1)S(1)}, u32[]{:S(2)}, u32[]{:S(2)}) async-start(bf16[8,224,128]{2,1,0:T(8,128)(2,1)} %shard_map.60), calls=%async_computation.3 | async-start | bytes 917504 | tf_op jit(solution)/shard_map/rotated_z/all_to_all | solution.py:21
  120.2 9.8 %collective-permute-start.12 = (bf16[8,16,512]{2,1,0:T(8,128)(2,1)S(1)}, bf16[8,16,512]{2,1,0:T(8,128)(2,1)S(1)}, u32[]{:S(2)}, u32[]{:S(2)}) collective-permute-start(bf16[8,16,512]{2,1,0:T(8,128)(2,1)S(1)} %add_convert_fusion), channel_id=1, source_target_pairs={{0,48},{16,32},{32,16},{48,0},{1,49},{17,33},{33,17},{49,1},{2,50}... | collective-permute-start | bytes 393224 | tf_op jit(solution)/shard_map/panel_x/ppermute | solution.py:26
  123.7 8.4 %collective-permute-start.11 = (bf16[8,16,512]{2,1,0:T(8,128)(2,1)S(1)}, bf16[8,16,512]{2,1,0:T(8,128)(2,1)S(1)}, u32[]{:S(2)}, u32[]{:S(2)}) collective-permute-start(bf16[8,16,512]{2,1,0:T(8,128)(2,1)S(1)} %add_convert_fusion), channel_id=1, source_target_pairs={{0,32},{16,48},{32,0},{48,16},{1,33},{17,49},{33,1},{49,17},{2,34}... | collective-permute-start | bytes 393224 | tf_op jit(solution)/shard_map/panel_x/ppermute | solution.py:26
  126.6 6.9 %collective-permute-start.10 = (bf16[8,16,512]{2,1,0:T(8,128)(2,1)S(1)}, bf16[8,16,512]{2,1,0:T(8,128)(2,1)S(1)}, u32[]{:S(2)}, u32[]{:S(2)}) collective-permute-start(bf16[8,16,512]{2,1,0:T(8,128)(2,1)S(1)} %add_convert_fusion), channel_id=1, source_target_pairs={{0,16},{16,0},{32,48},{48,32},{1,17},{17,1},{33,49},{49,33},{2,18}... | collective-permute-start | bytes 393224 | tf_op jit(solution)/shard_map/panel_x/ppermute | solution.py:26
  133.6 3.8 %collective-permute-start.13 = (bf16[4,8,16,512]{3,2,1,0:T(8,128)(2,1)S(1)}, bf16[4,8,16,512]{3,2,1,0:T(8,128)(2,1)S(1)}, u32[]{:S(2)}, u32[]{:S(2)}) collective-permute-start(bf16[4,8,16,512]{3,2,1,0:T(8,128)(2,1)S(1)} %pad_maximum_fusion.2.own_ref), channel_id=1, source_target_pairs={{0,1},{1,0},{2,3},{3,2},{4,5},{5,4},{6,7},{7,6},{8,9},{9,8},{10,11... | collective-permute-start | bytes 1572872 | tf_op jit(solution)/shard_map/panel_c/ppermute | solution.py:26

commit v5 on v4

--- a/solution.py
+++ b/solution.py
@@ -26,11 +26,6 @@
     return lax.ppermute(block, axis, [(i, i ^ bit) for i in range(count)])
 
 
-def bits(axis):
-    count = lax.axis_size(axis)
-    return [1 << k for k in reversed(range(count.bit_length() - 1))]
-
-
 def reverse(index, width):
     result = 0
     for k in range(width):
@@ -38,10 +33,9 @@
     return result
 
 
-def double(block, axis):
-    for bit in bits(axis):
-        block = jnp.concatenate([block, swap(block, axis, bit)], axis=0)
-    return block
+def direct(block, axis):
+    count = lax.axis_size(axis)
+    return jnp.stack([block] + [swap(block, axis, k) for k in range(1, count)])
 
 
 def add_from(block, axis, bit):
@@ -172,28 +166,29 @@
 
 
 def panel_kernel(at_ref, slab_ref, basis_ref, out_ref):
-    cores, count, slots, deep = slab_ref.shape
-    for q in range(basis_ref.shape[1]):
-        total = jnp.zeros((count * slots, basis_ref.shape[3]), F32)
-        for r in range(cores):
-            left = slab_ref[r].reshape(count * slots, deep)
-            right = basis_ref[r, reverse(q ^ at_ref[0], 2)]
-            total = total + jnp.dot(left, right, preferred_element_type=F32)
-        lanes = total.shape[1]
+    cores, nx, chips, _, lanes = basis_ref.shape
+    count, slots, _ = out_ref.shape
+    for q in range(nx):
+        total = jnp.zeros((count * slots, lanes), F32)
+        for yr in range(chips):
+            for cr in range(cores):
+                left = slab_ref[yr * cores + cr]
+                right = basis_ref[cr, q ^ at_ref[0], yr]
+                total = total + jnp.dot(left, right, preferred_element_type=F32)
         out_ref[:, :, q * lanes : (q + 1) * lanes] = total.reshape(count, slots, lanes)
 
 
 def panel_part(at, slab, basis):
-    cores, count, slots, deep = slab.shape
-    columns = basis.shape[1] * basis.shape[3]
+    terms, count, slots, deep = slab.shape
+    columns = basis.shape[1] * basis.shape[4]
     return pl.pallas_call(
         panel_kernel,
         out_shape=jax.ShapeDtypeStruct((count, slots, columns), F32),
         in_specs=[pl.BlockSpec(memory_space=SMEM)] + [pl.BlockSpec(memory_space=VMEM)] * 2,
         out_specs=pl.BlockSpec(memory_space=VMEM),
         compiler_params=PARAMS,
-        cost_estimate=cost(2 * count * slots * columns * deep * cores, 2 * basis.size),
-    )(at, slab, basis)
+        cost_estimate=cost(2 * count * slots * columns * deep * terms, 2 * basis.size),
+    )(at, slab.reshape(terms, count * slots, deep), basis)
 
 
 def example_kernel(nx, scale, at_ref, left_ref, own_ref, other_ref, out_ref):
@@ -248,44 +243,41 @@
     with jax.named_scope("rows_dp"):
         own = exchange(blocks, DP).reshape(nz * nx * half, wide)
 
-    mine = lax.dynamic_slice(inputs, (ic * half, (iy * nc + ic) * deep), (half, deep))
-    theirs = lax.dynamic_slice(inputs, (ic * half, (iy * nc + 1 - ic) * deep), (half, deep))
-    slab = jnp.stack([mine, theirs])[:, None]
-    basis_x = basis_in[None]
-    with jax.named_scope("panel_gather"):
-        more_slab = swap(slab, "z", 4)
-        basis_x = double(basis_x, "x")
+    def features(yr, cr):
+        start = ((iy ^ yr) * nc + (ic ^ cr)) * deep
+        return lax.dynamic_slice(inputs, (ic * half, start), (half, deep))
+
+    slab = jnp.stack([features(yr, cr) for yr in range(2) for cr in range(2)])[:, None]
+    with jax.named_scope("basis_yxc"):
+        basis_x = jnp.stack([basis_in, swap(basis_in, "y", 1)])
+        basis_x = direct(basis_x, "x")
+        own, basis_x, slab = tie((own, basis_x, slab))
         basis_x = jnp.stack([basis_x, swap(basis_x, "c", 1)])
-        own, more_slab, basis_x = tie((own, more_slab, basis_x))
-        slab = jnp.concatenate([slab, more_slab], axis=1)
-        more_slab = swap(slab, "z", 2)
 
     with jax.named_scope("rows_c"):
         other = swap(own, "c", 1)
     parts = rotate(own, basis_out, 0, nx)
-    other, more_slab = tie((other, more_slab))
+    other, basis_x = tie((other, basis_x))
     parts = rotate(other, basis_out, 1, nx, parts)
     with jax.named_scope("sum_x"):
         parts = exchange(parts, "x")
 
-    with jax.named_scope("panel_gather"):
-        slab = jnp.concatenate([slab, more_slab], axis=1)
-        slab = jnp.concatenate([slab, swap(slab, "z", 1)], axis=1)
+    with jax.named_scope("slab_z"):
+        for bit in (4, 2, 1):
+            slab = jnp.concatenate([slab, swap(slab, "z", bit)], axis=1)
     piece = panel_part(at, slab, basis_x)
-    with jax.named_scope("panel_sum"):
-        piece = add_from(piece, "y", 1)
-        piece = add_from(piece, "y", 2)
     parts, piece = tie((parts, piece))
     parts = sum_lanes(parts)
     with jax.named_scope("sum_z"):
         parts = exchange(parts, "z")
     with jax.named_scope("panel_sum"):
+        piece = add_from(piece, "y", 2)
         piece = add_from(piece, "y", 4).astype(BF)
     rotated = sum_parts(parts, nz)
     with jax.named_scope("rotated_z"):
         rotated = exchange(rotated, "z")
     with jax.named_scope("panel_x"):
-        piece = jnp.stack([piece] + [swap(piece, "x", k) for k in range(1, 4)])
+        piece = direct(piece, "x")
     with jax.named_scope("panel_c"):
         piece_other = swap(piece, "c", 1)
 

time: 155 us -> 166 us (1.071)
  the two profiles are of different devices: /device:TPU:56 before, /device:TPU:1 now
where the time goes in v5:
time: 166 us; the launch traced here: 165 us
  starting transfers between devices  89 us (54%)
  waiting for transfers between devices  45.1 us (27%)
  Pallas kernels  14.1 us (8%)
  blocking collectives  10.6 us (6%)
  other arithmetic  2.83 us (2%)
  local copies, waits for them, and re-layouts  2.78 us (2%)
    ppermute x15, starting transfers between devices, swap(): return lax.ppermute(block, axis, [(i, i ^ bit) for i in range(count)])  61.1 us
    ppermute x15, waiting for transfers between devices, swap(): return lax.ppermute(block, axis, [(i, i ^ bit) for i in range(count)])  45.1 us
    all_to_all x4, starting transfers between devices, exchange(): return lax.all_to_all(blocks, axis, split_axis=0, concat_axis=0, tiled=True)  27.8 us
    all_to_all x1, blocking collectives, exchange(): return lax.all_to_all(blocks, axis, split_axis=0, concat_axis=0, tiled=True)  10.6 us
    pallas_call x2, Pallas kernels, rotate(): pl.pallas_call(rotate_kernel, out_shape=jax.ShapeDtypeStruct((pieces, row...  4.61 us
  transfers between devices with their start and end apart: 19, of which 10 were waited for; matrix products, arithmetic and copies ran while one was open for 2% of the time, Pallas kernels for 3%

profile of v5, /device:TPU:1, one launch (start us, length us, event | category | flops | bytes accessed | tf_op | source)
XLA Modules:
  0.0 165.4 jit_solution(2919074746135397922)
XLA Ops:
  3.0 13.7 %all-to-all-start = ((bf16[32,16,896]{2,1,0:T(8,128)(2,1)}), bf16[32,16,896]{2,1,0:T(8,128)(2,1)S(1)}, u32[]{:S(2)}, u32[]{:S(2)}) async-start(bf16[32,16,896]{2,1,0:T(8,128)(2,1)} %shard_map.55), calls=%async_computation | async-start | bytes 1835008 | tf_op jit(solution)/shard_map/rows_dp/all_to_all | solution.py:21
  16.7 3.3 %collective-permute-start = (bf16[512,128]{1,0:T(8,128)(2,1)S(1)}, bf16[512,128]{1,0:T(8,128)(2,1)S(1)}, u32[]{:S(2)}, u32[]{:S(2)}) collective-permute-start(bf16[512,128]{1,0:T(8,128)(2,1)S(1)} %copy-done.3), channel_id=1, source_target_pairs={{0,2},{2,0},{4,6},{6,4},{8,10},{10,8},{12,14},{14,12},{1,3},{3,1},... | collective-permute-start | bytes 393224 | tf_op jit(solution)/shard_map/basis_yxc/ppermute | solution.py:26
  20.1 2.7 %collective-permute-done = bf16[512,128]{1,0:T(8,128)(2,1)S(1)} collective-permute-done((bf16[512,128]{1,0:T(8,128)(2,1)S(1)}, bf16[512,128]{1,0:T(8,128)(2,1)S(1)}, u32[]{:S(2)}, u32[]{:S(2)}) %collective-permute-start) | collective-permute-done | bytes 131104 | tf_op jit(solution)/shard_map/basis_yxc/ppermute | solution.py:26
  22.9 3.1 %collective-permute-start.1 = (bf16[2,512,128]{2,1,0:T(8,128)(2,1)S(1)}, bf16[2,512,128]{2,1,0:T(8,128)(2,1)}, u32[]{:S(2)}, u32[]{:S(2)}) collective-permute-start(bf16[2,512,128]{2,1,0:T(8,128)(2,1)S(1)} %get-tuple-element.24), channel_id=1, source_target_pairs={{0,16},{16,0},{32,48},{48,32},{1,17},{17,1},{33,49},{49,33},{2,18}... | collective-permute-start | bytes 786440 | tf_op jit(solution)/shard_map/basis_yxc/ppermute | solution.py:26
  25.9 4.4 %collective-permute-start.2 = (bf16[2,512,128]{2,1,0:T(8,128)(2,1)S(1)}, bf16[2,512,128]{2,1,0:T(8,128)(2,1)}, u32[]{:S(2)}, u32[]{:S(2)}) collective-permute-start(bf16[2,512,128]{2,1,0:T(8,128)(2,1)S(1)} %get-tuple-element.24), channel_id=1, source_target_pairs={{0,32},{16,48},{32,0},{48,16},{1,33},{17,49},{33,1},{49,17},{2,34}... | collective-permute-start | bytes 786440 | tf_op jit(solution)/shard_map/basis_yxc/ppermute | solution.py:26
  34.3 11.3 %collective-permute-done.2 = bf16[2,512,128]{2,1,0:T(8,128)(2,1)} collective-permute-done((bf16[2,512,128]{2,1,0:T(8,128)(2,1)S(1)}, bf16[2,512,128]{2,1,0:T(8,128)(2,1)}, u32[]{:S(2)}, u32[]{:S(2)}) %collective-permute-start.2) | collective-permute-done | bytes 262176 | tf_op jit(solution)/shard_map/basis_yxc/ppermute | solution.py:26
  50.5 4.3 %collective-permute-start.5 = (bf16[4,2,512,128]{3,2,1,0:T(8,128)(2,1)}, bf16[4,2,512,128]{3,2,1,0:T(8,128)(2,1)S(1)}, u32[]{:S(2)}, u32[]{:S(2)}) collective-permute-start(bf16[4,2,512,128]{3,2,1,0:T(8,128)(2,1)} %pad_maximum_fusion.1), channel_id=1, source_target_pairs={{0,1},{1,0},{2,3},{3,2},{4,5},{5,4},{6,7},{7,6},{8,9},{9,8},{10,11... | collective-permute-start | bytes 3145736 | tf_op jit(solution)/shard_map/basis_yxc/ppermute | solution.py:26
  62.7 4.4 %all-to-all-start.1 = ((bf16[4,224,1024]{2,1,0:T(8,128)(2,1)}), bf16[4,224,1024]{2,1,0:T(8,128)(2,1)}, u32[]{:S(2)}, u32[]{:S(2)}) async-start(bf16[4,224,1024]{2,1,0:T(8,128)(2,1)} %shard_map.57), calls=%async_computation.1 | async-start | bytes 3670016 | tf_op jit(solution)/shard_map/sum_x/all_to_all | solution.py:21
  67.2 6.3 %collective-permute-start.6 = (bf16[4,1,16,512]{3,2,1,0:T(8,128)(2,1)S(1)}, bf16[4,1,16,512]{3,2,1,0:T(8,128)(2,1)S(1)}, u32[]{:S(2)}, u32[]{:S(2)}) collective-permute-start(bf16[4,1,16,512]{3,2,1,0:T(8,128)(2,1)S(1)} %maximum_bitcast_fusion), channel_id=1, source_target_pairs={{0,256},{64,320},{128,384},{192,448},{256,0},{320,64},{384,128},{4... | collective-permute-start | bytes 196616 | tf_op jit(solution)/shard_map/slab_z/ppermute | solution.py:26
  73.4 2.7 %collective-permute-done.6 = bf16[4,1,16,512]{3,2,1,0:T(8,128)(2,1)S(1)} collective-permute-done((bf16[4,1,16,512]{3,2,1,0:T(8,128)(2,1)S(1)}, bf16[4,1,16,512]{3,2,1,0:T(8,128)(2,1)S(1)}, u32[]{:S(2)}, u32[]{:S(2)}) %collective-permute-start.6) | collective-permute-done | bytes 65568 | tf_op jit(solution)/shard_map/slab_z/ppermute | solution.py:26
  76.2 5.9 %collective-permute-start.7 = (bf16[4,2,16,512]{3,2,1,0:T(8,128)(2,1)S(1)}, bf16[4,2,16,512]{3,2,1,0:T(8,128)(2,1)S(1)}, u32[]{:S(2)}, u32[]{:S(2)}) collective-permute-start(bf16[4,2,16,512]{3,2,1,0:T(8,128)(2,1)S(1)} %pad_maximum_fusion.6), channel_id=1, source_target_pairs={{0,128},{64,192},{128,0},{192,64},{256,384},{320,448},{384,256},{4... | collective-permute-start | bytes 393224 | tf_op jit(solution)/shard_map/slab_z/ppermute | solution.py:26
  82.1 5.8 %collective-permute-done.7 = bf16[4,2,16,512]{3,2,1,0:T(8,128)(2,1)S(1)} collective-permute-done((bf16[4,2,16,512]{3,2,1,0:T(8,128)(2,1)S(1)}, bf16[4,2,16,512]{3,2,1,0:T(8,128)(2,1)S(1)}, u32[]{:S(2)}, u32[]{:S(2)}) %collective-permute-start.7) | collective-permute-done | bytes 131104 | tf_op jit(solution)/shard_map/slab_z/ppermute | solution.py:26
  90.0 7.2 %collective-permute-done.8 = bf16[4,4,16,512]{3,2,1,0:T(8,128)(2,1)S(1)} collective-permute-done((bf16[4,4,16,512]{3,2,1,0:T(8,128)(2,1)S(1)}, bf16[4,4,16,512]{3,2,1,0:T(8,128)(2,1)S(1)}, u32[]{:S(2)}, u32[]{:S(2)}) %collective-permute-start.8) | collective-permute-done | bytes 262176 | tf_op jit(solution)/shard_map/slab_z/ppermute | solution.py:26
  100.8 3.5 %all-to-all-start.2 = ((bf16[8,224,128]{2,1,0:T(8,128)(2,1)}), bf16[8,224,128]{2,1,0:T(8,128)(2,1)S(1)}, u32[]{:S(2)}, u32[]{:S(2)}) async-start(bf16[8,224,128]{2,1,0:T(8,128)(2,1)} %shard_map.59), calls=%async_computation.2 | async-start | bytes 917504 | tf_op jit(solution)/shard_map/sum_z/all_to_all | solution.py:21
  104.3 4.2 %collective-permute-start.9 = (bf16[8,16,512]{2,1,0:T(8,128)(2,1)S(1)}, bf16[8,16,512]{2,1,0:T(8,128)(2,1)S(1)}, u32[]{:S(2)}, u32[]{:S(2)}) collective-permute-start(bf16[8,16,512]{2,1,0:T(8,128)(2,1)S(1)} %convert_element_type.15), channel_id=1, source_target_pairs={{0,4},{2,6},{4,0},{6,2},{8,12},{10,14},{12,8},{14,10},{1,5},{3,7},... | collective-permute-start | bytes 393224 | tf_op jit(solution)/shard_map/panel_sum/ppermute | solution.py:26
  108.5 5.7 %collective-permute-done.9 = bf16[8,16,512]{2,1,0:T(8,128)(2,1)S(1)} collective-permute-done((bf16[8,16,512]{2,1,0:T(8,128)(2,1)S(1)}, bf16[8,16,512]{2,1,0:T(8,128)(2,1)S(1)}, u32[]{:S(2)}, u32[]{:S(2)}) %collective-permute-start.9) | collective-permute-done | bytes 131104 | tf_op jit(solution)/shard_map/panel_sum/ppermute | solution.py:26
  114.3 8.0 %collective-permute-start.10 = (bf16[8,16,512]{2,1,0:T(8,128)(2,1)S(1)}, bf16[8,16,512]{2,1,0:T(8,128)(2,1)S(1)}, u32[]{:S(2)}, u32[]{:S(2)}) collective-permute-start(bf16[8,16,512]{2,1,0:T(8,128)(2,1)S(1)} %fusion), channel_id=1, source_target_pairs={{0,8},{2,10},{4,12},{6,14},{8,0},{10,2},{12,4},{14,6},{1,9},{3,11}... | collective-permute-start | bytes 393224 | tf_op jit(solution)/shard_map/panel_sum/ppermute | solution.py:26
  123.1 6.2 %all-to-all-start.3 = ((bf16[8,224,128]{2,1,0:T(8,128)(2,1)}), bf16[8,224,128]{2,1,0:T(8,128)(2,1)S(1)}, u32[]{:S(2)}, u32[]{:S(2)}) async-start(bf16[8,224,128]{2,1,0:T(8,128)(2,1)} %shard_map.60), calls=%async_computation.3 | async-start | bytes 917504 | tf_op jit(solution)/shard_map/rotated_z/all_to_all | solution.py:21
  131.3 3.7 %collective-permute-start.12 = (bf16[8,16,512]{2,1,0:T(8,128)(2,1)S(1)}, bf16[8,16,512]{2,1,0:T(8,128)(2,1)S(1)}, u32[]{:S(2)}, u32[]{:S(2)}) collective-permute-start(bf16[8,16,512]{2,1,0:T(8,128)(2,1)S(1)} %add_convert_fusion), channel_id=1, source_target_pairs={{0,32},{16,48},{32,0},{48,16},{1,33},{17,49},{33,1},{49,17},{2,34}... | collective-permute-start | bytes 393224 | tf_op jit(solution)/shard_map/panel_x/ppermute | solution.py:26
  135.1 3.9 %collective-permute-start.13 = (bf16[8,16,512]{2,1,0:T(8,128)(2,1)S(1)}, bf16[8,16,512]{2,1,0:T(8,128)(2,1)S(1)}, u32[]{:S(2)}, u32[]{:S(2)}) collective-permute-start(bf16[8,16,512]{2,1,0:T(8,128)(2,1)S(1)} %add_convert_fusion), channel_id=1, source_target_pairs={{0,48},{16,32},{32,16},{48,0},{1,49},{17,33},{33,17},{49,1},{2,50}... | collective-permute-start | bytes 393224 | tf_op jit(solution)/shard_map/panel_x/ppermute | solution.py:26
  139.0 4.4 %collective-permute-done.13 = bf16[8,16,512]{2,1,0:T(8,128)(2,1)S(1)} collective-permute-done((bf16[8,16,512]{2,1,0:T(8,128)(2,1)S(1)}, bf16[8,16,512]{2,1,0:T(8,128)(2,1)S(1)}, u32[]{:S(2)}, u32[]{:S(2)}) %collective-permute-start.13) | collective-permute-done | bytes 131104 | tf_op jit(solution)/shard_map/panel_x/ppermute | solution.py:26
  143.5 6.1 %collective-permute-start.14 = (bf16[4,8,16,512]{3,2,1,0:T(8,128)(2,1)S(1)}, bf16[4,8,16,512]{3,2,1,0:T(8,128)(2,1)S(1)}, u32[]{:S(2)}, u32[]{:S(2)}) collective-permute-start(bf16[4,8,16,512]{3,2,1,0:T(8,128)(2,1)S(1)} %pad_maximum_fusion.3.own_ref), channel_id=1, source_target_pairs={{0,1},{1,0},{2,3},{3,2},{4,5},{5,4},{6,7},{7,6},{8,9},{9,8},{10,11... | collective-permute-start | bytes 1572872 | tf_op jit(solution)/shard_map/panel_c/ppermute | solution.py:26
  151.1 2.8 %shard_map.61 = f32[4,224,128]{2,1,0:T(8,128)S(1)} custom-call(s32[2]{0:T(128)S(1)} %pad_add_fusion.at_ref, bf16[8,224,128]{2,1,0:T(8,128)(2,1)S(1)} %all-to-all-done.3.left_ref, bf16[4,8,16,512]{3,2,1,0:T(8,128)(2,1)S(1)} %pad_maximum_fusion.3.own_ref, bf16[4,8,16,512]{3,2,1,0:T(8,128)(2,1)S(1)} %collective-permute-done.14.other_ref), custom_call_target="tpu_custom_call" | custom-call | flops 234881024 | bytes 1048576 | tf_op jit(solution)/shard_map/pallas_call | solution.py:222
  154.0 10.6 %all_to_all.25 = f32[4,224,128]{2,1,0:T(8,128)S(1)} all-to-all(f32[4,224,128]{2,1,0:T(8,128)S(1)} %shard_map.61), channel_id=1, replica_groups=mesh['z'=8,'x'=4,'y'=8,'c'=2] {'x'}, dimensions={0} | all-to-all | bytes 917504 | tf_op jit(solution)/shard_map/out_x/all_to_all | solution.py:21
  (44 shorter events, 29.9 us)
Async XLA Ops:
  0.7 16.1 %copy-start.3 = (bf16[512,128]{1,0:T(8,128)(2,1)S(1)}, bf16[512,128]{1,0:T(8,128)(2,1)}, u32[]{:S(2)}) copy-start(bf16[512,128]{1,0:T(8,128)(2,1)} %param.8) | copy-start | bytes 393220
  3.0 47.5 %all-to-all-start = ((bf16[32,16,896]{2,1,0:T(8,128)(2,1)}), bf16[32,16,896]{2,1,0:T(8,128)(2,1)S(1)}, u32[]{:S(2)}, u32[]{:S(2)}) async-start(bf16[32,16,896]{2,1,0:T(8,128)(2,1)} %shard_map.55), calls=%async_computation | async-start | bytes 1835008 | tf_op jit(solution)/shard_map/rows_dp/all_to_all | solution.py:21
  16.7 40.0 %copy-start = (bf16[896,896]{1,0:T(8,128)(2,1)S(1)}, bf16[896,896]{1,0:T(8,128)(2,1)}, u32[]{:S(2)}) copy-start(bf16[896,896]{1,0:T(8,128)(2,1)} %basis_ref.3) | copy-start | bytes 4816900
  16.7 6.1 %collective-permute-start = (bf16[512,128]{1,0:T(8,128)(2,1)S(1)}, bf16[512,128]{1,0:T(8,128)(2,1)S(1)}, u32[]{:S(2)}, u32[]{:S(2)}) collective-permute-start(bf16[512,128]{1,0:T(8,128)(2,1)S(1)} %copy-done.3), channel_id=1, source_target_pairs={{0,2},{2,0},{4,6},{6,4},{8,10},{10,8},{12,14},{14,12},{1,3},{3,1},... | collective-permute-start | bytes 393224 | tf_op jit(solution)/shard_map/basis_yxc/ppermute | solution.py:26
  22.9 11.5 %collective-permute-start.1 = (bf16[2,512,128]{2,1,0:T(8,128)(2,1)S(1)}, bf16[2,512,128]{2,1,0:T(8,128)(2,1)}, u32[]{:S(2)}, u32[]{:S(2)}) collective-permute-start(bf16[2,512,128]{2,1,0:T(8,128)(2,1)S(1)} %get-tuple-element.24), channel_id=1, source_target_pairs={{0,16},{16,0},{32,48},{48,32},{1,17},{17,1},{33,49},{49,33},{2,18}... | collective-permute-start | bytes 786440 | tf_op jit(solution)/shard_map/basis_yxc/ppermute | solution.py:26
  25.9 19.7 %collective-permute-start.2 = (bf16[2,512,128]{2,1,0:T(8,128)(2,1)S(1)}, bf16[2,512,128]{2,1,0:T(8,128)(2,1)}, u32[]{:S(2)}, u32[]{:S(2)}) collective-permute-start(bf16[2,512,128]{2,1,0:T(8,128)(2,1)S(1)} %get-tuple-element.24), channel_id=1, source_target_pairs={{0,32},{16,48},{32,0},{48,16},{1,33},{17,49},{33,1},{49,17},{2,34}... | collective-permute-start | bytes 786440 | tf_op jit(solution)/shard_map/basis_yxc/ppermute | solution.py:26
  30.4 17.8 %collective-permute-start.3 = (bf16[2,512,128]{2,1,0:T(8,128)(2,1)S(1)}, bf16[2,512,128]{2,1,0:T(8,128)(2,1)}, u32[]{:S(2)}, u32[]{:S(2)}) collective-permute-start(bf16[2,512,128]{2,1,0:T(8,128)(2,1)S(1)} %get-tuple-element.24), channel_id=1, source_target_pairs={{0,48},{16,32},{32,16},{48,0},{1,49},{17,33},{33,17},{49,1},{2,50}... | collective-permute-start | bytes 786440 | tf_op jit(solution)/shard_map/basis_yxc/ppermute | solution.py:26
  50.5 8.5 %copy-start.2 = (bf16[4,2,512,128]{3,2,1,0:T(8,128)(2,1)S(1)}, bf16[4,2,512,128]{3,2,1,0:T(8,128)(2,1)}, u32[]{:S(2)}) copy-start(bf16[4,2,512,128]{3,2,1,0:T(8,128)(2,1)} %pad_maximum_fusion.1) | copy-start | bytes 3145732
  50.5 8.5 %collective-permute-start.5 = (bf16[4,2,512,128]{3,2,1,0:T(8,128)(2,1)}, bf16[4,2,512,128]{3,2,1,0:T(8,128)(2,1)S(1)}, u32[]{:S(2)}, u32[]{:S(2)}) collective-permute-start(bf16[4,2,512,128]{3,2,1,0:T(8,128)(2,1)} %pad_maximum_fusion.1), channel_id=1, source_target_pairs={{0,1},{1,0},{2,3},{3,2},{4,5},{5,4},{6,7},{7,6},{8,9},{9,8},{10,11... | collective-permute-start | bytes 3145736 | tf_op jit(solution)/shard_map/basis_yxc/ppermute | solution.py:26
  54.8 4.4 %collective-permute-start.4 = (bf16[512,896]{1,0:T(8,128)(2,1)S(1)}, bf16[512,896]{1,0:T(8,128)(2,1)S(1)}, u32[]{:S(2)}, u32[]{:S(2)}) collective-permute-start(bf16[512,896]{1,0:T(8,128)(2,1)S(1)} %bitcast.28), channel_id=1, source_target_pairs={{0,1},{1,0},{2,3},{3,2},{4,5},{5,4},{6,7},{7,6},{8,9},{9,8},{10,11... | collective-permute-start | bytes 2752520 | tf_op jit(solution)/shard_map/rows_c/ppermute | solution.py:26
  59.0 1.4 copy-start.1
  62.7 35.8 %all-to-all-start.1 = ((bf16[4,224,1024]{2,1,0:T(8,128)(2,1)}), bf16[4,224,1024]{2,1,0:T(8,128)(2,1)}, u32[]{:S(2)}, u32[]{:S(2)}) async-start(bf16[4,224,1024]{2,1,0:T(8,128)(2,1)} %shard_map.57), calls=%async_computation.1 | async-start | bytes 3670016 | tf_op jit(solution)/shard_map/sum_x/all_to_all | solution.py:21
  67.2 9.0 %collective-permute-start.6 = (bf16[4,1,16,512]{3,2,1,0:T(8,128)(2,1)S(1)}, bf16[4,1,16,512]{3,2,1,0:T(8,128)(2,1)S(1)}, u32[]{:S(2)}, u32[]{:S(2)}) collective-permute-start(bf16[4,1,16,512]{3,2,1,0:T(8,128)(2,1)S(1)} %maximum_bitcast_fusion), channel_id=1, source_target_pairs={{0,256},{64,320},{128,384},{192,448},{256,0},{320,64},{384,128},{4... | collective-permute-start | bytes 196616 | tf_op jit(solution)/shard_map/slab_z/ppermute | solution.py:26
  76.2 11.8 %collective-permute-start.7 = (bf16[4,2,16,512]{3,2,1,0:T(8,128)(2,1)S(1)}, bf16[4,2,16,512]{3,2,1,0:T(8,128)(2,1)S(1)}, u32[]{:S(2)}, u32[]{:S(2)}) collective-permute-start(bf16[4,2,16,512]{3,2,1,0:T(8,128)(2,1)S(1)} %pad_maximum_fusion.6), channel_id=1, source_target_pairs={{0,128},{64,192},{128,0},{192,64},{256,384},{320,448},{384,256},{4... | collective-permute-start | bytes 393224 | tf_op jit(solution)/shard_map/slab_z/ppermute | solution.py:26
  88.0 9.2 %collective-permute-start.8 = (bf16[4,4,16,512]{3,2,1,0:T(8,128)(2,1)S(1)}, bf16[4,4,16,512]{3,2,1,0:T(8,128)(2,1)S(1)}, u32[]{:S(2)}, u32[]{:S(2)}) collective-permute-start(bf16[4,4,16,512]{3,2,1,0:T(8,128)(2,1)S(1)} %pad_maximum_fusion.5), channel_id=1, source_target_pairs={{0,64},{64,0},{128,192},{192,128},{256,320},{320,256},{384,448},{4... | collective-permute-start | bytes 786440 | tf_op jit(solution)/shard_map/slab_z/ppermute | solution.py:26
  100.8 21.5 %all-to-all-start.2 = ((bf16[8,224,128]{2,1,0:T(8,128)(2,1)}), bf16[8,224,128]{2,1,0:T(8,128)(2,1)S(1)}, u32[]{:S(2)}, u32[]{:S(2)}) async-start(bf16[8,224,128]{2,1,0:T(8,128)(2,1)} %shard_map.59), calls=%async_computation.2 | async-start | bytes 917504 | tf_op jit(solution)/shard_map/sum_z/all_to_all | solution.py:21
  104.3 10.0 %collective-permute-start.9 = (bf16[8,16,512]{2,1,0:T(8,128)(2,1)S(1)}, bf16[8,16,512]{2,1,0:T(8,128)(2,1)S(1)}, u32[]{:S(2)}, u32[]{:S(2)}) collective-permute-start(bf16[8,16,512]{2,1,0:T(8,128)(2,1)S(1)} %convert_element_type.15), channel_id=1, source_target_pairs={{0,4},{2,6},{4,0},{6,2},{8,12},{10,14},{12,8},{14,10},{1,5},{3,7},... | collective-permute-start | bytes 393224 | tf_op jit(solution)/shard_map/panel_sum/ppermute | solution.py:26
  114.3 15.1 %collective-permute-start.10 = (bf16[8,16,512]{2,1,0:T(8,128)(2,1)S(1)}, bf16[8,16,512]{2,1,0:T(8,128)(2,1)S(1)}, u32[]{:S(2)}, u32[]{:S(2)}) collective-permute-start(bf16[8,16,512]{2,1,0:T(8,128)(2,1)S(1)} %fusion), channel_id=1, source_target_pairs={{0,8},{2,10},{4,12},{6,14},{8,0},{10,2},{12,4},{14,6},{1,9},{3,11}... | collective-permute-start | bytes 393224 | tf_op jit(solution)/shard_map/panel_sum/ppermute | solution.py:26
  123.1 28.0 %all-to-all-start.3 = ((bf16[8,224,128]{2,1,0:T(8,128)(2,1)}), bf16[8,224,128]{2,1,0:T(8,128)(2,1)S(1)}, u32[]{:S(2)}, u32[]{:S(2)}) async-start(bf16[8,224,128]{2,1,0:T(8,128)(2,1)} %shard_map.60), calls=%async_computation.3 | async-start | bytes 917504 | tf_op jit(solution)/shard_map/rotated_z/all_to_all | solution.py:21
  129.4 9.6 %collective-permute-start.11 = (bf16[8,16,512]{2,1,0:T(8,128)(2,1)S(1)}, bf16[8,16,512]{2,1,0:T(8,128)(2,1)S(1)}, u32[]{:S(2)}, u32[]{:S(2)}) collective-permute-start(bf16[8,16,512]{2,1,0:T(8,128)(2,1)S(1)} %add_convert_fusion), channel_id=1, source_target_pairs={{0,16},{16,0},{32,48},{48,32},{1,17},{17,1},{33,49},{49,33},{2,18}... | collective-permute-start | bytes 393224 | tf_op jit(solution)/shard_map/panel_x/ppermute | solution.py:26
  131.3 7.7 %collective-permute-start.12 = (bf16[8,16,512]{2,1,0:T(8,128)(2,1)S(1)}, bf16[8,16,512]{2,1,0:T(8,128)(2,1)S(1)}, u32[]{:S(2)}, u32[]{:S(2)}) collective-permute-start(bf16[8,16,512]{2,1,0:T(8,128)(2,1)S(1)} %add_convert_fusion), channel_id=1, source_target_pairs={{0,32},{16,48},{32,0},{48,16},{1,33},{17,49},{33,1},{49,17},{2,34}... | collective-permute-start | bytes 393224 | tf_op jit(solution)/shard_map/panel_x/ppermute | solution.py:26
  135.1 8.3 %collective-permute-start.13 = (bf16[8,16,512]{2,1,0:T(8,128)(2,1)S(1)}, bf16[8,16,512]{2,1,0:T(8,128)(2,1)S(1)}, u32[]{:S(2)}, u32[]{:S(2)}) collective-permute-start(bf16[8,16,512]{2,1,0:T(8,128)(2,1)S(1)} %add_convert_fusion), channel_id=1, source_target_pairs={{0,48},{16,32},{32,16},{48,0},{1,49},{17,33},{33,17},{49,1},{2,50}... | collective-permute-start | bytes 393224 | tf_op jit(solution)/shard_map/panel_x/ppermute | solution.py:26
  143.5 7.6 %collective-permute-start.14 = (bf16[4,8,16,512]{3,2,1,0:T(8,128)(2,1)S(1)}, bf16[4,8,16,512]{3,2,1,0:T(8,128)(2,1)S(1)}, u32[]{:S(2)}, u32[]{:S(2)}) collective-permute-start(bf16[4,8,16,512]{3,2,1,0:T(8,128)(2,1)S(1)} %pad_maximum_fusion.3.own_ref), channel_id=1, source_target_pairs={{0,1},{1,0},{2,3},{3,2},{4,5},{5,4},{6,7},{7,6},{8,9},{9,8},{10,11... | collective-permute-start | bytes 1572872 | tf_op jit(solution)/shard_map/panel_c/ppermute | solution.py:26

commit v6 on v4

--- a/solution.py
+++ b/solution.py
@@ -26,22 +26,11 @@
     return lax.ppermute(block, axis, [(i, i ^ bit) for i in range(count)])
 
 
-def bits(axis):
-    count = lax.axis_size(axis)
-    return [1 << k for k in reversed(range(count.bit_length() - 1))]
-
-
 def reverse(index, width):
     result = 0
     for k in range(width):
         result = result | (((index >> k) & 1) << (width - 1 - k))
     return result
-
-
-def double(block, axis):
-    for bit in bits(axis):
-        block = jnp.concatenate([block, swap(block, axis, bit)], axis=0)
-    return block
 
 
 def add_from(block, axis, bit):
@@ -171,29 +160,31 @@
     )(parts)
 
 
-def panel_kernel(at_ref, slab_ref, basis_ref, out_ref):
-    cores, count, slots, deep = slab_ref.shape
-    for q in range(basis_ref.shape[1]):
-        total = jnp.zeros((count * slots, basis_ref.shape[3]), F32)
-        for r in range(cores):
-            left = slab_ref[r].reshape(count * slots, deep)
-            right = basis_ref[r, reverse(q ^ at_ref[0], 2)]
+def panel_kernel(slab_ref, basis_ref, out_ref):
+    count, slots, columns = out_ref.shape
+    deep, lanes = basis_ref.shape[1:]
+    pieces = columns // lanes
+    cores = basis_ref.shape[0] // pieces
+    for q in range(pieces):
+        total = jnp.zeros((count * slots, lanes), F32)
+        for c in range(cores):
+            left = slab_ref[:, c * deep : (c + 1) * deep]
+            right = basis_ref[q * cores + c]
             total = total + jnp.dot(left, right, preferred_element_type=F32)
-        lanes = total.shape[1]
         out_ref[:, :, q * lanes : (q + 1) * lanes] = total.reshape(count, slots, lanes)
 
 
-def panel_part(at, slab, basis):
-    cores, count, slots, deep = slab.shape
-    columns = basis.shape[1] * basis.shape[3]
+def panel_part(slab, basis, cores):
+    count, slots, deep = slab.shape
+    columns = basis.shape[0] // cores * basis.shape[2]
     return pl.pallas_call(
         panel_kernel,
         out_shape=jax.ShapeDtypeStruct((count, slots, columns), F32),
-        in_specs=[pl.BlockSpec(memory_space=SMEM)] + [pl.BlockSpec(memory_space=VMEM)] * 2,
+        in_specs=[pl.BlockSpec(memory_space=VMEM)] * 2,
         out_specs=pl.BlockSpec(memory_space=VMEM),
         compiler_params=PARAMS,
-        cost_estimate=cost(2 * count * slots * columns * deep * cores, 2 * basis.size),
-    )(at, slab, basis)
+        cost_estimate=cost(2 * count * slots * columns * deep, 2 * basis.size),
+    )(slab.reshape(count * slots, deep), basis)
 
 
 def example_kernel(nx, scale, at_ref, left_ref, own_ref, other_ref, out_ref):
@@ -248,16 +239,13 @@
     with jax.named_scope("rows_dp"):
         own = exchange(blocks, DP).reshape(nz * nx * half, wide)
 
-    mine = lax.dynamic_slice(inputs, (ic * half, (iy * nc + ic) * deep), (half, deep))
-    theirs = lax.dynamic_slice(inputs, (ic * half, (iy * nc + 1 - ic) * deep), (half, deep))
-    slab = jnp.stack([mine, theirs])[:, None]
-    basis_x = basis_in[None]
-    with jax.named_scope("panel_gather"):
+    with jax.named_scope("basis_xc"):
+        basis_x = lax.all_gather(basis_in, ("x", "c"), axis=0)
+    slab = lax.dynamic_slice(inputs, (ic * half, iy * nc * deep), (half, nc * deep))[None]
+    with jax.named_scope("slab_z"):
         more_slab = swap(slab, "z", 4)
-        basis_x = double(basis_x, "x")
-        basis_x = jnp.stack([basis_x, swap(basis_x, "c", 1)])
-        own, more_slab, basis_x = tie((own, more_slab, basis_x))
-        slab = jnp.concatenate([slab, more_slab], axis=1)
+        own, more_slab = tie((own, more_slab))
+        slab = jnp.concatenate([slab, more_slab], axis=0)
         more_slab = swap(slab, "z", 2)
 
     with jax.named_scope("rows_c"):
@@ -268,10 +256,10 @@
     with jax.named_scope("sum_x"):
         parts = exchange(parts, "x")
 
-    with jax.named_scope("panel_gather"):
-        slab = jnp.concatenate([slab, more_slab], axis=1)
-        slab = jnp.concatenate([slab, swap(slab, "z", 1)], axis=1)
-    piece = panel_part(at, slab, basis_x)
+    with jax.named_scope("slab_z"):
+        slab = jnp.concatenate([slab, more_slab], axis=0)
+        slab = jnp.concatenate([slab, swap(slab, "z", 1)], axis=0)
+    piece = panel_part(slab, basis_x, nc)
     with jax.named_scope("panel_sum"):
         piece = add_from(piece, "y", 1)
         piece = add_from(piece, "y", 2)

time: 155 us -> 157 us (1.013)
  between operations: 0.95 us -> 14.4 us
  starting transfers between devices: 77.3 us -> 64.8 us
  waiting for transfers between devices: 44.9 us -> 49.2 us
  Pallas kernels: 13.9 us -> 12.1 us
    ppermute x14 -> x11, starting transfers between devices: 49.8 us -> 39.8 us  [swap(): return lax.ppermute(block, axis, [(i, i ^ bit) for i in range(count)])]
    ppermute x14 -> x11, waiting for transfers between devices: 34.9 us -> 38.8 us  [swap(): return lax.ppermute(block, axis, [(i, i ^ bit) for i in range(count)])]
    all_to_all x4, starting transfers between devices: 27.5 us -> 24.9 us  [exchange(): return lax.all_to_all(blocks, axis, split_axis=0, concat_axis=0, tiled=True)]
  transfers between devices with their start and end apart: 18 -> 16, of which waited for: 11 -> 9; matrix products, arithmetic and copies ran while one was open for 2% -> 0% of each run, Pallas kernels for 3% -> 4%
where the time goes in v6:
time: 157 us; the launch traced here: 156 us
  starting transfers between devices  64.8 us (41%)
  waiting for transfers between devices  49.2 us (31%)
  between operations  14.4 us (9%)
  blocking collectives  13 us (8%)
  Pallas kernels  12.1 us (8%)
  local copies, waits for them, and re-layouts  2 us (1%)
    ppermute x11, starting transfers between devices, swap(): return lax.ppermute(block, axis, [(i, i ^ bit) for i in range(count)])  39.8 us
    ppermute x11, waiting for transfers between devices, swap(): return lax.ppermute(block, axis, [(i, i ^ bit) for i in range(count)])  38.8 us
    all_to_all x4, starting transfers between devices, exchange(): return lax.all_to_all(blocks, axis, split_axis=0, concat_axis=0, tiled=True)  24.9 us
    all_to_all x1, blocking collectives, exchange(): return lax.all_to_all(blocks, axis, split_axis=0, concat_axis=0, tiled=True)  13 us
    all_to_all x4, waiting for transfers between devices, exchange(): return lax.all_to_all(blocks, axis, split_axis=0, concat_axis=0, tiled=True)  9.61 us
    pallas_call x2, Pallas kernels, rotate(): pl.pallas_call(rotate_kernel, out_shape=jax.ShapeDtypeStruct((pieces, row...  4.71 us
  transfers between devices with their start and end apart: 16, of which 9 were waited for; matrix products, arithmetic and copies ran while one was open for 0% of the time, Pallas kernels for 4%

profile of v6, /device:TPU:56, one launch (start us, length us, event | category | flops | bytes accessed | tf_op | source)
XLA Modules:
  0.0 155.8 jit_solution(2389805232691207147)
XLA Ops:
  7.3 2.4 %shard_map.55 = bf16[32,16,896]{2,1,0:T(8,128)(2,1)} custom-call(s32[1]{0:T(128)S(6)} %copy.9.length_ref, bf16[32,28672]{1,0:T(8,128)(2,1)} %grads_ref.1), custom_call_target="tpu_custom_call" | custom-call | bytes 1835008 | tf_op jit(solution)/shard_map/pallas_call | solution.py:68
  9.7 13.2 %all-to-all-start = ((bf16[32,16,896]{2,1,0:T(8,128)(2,1)}), bf16[32,16,896]{2,1,0:T(8,128)(2,1)S(1)}, u32[]{:S(2)}, u32[]{:S(2)}) async-start(bf16[32,16,896]{2,1,0:T(8,128)(2,1)} %shard_map.55), calls=%async_computation | async-start | bytes 1835008 | tf_op jit(solution)/shard_map/rows_dp/all_to_all | solution.py:21
  23.6 7.6 %collective-permute-start = (bf16[1,16,1024]{2,1,0:T(8,128)(2,1)S(1)}, bf16[1,16,1024]{2,1,0:T(8,128)(2,1)S(1)}, u32[]{:S(2)}, u32[]{:S(2)}) collective-permute-start(bf16[1,16,1024]{2,1,0:T(8,128)(2,1)S(1)} %dynamic-slice_bitcast_fusion), channel_id=1, source_target_pairs={{0,256},{64,320},{128,384},{192,448},{256,0},{320,64},{384,128},{4... | collective-permute-start | bytes 98312 | tf_op jit(solution)/shard_map/slab_z/ppermute | solution.py:26
  31.2 17.8 %collective-permute-done = bf16[1,16,1024]{2,1,0:T(8,128)(2,1)S(1)} collective-permute-done((bf16[1,16,1024]{2,1,0:T(8,128)(2,1)S(1)}, bf16[1,16,1024]{2,1,0:T(8,128)(2,1)S(1)}, u32[]{:S(2)}, u32[]{:S(2)}) %collective-permute-start) | collective-permute-done | bytes 32800 | tf_op jit(solution)/shard_map/slab_z/ppermute | solution.py:26
  51.0 4.7 %collective-permute-start.2 = (bf16[2,16,1024]{2,1,0:T(8,128)(2,1)S(1)}, bf16[2,16,1024]{2,1,0:T(8,128)(2,1)S(1)}, u32[]{:S(2)}, u32[]{:S(2)}) collective-permute-start(bf16[2,16,1024]{2,1,0:T(8,128)(2,1)S(1)} %pad_maximum_fusion.3), channel_id=1, source_target_pairs={{0,128},{64,192},{128,0},{192,64},{256,384},{320,448},{384,256},{4... | collective-permute-start | bytes 196616 | tf_op jit(solution)/shard_map/slab_z/ppermute | solution.py:26
  55.7 2.4 %shard_map.56.rest_0_ = bf16[4,224,1024]{2,1,0:T(8,128)(2,1)} custom-call(bf16[512,896]{1,0:T(8,128)(2,1)S(1)} %bitcast.13, bf16[896,896]{1,0:T(8,128)(2,1)S(1)} %copy-done.1), custom_call_target="tpu_custom_call" | custom-call | flops 822083584 | bytes 1835008 | tf_op jit(solution)/shard_map/pallas_call | solution.py:106
  59.9 2.3 %shard_map.57 = bf16[4,224,1024]{2,1,0:T(8,128)(2,1)} custom-call(bf16[512,896]{1,0:T(8,128)(2,1)S(1)} %collective-permute-done.1.tokens_ref, bf16[896,896]{1,0:T(8,128)(2,1)S(1)} %copy-done.1, bf16[4,224,1024]{2,1,0:T(8,128)(2,1)} %shard_map.56.rest_0_), custom_call_target="tpu_custom_call", output_to_operand_aliasing={{}: (2, {})} | custom-call | flops 822083584 | bytes 1835008 | tf_op jit(solution)/shard_map/pallas_call | solution.py:106
  62.2 4.8 %all-to-all-start.1 = ((bf16[4,224,1024]{2,1,0:T(8,128)(2,1)}), bf16[4,224,1024]{2,1,0:T(8,128)(2,1)S(1)}, u32[]{:S(2)}, u32[]{:S(2)}) async-start(bf16[4,224,1024]{2,1,0:T(8,128)(2,1)} %shard_map.57), calls=%async_computation.1 | async-start | bytes 3670016 | tf_op jit(solution)/shard_map/sum_x/all_to_all | solution.py:21
  67.1 1.9 %collective-permute-start.3 = (bf16[4,16,1024]{2,1,0:T(8,128)(2,1)S(1)}, bf16[4,16,1024]{2,1,0:T(8,128)(2,1)S(1)}, u32[]{:S(2)}, u32[]{:S(2)}) collective-permute-start(bf16[4,16,1024]{2,1,0:T(8,128)(2,1)S(1)} %pad_maximum_fusion.2), channel_id=1, source_target_pairs={{0,64},{64,0},{128,192},{192,128},{256,320},{320,256},{384,448},{4... | collective-permute-start | bytes 393224 | tf_op jit(solution)/shard_map/slab_z/ppermute | solution.py:26
  69.0 5.1 %collective-permute-done.3 = bf16[4,16,1024]{2,1,0:T(8,128)(2,1)S(1)} collective-permute-done((bf16[4,16,1024]{2,1,0:T(8,128)(2,1)S(1)}, bf16[4,16,1024]{2,1,0:T(8,128)(2,1)S(1)}, u32[]{:S(2)}, u32[]{:S(2)}) %collective-permute-start.3) | collective-permute-done | bytes 131104 | tf_op jit(solution)/shard_map/slab_z/ppermute | solution.py:26
  75.8 3.3 %collective-permute-start.4 = (bf16[8,16,512]{2,1,0:T(8,128)(2,1)S(1)}, bf16[8,16,512]{2,1,0:T(8,128)(2,1)S(1)}, u32[]{:S(2)}, u32[]{:S(2)}) collective-permute-start(bf16[8,16,512]{2,1,0:T(8,128)(2,1)S(1)} %convert_element_type.21), channel_id=1, source_target_pairs={{0,2},{2,0},{4,6},{6,4},{8,10},{10,8},{12,14},{14,12},{1,3},{3,1},... | collective-permute-start | bytes 393224 | tf_op jit(solution)/shard_map/panel_sum/ppermute | solution.py:26
  79.1 3.6 %collective-permute-done.4 = bf16[8,16,512]{2,1,0:T(8,128)(2,1)S(1)} collective-permute-done((bf16[8,16,512]{2,1,0:T(8,128)(2,1)S(1)}, bf16[8,16,512]{2,1,0:T(8,128)(2,1)S(1)}, u32[]{:S(2)}, u32[]{:S(2)}) %collective-permute-start.4) | collective-permute-done | bytes 131104 | tf_op jit(solution)/shard_map/panel_sum/ppermute | solution.py:26
  82.7 4.0 %collective-permute-start.5 = (bf16[8,16,512]{2,1,0:T(8,128)(2,1)S(1)}, bf16[8,16,512]{2,1,0:T(8,128)(2,1)S(1)}, u32[]{:S(2)}, u32[]{:S(2)}) collective-permute-start(bf16[8,16,512]{2,1,0:T(8,128)(2,1)S(1)} %fusion), channel_id=1, source_target_pairs={{0,4},{2,6},{4,0},{6,2},{8,12},{10,14},{12,8},{14,10},{1,5},{3,7},... | collective-permute-start | bytes 393224 | tf_op jit(solution)/shard_map/panel_sum/ppermute | solution.py:26
  86.7 5.1 %collective-permute-done.5 = bf16[8,16,512]{2,1,0:T(8,128)(2,1)S(1)} collective-permute-done((bf16[8,16,512]{2,1,0:T(8,128)(2,1)S(1)}, bf16[8,16,512]{2,1,0:T(8,128)(2,1)S(1)}, u32[]{:S(2)}, u32[]{:S(2)}) %collective-permute-start.5) | collective-permute-done | bytes 131104 | tf_op jit(solution)/shard_map/panel_sum/ppermute | solution.py:26
  93.0 3.5 %all-to-all-start.2 = ((bf16[8,224,128]{2,1,0:T(8,128)(2,1)}), bf16[8,224,128]{2,1,0:T(8,128)(2,1)S(1)}, u32[]{:S(2)}, u32[]{:S(2)}) async-start(bf16[8,224,128]{2,1,0:T(8,128)(2,1)} %shard_map.59), calls=%async_computation.2 | async-start | bytes 917504 | tf_op jit(solution)/shard_map/sum_z/all_to_all | solution.py:21
  96.5 4.6 %collective-permute-start.6 = (bf16[8,16,512]{2,1,0:T(8,128)(2,1)S(1)}, bf16[8,16,512]{2,1,0:T(8,128)(2,1)S(1)}, u32[]{:S(2)}, u32[]{:S(2)}) collective-permute-start(bf16[8,16,512]{2,1,0:T(8,128)(2,1)S(1)} %convert_element_type.25), channel_id=1, source_target_pairs={{0,8},{2,10},{4,12},{6,14},{8,0},{10,2},{12,4},{14,6},{1,9},{3,11}... | collective-permute-start | bytes 393224 | tf_op jit(solution)/shard_map/panel_sum/ppermute | solution.py:26
  101.1 9.6 %all-to-all-done.2.parts_ref = bf16[8,224,128]{2,1,0:T(8,128)(2,1)S(1)} async-done(((bf16[8,224,128]{2,1,0:T(8,128)(2,1)}), bf16[8,224,128]{2,1,0:T(8,128)(2,1)S(1)}, u32[]{:S(2)}, u32[]{:S(2)}) %all-to-all-start.2) | async-done | bytes 458784 | tf_op jit(solution)/shard_map/sum_z/all_to_all | solution.py:21
  111.6 3.5 %all-to-all-start.3 = ((bf16[8,224,128]{2,1,0:T(8,128)(2,1)}), bf16[8,224,128]{2,1,0:T(8,128)(2,1)S(1)}, u32[]{:S(2)}, u32[]{:S(2)}) async-start(bf16[8,224,128]{2,1,0:T(8,128)(2,1)} %shard_map.60), calls=%async_computation.3 | async-start | bytes 917504 | tf_op jit(solution)/shard_map/rotated_z/all_to_all | solution.py:21
  115.1 4.1 %collective-permute-start.9 = (bf16[8,16,512]{2,1,0:T(8,128)(2,1)S(1)}, bf16[8,16,512]{2,1,0:T(8,128)(2,1)S(1)}, u32[]{:S(2)}, u32[]{:S(2)}) collective-permute-start(bf16[8,16,512]{2,1,0:T(8,128)(2,1)S(1)} %add_convert_fusion), channel_id=1, source_target_pairs={{0,48},{16,32},{32,16},{48,0},{1,49},{17,33},{33,17},{49,1},{2,50}... | collective-permute-start | bytes 393224 | tf_op jit(solution)/shard_map/panel_x/ppermute | solution.py:26
  119.2 2.6 %collective-permute-start.8 = (bf16[8,16,512]{2,1,0:T(8,128)(2,1)S(1)}, bf16[8,16,512]{2,1,0:T(8,128)(2,1)S(1)}, u32[]{:S(2)}, u32[]{:S(2)}) collective-permute-start(bf16[8,16,512]{2,1,0:T(8,128)(2,1)S(1)} %add_convert_fusion), channel_id=1, source_target_pairs={{0,32},{16,48},{32,0},{48,16},{1,33},{17,49},{33,1},{49,17},{2,34}... | collective-permute-start | bytes 393224 | tf_op jit(solution)/shard_map/panel_x/ppermute | solution.py:26
  121.8 3.2 %collective-permute-start.7 = (bf16[8,16,512]{2,1,0:T(8,128)(2,1)S(1)}, bf16[8,16,512]{2,1,0:T(8,128)(2,1)S(1)}, u32[]{:S(2)}, u32[]{:S(2)}) collective-permute-start(bf16[8,16,512]{2,1,0:T(8,128)(2,1)S(1)} %add_convert_fusion), channel_id=1, source_target_pairs={{0,16},{16,0},{32,48},{48,32},{1,17},{17,1},{33,49},{49,33},{2,18}... | collective-permute-start | bytes 393224 | tf_op jit(solution)/shard_map/panel_x/ppermute | solution.py:26
  125.0 2.6 %collective-permute-done.8 = bf16[8,16,512]{2,1,0:T(8,128)(2,1)S(1)} collective-permute-done((bf16[8,16,512]{2,1,0:T(8,128)(2,1)S(1)}, bf16[8,16,512]{2,1,0:T(8,128)(2,1)S(1)}, u32[]{:S(2)}, u32[]{:S(2)}) %collective-permute-start.8) | collective-permute-done | bytes 131104 | tf_op jit(solution)/shard_map/panel_x/ppermute | solution.py:26
  132.5 2.6 %shard_map.61 = f32[4,224,128]{2,1,0:T(8,128)S(1)} custom-call(s32[2]{0:T(128)S(1)} %pad_add_fusion.at_ref, bf16[8,224,128]{2,1,0:T(8,128)(2,1)S(1)} %all-to-all-done.3.left_ref, bf16[4,8,16,512]{3,2,1,0:T(8,128)(2,1)S(1)} %pad_maximum_fusion.own_ref, bf16[4,8,16,512]{3,2,1,0:T(8,128)(2,1)S(1)} %collective-permute-done.10.other_ref), custom_call_target="tpu_custom_call" | custom-call | flops 234881024 | bytes 1048576 | tf_op jit(solution)/shard_map/pallas_call | solution.py:218
  135.2 13.0 %all_to_all.25 = f32[4,224,128]{2,1,0:T(8,128)S(1)} all-to-all(f32[4,224,128]{2,1,0:T(8,128)S(1)} %shard_map.61), channel_id=1, replica_groups=mesh['z'=8,'x'=4,'y'=8,'c'=2] {'x'}, dimensions={0} | all-to-all | bytes 917504 | tf_op jit(solution)/shard_map/out_x/all_to_all | solution.py:21
  (35 shorter events, 13.9 us)
Async XLA Ops:
  6.5 17.0 %copy-start = (bf16[32,8192]{1,0:T(8,128)(2,1)S(1)}, bf16[32,8192]{1,0:T(8,128)(2,1)}, u32[]{:S(2)}) copy-start(bf16[32,8192]{1,0:T(8,128)(2,1)} %param.6) | copy-start | bytes 1572868
  7.2 48.5 %copy-start.1 = (bf16[896,896]{1,0:T(8,128)(2,1)S(1)}, bf16[896,896]{1,0:T(8,128)(2,1)}, u32[]{:S(2)}) copy-start(bf16[896,896]{1,0:T(8,128)(2,1)} %basis_ref.3) | copy-start | bytes 4816900
  9.7 39.4 %all-to-all-start = ((bf16[32,16,896]{2,1,0:T(8,128)(2,1)}), bf16[32,16,896]{2,1,0:T(8,128)(2,1)S(1)}, u32[]{:S(2)}, u32[]{:S(2)}) async-start(bf16[32,16,896]{2,1,0:T(8,128)(2,1)} %shard_map.55), calls=%async_computation | async-start | bytes 1835008 | tf_op jit(solution)/shard_map/rows_dp/all_to_all | solution.py:21
  22.8 51.3 %all-gather.3.cloned.1.call-start = ((), (), s32[]{:S(2)}) async-start(), calls=%async_computation.5 | async-start | bytes 1179648 | tf_op jit(solution)/shard_map/basis_xc/all_gather | solution.py:243
  23.6 25.4 %collective-permute-start = (bf16[1,16,1024]{2,1,0:T(8,128)(2,1)S(1)}, bf16[1,16,1024]{2,1,0:T(8,128)(2,1)S(1)}, u32[]{:S(2)}, u32[]{:S(2)}) collective-permute-start(bf16[1,16,1024]{2,1,0:T(8,128)(2,1)S(1)} %dynamic-slice_bitcast_fusion), channel_id=1, source_target_pairs={{0,256},{64,320},{128,384},{192,448},{256,0},{320,64},{384,128},{4... | collective-permute-start | bytes 98312 | tf_op jit(solution)/shard_map/slab_z/ppermute | solution.py:26
  49.1 10.8 %collective-permute-start.1 = (bf16[512,896]{1,0:T(8,128)(2,1)S(1)}, bf16[512,896]{1,0:T(8,128)(2,1)S(1)}, u32[]{:S(2)}, u32[]{:S(2)}) collective-permute-start(bf16[512,896]{1,0:T(8,128)(2,1)S(1)} %bitcast.12), channel_id=1, source_target_pairs={{0,1},{1,0},{2,3},{3,2},{4,5},{5,4},{6,7},{7,6},{8,9},{9,8},{10,11... | collective-permute-start | bytes 2752520 | tf_op jit(solution)/shard_map/rows_c/ppermute | solution.py:26
  51.0 8.9 %collective-permute-start.2 = (bf16[2,16,1024]{2,1,0:T(8,128)(2,1)S(1)}, bf16[2,16,1024]{2,1,0:T(8,128)(2,1)S(1)}, u32[]{:S(2)}, u32[]{:S(2)}) collective-permute-start(bf16[2,16,1024]{2,1,0:T(8,128)(2,1)S(1)} %pad_maximum_fusion.3), channel_id=1, source_target_pairs={{0,128},{64,192},{128,0},{192,64},{256,384},{320,448},{384,256},{4... | collective-permute-start | bytes 196616 | tf_op jit(solution)/shard_map/slab_z/ppermute | solution.py:26
  62.2 29.7 %all-to-all-start.1 = ((bf16[4,224,1024]{2,1,0:T(8,128)(2,1)}), bf16[4,224,1024]{2,1,0:T(8,128)(2,1)S(1)}, u32[]{:S(2)}, u32[]{:S(2)}) async-start(bf16[4,224,1024]{2,1,0:T(8,128)(2,1)} %shard_map.57), calls=%async_computation.1 | async-start | bytes 3670016 | tf_op jit(solution)/shard_map/sum_x/all_to_all | solution.py:21
  67.1 7.0 %collective-permute-start.3 = (bf16[4,16,1024]{2,1,0:T(8,128)(2,1)S(1)}, bf16[4,16,1024]{2,1,0:T(8,128)(2,1)S(1)}, u32[]{:S(2)}, u32[]{:S(2)}) collective-permute-start(bf16[4,16,1024]{2,1,0:T(8,128)(2,1)S(1)} %pad_maximum_fusion.2), channel_id=1, source_target_pairs={{0,64},{64,0},{128,192},{192,128},{256,320},{320,256},{384,448},{4... | collective-permute-start | bytes 393224 | tf_op jit(solution)/shard_map/slab_z/ppermute | solution.py:26
  74.1 1.2 copy-start.2
  75.8 6.9 %collective-permute-start.4 = (bf16[8,16,512]{2,1,0:T(8,128)(2,1)S(1)}, bf16[8,16,512]{2,1,0:T(8,128)(2,1)S(1)}, u32[]{:S(2)}, u32[]{:S(2)}) collective-permute-start(bf16[8,16,512]{2,1,0:T(8,128)(2,1)S(1)} %convert_element_type.21), channel_id=1, source_target_pairs={{0,2},{2,0},{4,6},{6,4},{8,10},{10,8},{12,14},{14,12},{1,3},{3,1},... | collective-permute-start | bytes 393224 | tf_op jit(solution)/shard_map/panel_sum/ppermute | solution.py:26
  82.7 9.2 %collective-permute-start.5 = (bf16[8,16,512]{2,1,0:T(8,128)(2,1)S(1)}, bf16[8,16,512]{2,1,0:T(8,128)(2,1)S(1)}, u32[]{:S(2)}, u32[]{:S(2)}) collective-permute-start(bf16[8,16,512]{2,1,0:T(8,128)(2,1)S(1)} %fusion), channel_id=1, source_target_pairs={{0,4},{2,6},{4,0},{6,2},{8,12},{10,14},{12,8},{14,10},{1,5},{3,7},... | collective-permute-start | bytes 393224 | tf_op jit(solution)/shard_map/panel_sum/ppermute | solution.py:26
  93.0 17.7 %all-to-all-start.2 = ((bf16[8,224,128]{2,1,0:T(8,128)(2,1)}), bf16[8,224,128]{2,1,0:T(8,128)(2,1)S(1)}, u32[]{:S(2)}, u32[]{:S(2)}) async-start(bf16[8,224,128]{2,1,0:T(8,128)(2,1)} %shard_map.59), calls=%async_computation.2 | async-start | bytes 917504 | tf_op jit(solution)/shard_map/sum_z/all_to_all | solution.py:21
  96.5 18.5 %collective-permute-start.6 = (bf16[8,16,512]{2,1,0:T(8,128)(2,1)S(1)}, bf16[8,16,512]{2,1,0:T(8,128)(2,1)S(1)}, u32[]{:S(2)}, u32[]{:S(2)}) collective-permute-start(bf16[8,16,512]{2,1,0:T(8,128)(2,1)S(1)} %convert_element_type.25), channel_id=1, source_target_pairs={{0,8},{2,10},{4,12},{6,14},{8,0},{10,2},{12,4},{14,6},{1,9},{3,11}... | collective-permute-start | bytes 393224 | tf_op jit(solution)/shard_map/panel_sum/ppermute | solution.py:26
  111.6 20.9 %all-to-all-start.3 = ((bf16[8,224,128]{2,1,0:T(8,128)(2,1)}), bf16[8,224,128]{2,1,0:T(8,128)(2,1)S(1)}, u32[]{:S(2)}, u32[]{:S(2)}) async-start(bf16[8,224,128]{2,1,0:T(8,128)(2,1)} %shard_map.60), calls=%async_computation.3 | async-start | bytes 917504 | tf_op jit(solution)/shard_map/rotated_z/all_to_all | solution.py:21
  115.1 9.8 %collective-permute-start.9 = (bf16[8,16,512]{2,1,0:T(8,128)(2,1)S(1)}, bf16[8,16,512]{2,1,0:T(8,128)(2,1)S(1)}, u32[]{:S(2)}, u32[]{:S(2)}) collective-permute-start(bf16[8,16,512]{2,1,0:T(8,128)(2,1)S(1)} %add_convert_fusion), channel_id=1, source_target_pairs={{0,48},{16,32},{32,16},{48,0},{1,49},{17,33},{33,17},{49,1},{2,50}... | collective-permute-start | bytes 393224 | tf_op jit(solution)/shard_map/panel_x/ppermute | solution.py:26
  119.2 8.4 %collective-permute-start.8 = (bf16[8,16,512]{2,1,0:T(8,128)(2,1)S(1)}, bf16[8,16,512]{2,1,0:T(8,128)(2,1)S(1)}, u32[]{:S(2)}, u32[]{:S(2)}) collective-permute-start(bf16[8,16,512]{2,1,0:T(8,128)(2,1)S(1)} %add_convert_fusion), channel_id=1, source_target_pairs={{0,32},{16,48},{32,0},{48,16},{1,33},{17,49},{33,1},{49,17},{2,34}... | collective-permute-start | bytes 393224 | tf_op jit(solution)/shard_map/panel_x/ppermute | solution.py:26
  121.8 6.9 %collective-permute-start.7 = (bf16[8,16,512]{2,1,0:T(8,128)(2,1)S(1)}, bf16[8,16,512]{2,1,0:T(8,128)(2,1)S(1)}, u32[]{:S(2)}, u32[]{:S(2)}) collective-permute-start(bf16[8,16,512]{2,1,0:T(8,128)(2,1)S(1)} %add_convert_fusion), channel_id=1, source_target_pairs={{0,16},{16,0},{32,48},{48,32},{1,17},{17,1},{33,49},{49,33},{2,18}... | collective-permute-start | bytes 393224 | tf_op jit(solution)/shard_map/panel_x/ppermute | solution.py:26
  128.7 3.8 %collective-permute-start.10 = (bf16[4,8,16,512]{3,2,1,0:T(8,128)(2,1)S(1)}, bf16[4,8,16,512]{3,2,1,0:T(8,128)(2,1)S(1)}, u32[]{:S(2)}, u32[]{:S(2)}) collective-permute-start(bf16[4,8,16,512]{3,2,1,0:T(8,128)(2,1)S(1)} %pad_maximum_fusion.own_ref), channel_id=1, source_target_pairs={{0,1},{1,0},{2,3},{3,2},{4,5},{5,4},{6,7},{7,6},{8,9},{9,8},{10,11... | collective-permute-start | bytes 1572872 | tf_op jit(solution)/shard_map/panel_c/ppermute | solution.py:26
Sparse Core Ops, SparseCore 0:
  25.8 30.4 all-gather.2

commit v7 on v6

--- a/solution.py
+++ b/solution.py
@@ -160,31 +160,27 @@
     )(parts)
 
 
-def panel_kernel(slab_ref, basis_ref, out_ref):
-    count, slots, columns = out_ref.shape
-    deep, lanes = basis_ref.shape[1:]
-    pieces = columns // lanes
-    cores = basis_ref.shape[0] // pieces
+def panel_kernel(at_ref, slab_ref, own_ref, other_ref, out_ref):
+    count, slots, _ = out_ref.shape
+    pieces, deep, lanes = own_ref.shape
     for q in range(pieces):
-        total = jnp.zeros((count * slots, lanes), F32)
-        for c in range(cores):
-            left = slab_ref[:, c * deep : (c + 1) * deep]
-            right = basis_ref[q * cores + c]
-            total = total + jnp.dot(left, right, preferred_element_type=F32)
+        place = q ^ at_ref[0]
+        total = jnp.dot(slab_ref[:, :deep], own_ref[place], preferred_element_type=F32)
+        total = total + jnp.dot(slab_ref[:, deep:], other_ref[place], preferred_element_type=F32)
         out_ref[:, :, q * lanes : (q + 1) * lanes] = total.reshape(count, slots, lanes)
 
 
-def panel_part(slab, basis, cores):
+def panel_part(at, slab, own, other):
     count, slots, deep = slab.shape
-    columns = basis.shape[0] // cores * basis.shape[2]
+    columns = own.shape[0] * own.shape[2]
     return pl.pallas_call(
         panel_kernel,
         out_shape=jax.ShapeDtypeStruct((count, slots, columns), F32),
-        in_specs=[pl.BlockSpec(memory_space=VMEM)] * 2,
+        in_specs=[pl.BlockSpec(memory_space=SMEM)] + [pl.BlockSpec(memory_space=VMEM)] * 3,
         out_specs=pl.BlockSpec(memory_space=VMEM),
         compiler_params=PARAMS,
-        cost_estimate=cost(2 * count * slots * columns * deep, 2 * basis.size),
-    )(slab.reshape(count * slots, deep), basis)
+        cost_estimate=cost(2 * count * slots * columns * deep, 4 * own.size),
+    )(at, slab.reshape(count * slots, deep), own, other)
 
 
 def example_kernel(nx, scale, at_ref, left_ref, own_ref, other_ref, out_ref):
@@ -198,7 +194,7 @@
     for k in range(groups):
         left = jnp.concatenate([left_ref[k], left_ref[groups + k]], axis=1)
         places = [divmod(k * per_group + j, nx) for j in range(per_group)]
-        places = [(xp ^ at_ref[0], reverse(zp ^ at_ref[1], 3)) for zp, xp in places]
+        places = [(xp, reverse(zp ^ at_ref[1], 3)) for zp, xp in places]
         right = jnp.concatenate(
             [own_ref[a, b] for a, b in places] + [other_ref[a, b] for a, b in places], axis=0
         )
@@ -239,27 +235,34 @@
     with jax.named_scope("rows_dp"):
         own = exchange(blocks, DP).reshape(nz * nx * half, wide)
 
-    with jax.named_scope("basis_xc"):
-        basis_x = lax.all_gather(basis_in, ("x", "c"), axis=0)
-    slab = lax.dynamic_slice(inputs, (ic * half, iy * nc * deep), (half, nc * deep))[None]
+    def features(cr):
+        start = (iy * nc + (ic ^ cr)) * deep
+        return lax.dynamic_slice(inputs, (ic * half, start), (half, deep))
+
+    slab = jnp.concatenate([features(0), features(1)], axis=1)[None]
     with jax.named_scope("slab_z"):
         more_slab = swap(slab, "z", 4)
-        own, more_slab = tie((own, more_slab))
-        slab = jnp.concatenate([slab, more_slab], axis=0)
-        more_slab = swap(slab, "z", 2)
-
+    with jax.named_scope("basis_x"):
+        basis_x = jnp.stack([basis_in] + [swap(basis_in, "x", k) for k in range(1, nx)])
+    own, more_slab, basis_x = tie((own, more_slab, basis_x))
     with jax.named_scope("rows_c"):
         other = swap(own, "c", 1)
     parts = rotate(own, basis_out, 0, nx)
-    other, more_slab = tie((other, more_slab))
+    slab = jnp.concatenate([slab, more_slab], axis=0)
+    parts, slab, basis_x = tie((parts, slab, basis_x))
+    with jax.named_scope("slab_z"):
+        more_slab = swap(slab, "z", 2)
+    with jax.named_scope("basis_c"):
+        more_basis = swap(basis_x, "c", 1)
     parts = rotate(other, basis_out, 1, nx, parts)
+    parts, more_slab, more_basis = tie((parts, more_slab, more_basis))
     with jax.named_scope("sum_x"):
         parts = exchange(parts, "x")
 
     with jax.named_scope("slab_z"):
         slab = jnp.concatenate([slab, more_slab], axis=0)
         slab = jnp.concatenate([slab, swap(slab, "z", 1)], axis=0)
-    piece = panel_part(slab, basis_x, nc)
+    piece = panel_part(at, slab, basis_x, more_basis)
     with jax.named_scope("panel_sum"):
         piece = add_from(piece, "y", 1)
         piece = add_from(piece, "y", 2)
@@ -273,7 +276,7 @@
     with jax.named_scope("rotated_z"):
         rotated = exchange(rotated, "z")
     with jax.named_scope("panel_x"):
-        piece = jnp.stack([piece] + [swap(piece, "x", k) for k in range(1, 4)])
+        piece = lax.all_gather(piece, "x", axis=0)
     with jax.named_scope("panel_c"):
         piece_other = swap(piece, "c", 1)
 

time: 157 us -> 145 us (0.924)
  waiting for transfers between devices: 49.2 us -> 32.1 us
  between operations: 14.4 us -> 0.95 us
  blocking collectives: 13 us -> 25.8 us
  starting transfers between devices: 64.8 us -> 67.2 us
  local copies, waits for them, and re-layouts: 2 us -> 4.02 us
    ppermute x11 -> x12, waiting for transfers between devices: 38.8 us -> 23.1 us  [swap(): return lax.ppermute(block, axis, [(i, i ^ bit) for i in range(count)])]
    all_gather x0 -> x1, blocking collectives: none -> 13.1 us  [per_device(): piece = lax.all_gather(piece, 'x', axis=0)]
    ppermute x11 -> x12, starting transfers between devices: 39.8 us -> 42.2 us  [swap(): return lax.ppermute(block, axis, [(i, i ^ bit) for i in range(count)])]
    unnamed x7 -> x11, local copies, waits for them, and re-layouts: 1.99 us -> 3.28 us
  transfers between devices with their start and end apart: 16 -> 16, of which waited for: 9 -> 8; matrix products, arithmetic and copies ran while one was open for 0% -> 1% of each run, Pallas kernels for 4% -> 5%
where the time goes in v7:
time: 145 us; the launch traced here: 144 us
  starting transfers between devices  67.2 us (46%)
  waiting for transfers between devices  32.1 us (22%)
  blocking collectives  25.8 us (18%)
  Pallas kernels  12.8 us (9%)
  local copies, waits for them, and re-layouts  4.02 us (3%)
    ppermute x12, starting transfers between devices, swap(): return lax.ppermute(block, axis, [(i, i ^ bit) for i in range(count)])  42.2 us
    all_to_all x4, starting transfers between devices, exchange(): return lax.all_to_all(blocks, axis, split_axis=0, concat_axis=0, tiled=True)  25.1 us
    ppermute x12, waiting for transfers between devices, swap(): return lax.ppermute(block, axis, [(i, i ^ bit) for i in range(count)])  23.1 us
    all_gather x1, blocking collectives, per_device(): piece = lax.all_gather(piece, 'x', axis=0)  13.1 us
    all_to_all x1, blocking collectives, exchange(): return lax.all_to_all(blocks, axis, split_axis=0, concat_axis=0, tiled=True)  12.6 us
    all_to_all x4, waiting for transfers between devices, exchange(): return lax.all_to_all(blocks, axis, split_axis=0, concat_axis=0, tiled=True)  8.93 us
    pallas_call x2, Pallas kernels, rotate(): pl.pallas_call(rotate_kernel, out_shape=jax.ShapeDtypeStruct((pieces, row...  4.7 us
    unnamed x11, local copies, waits for them, and re-layouts  3.28 us
  transfers between devices with their start and end apart: 16, of which 8 were waited for; matrix products, arithmetic and copies ran while one was open for 1% of the time, Pallas kernels for 5%

profile of v7, /device:TPU:56, one launch (start us, length us, event | category | flops | bytes accessed | tf_op | source)
XLA Modules:
  0.0 144.0 jit_solution(8539028763793496930)
XLA Ops:
  0.7 2.3 %shard_map.55 = bf16[32,16,896]{2,1,0:T(8,128)(2,1)} custom-call(s32[1]{0:T(128)S(6)} %copy.9.length_ref, bf16[32,28672]{1,0:T(8,128)(2,1)} %grads_ref.1), custom_call_target="tpu_custom_call" | custom-call | bytes 1835008 | tf_op jit(solution)/shard_map/pallas_call | solution.py:68
  3.0 13.3 %all-to-all-start = ((bf16[32,16,896]{2,1,0:T(8,128)(2,1)}), bf16[32,16,896]{2,1,0:T(8,128)(2,1)S(1)}, u32[]{:S(2)}, u32[]{:S(2)}) async-start(bf16[32,16,896]{2,1,0:T(8,128)(2,1)} %shard_map.55), calls=%async_computation | async-start | bytes 1835008 | tf_op jit(solution)/shard_map/rows_dp/all_to_all | solution.py:21
  16.3 3.7 %collective-permute-start.1 = (bf16[512,128]{1,0:T(8,128)(2,1)S(1)}, bf16[512,128]{1,0:T(8,128)(2,1)S(1)}, u32[]{:S(2)}, u32[]{:S(2)}) collective-permute-start(bf16[512,128]{1,0:T(8,128)(2,1)S(1)} %copy-done.3), channel_id=1, source_target_pairs={{0,16},{16,0},{32,48},{48,32},{1,17},{17,1},{33,49},{49,33},{2,18}... | collective-permute-start | bytes 393224 | tf_op jit(solution)/shard_map/basis_x/ppermute | solution.py:26
  20.0 4.0 %collective-permute-start.3 = (bf16[512,128]{1,0:T(8,128)(2,1)S(1)}, bf16[512,128]{1,0:T(8,128)(2,1)S(1)}, u32[]{:S(2)}, u32[]{:S(2)}) collective-permute-start(bf16[512,128]{1,0:T(8,128)(2,1)S(1)} %copy-done.3), channel_id=1, source_target_pairs={{0,48},{16,32},{32,16},{48,0},{1,49},{17,33},{33,17},{49,1},{2,50}... | collective-permute-start | bytes 393224 | tf_op jit(solution)/shard_map/basis_x/ppermute | solution.py:26
  24.0 2.5 %collective-permute-start.2 = (bf16[512,128]{1,0:T(8,128)(2,1)S(1)}, bf16[512,128]{1,0:T(8,128)(2,1)S(1)}, u32[]{:S(2)}, u32[]{:S(2)}) collective-permute-start(bf16[512,128]{1,0:T(8,128)(2,1)S(1)} %copy-done.3), channel_id=1, source_target_pairs={{0,32},{16,48},{32,0},{48,16},{1,33},{17,49},{33,1},{49,17},{2,34}... | collective-permute-start | bytes 393224 | tf_op jit(solution)/shard_map/basis_x/ppermute | solution.py:26
  27.3 7.3 %collective-permute-start = (bf16[1,16,1024]{2,1,0:T(8,128)(2,1)S(1)}, bf16[1,16,1024]{2,1,0:T(8,128)(2,1)S(1)}, u32[]{:S(2)}, u32[]{:S(2)}) collective-permute-start(bf16[1,16,1024]{2,1,0:T(8,128)(2,1)S(1)} %maximum_bitcast_fusion), channel_id=1, source_target_pairs={{0,256},{64,320},{128,384},{192,448},{256,0},{320,64},{384,128},{4... | collective-permute-start | bytes 98312 | tf_op jit(solution)/shard_map/slab_z/ppermute | solution.py:26
  37.5 5.1 %collective-permute-done = bf16[1,16,1024]{2,1,0:T(8,128)(2,1)S(1)} collective-permute-done((bf16[1,16,1024]{2,1,0:T(8,128)(2,1)S(1)}, bf16[1,16,1024]{2,1,0:T(8,128)(2,1)S(1)}, u32[]{:S(2)}, u32[]{:S(2)}) %collective-permute-start) | collective-permute-done | bytes 32800 | tf_op jit(solution)/shard_map/slab_z/ppermute | solution.py:26
  44.5 2.4 %shard_map.56.rest_0_ = bf16[4,224,1024]{2,1,0:T(8,128)(2,1)} custom-call(bf16[512,896]{1,0:T(8,128)(2,1)S(1)} %bitcast.13, bf16[896,896]{1,0:T(8,128)(2,1)S(1)} %copy-done), custom_call_target="tpu_custom_call" | custom-call | flops 822083584 | bytes 1835008 | tf_op jit(solution)/shard_map/pallas_call | solution.py:106
  46.9 2.4 %collective-permute-start.6 = (bf16[4,512,128]{2,1,0:T(8,128)(2,1)S(1)}, bf16[4,512,128]{2,1,0:T(8,128)(2,1)S(1)}, u32[]{:S(2)}, u32[]{:S(2)}) collective-permute-start(bf16[4,512,128]{2,1,0:T(8,128)(2,1)S(1)} %pad_maximum_fusion.own_ref), channel_id=1, source_target_pairs={{0,1},{1,0},{2,3},{3,2},{4,5},{5,4},{6,7},{7,6},{8,9},{9,8},{10,11... | collective-permute-start | bytes 1572872 | tf_op jit(solution)/shard_map/basis_c/ppermute | solution.py:26
  49.3 4.6 %collective-permute-start.5 = (bf16[2,16,1024]{2,1,0:T(8,128)(2,1)S(1)}, bf16[2,16,1024]{2,1,0:T(8,128)(2,1)S(1)}, u32[]{:S(2)}, u32[]{:S(2)}) collective-permute-start(bf16[2,16,1024]{2,1,0:T(8,128)(2,1)S(1)} %pad_maximum_fusion.3), channel_id=1, source_target_pairs={{0,128},{64,192},{128,0},{192,64},{256,384},{320,448},{384,256},{4... | collective-permute-start | bytes 196616 | tf_op jit(solution)/shard_map/slab_z/ppermute | solution.py:26
  54.0 2.3 %shard_map.57 = bf16[4,224,1024]{2,1,0:T(8,128)(2,1)} custom-call(bf16[512,896]{1,0:T(8,128)(2,1)S(1)} %collective-permute-done.4.tokens_ref, bf16[896,896]{1,0:T(8,128)(2,1)S(1)} %copy-done, bf16[4,224,1024]{2,1,0:T(8,128)(2,1)} %shard_map.56.rest_0_), custom_call_target="tpu_custom_call", output_to_operand_aliasing={{}: (2, {})} | custom-call | flops 822083584 | bytes 1835008 | tf_op jit(solution)/shard_map/pallas_call | solution.py:106
  58.4 4.8 %all-to-all-start.1 = ((bf16[4,224,1024]{2,1,0:T(8,128)(2,1)}), bf16[4,224,1024]{2,1,0:T(8,128)(2,1)S(1)}, u32[]{:S(2)}, u32[]{:S(2)}) async-start(bf16[4,224,1024]{2,1,0:T(8,128)(2,1)} %shard_map.57), calls=%async_computation.1 | async-start | bytes 3670016 | tf_op jit(solution)/shard_map/sum_x/all_to_all | solution.py:21
  65.3 4.9 %collective-permute-done.7 = bf16[4,16,1024]{2,1,0:T(8,128)(2,1)S(1)} collective-permute-done((bf16[4,16,1024]{2,1,0:T(8,128)(2,1)S(1)}, bf16[4,16,1024]{2,1,0:T(8,128)(2,1)S(1)}, u32[]{:S(2)}, u32[]{:S(2)}) %collective-permute-start.7) | collective-permute-done | bytes 131104 | tf_op jit(solution)/shard_map/slab_z/ppermute | solution.py:26
  72.2 3.3 %collective-permute-start.8 = (bf16[8,16,512]{2,1,0:T(8,128)(2,1)S(1)}, bf16[8,16,512]{2,1,0:T(8,128)(2,1)S(1)}, u32[]{:S(2)}, u32[]{:S(2)}) collective-permute-start(bf16[8,16,512]{2,1,0:T(8,128)(2,1)S(1)} %convert_element_type.21), channel_id=1, source_target_pairs={{0,2},{2,0},{4,6},{6,4},{8,10},{10,8},{12,14},{14,12},{1,3},{3,1},... | collective-permute-start | bytes 393224 | tf_op jit(solution)/shard_map/panel_sum/ppermute | solution.py:26
  75.5 3.6 %collective-permute-done.8 = bf16[8,16,512]{2,1,0:T(8,128)(2,1)S(1)} collective-permute-done((bf16[8,16,512]{2,1,0:T(8,128)(2,1)S(1)}, bf16[8,16,512]{2,1,0:T(8,128)(2,1)S(1)}, u32[]{:S(2)}, u32[]{:S(2)}) %collective-permute-start.8) | collective-permute-done | bytes 131104 | tf_op jit(solution)/shard_map/panel_sum/ppermute | solution.py:26
  79.1 4.0 %collective-permute-start.9 = (bf16[8,16,512]{2,1,0:T(8,128)(2,1)S(1)}, bf16[8,16,512]{2,1,0:T(8,128)(2,1)S(1)}, u32[]{:S(2)}, u32[]{:S(2)}) collective-permute-start(bf16[8,16,512]{2,1,0:T(8,128)(2,1)S(1)} %fusion), channel_id=1, source_target_pairs={{0,4},{2,6},{4,0},{6,2},{8,12},{10,14},{12,8},{14,10},{1,5},{3,7},... | collective-permute-start | bytes 393224 | tf_op jit(solution)/shard_map/panel_sum/ppermute | solution.py:26
  83.2 5.1 %collective-permute-done.9 = bf16[8,16,512]{2,1,0:T(8,128)(2,1)S(1)} collective-permute-done((bf16[8,16,512]{2,1,0:T(8,128)(2,1)S(1)}, bf16[8,16,512]{2,1,0:T(8,128)(2,1)S(1)}, u32[]{:S(2)}, u32[]{:S(2)}) %collective-permute-start.9) | collective-permute-done | bytes 131104 | tf_op jit(solution)/shard_map/panel_sum/ppermute | solution.py:26
  89.5 3.5 %all-to-all-start.2 = ((bf16[8,224,128]{2,1,0:T(8,128)(2,1)}), bf16[8,224,128]{2,1,0:T(8,128)(2,1)S(1)}, u32[]{:S(2)}, u32[]{:S(2)}) async-start(bf16[8,224,128]{2,1,0:T(8,128)(2,1)} %shard_map.59), calls=%async_computation.2 | async-start | bytes 917504 | tf_op jit(solution)/shard_map/sum_z/all_to_all | solution.py:21
  93.0 4.6 %collective-permute-start.10 = (bf16[8,16,512]{2,1,0:T(8,128)(2,1)S(1)}, bf16[8,16,512]{2,1,0:T(8,128)(2,1)S(1)}, u32[]{:S(2)}, u32[]{:S(2)}) collective-permute-start(bf16[8,16,512]{2,1,0:T(8,128)(2,1)S(1)} %convert_element_type.25), channel_id=1, source_target_pairs={{0,8},{2,10},{4,12},{6,14},{8,0},{10,2},{12,4},{14,6},{1,9},{3,11}... | collective-permute-start | bytes 393224 | tf_op jit(solution)/shard_map/panel_sum/ppermute | solution.py:26
  97.6 8.9 %all-to-all-done.2.parts_ref = bf16[8,224,128]{2,1,0:T(8,128)(2,1)S(1)} async-done(((bf16[8,224,128]{2,1,0:T(8,128)(2,1)}), bf16[8,224,128]{2,1,0:T(8,128)(2,1)S(1)}, u32[]{:S(2)}, u32[]{:S(2)}) %all-to-all-start.2) | async-done | bytes 458784 | tf_op jit(solution)/shard_map/sum_z/all_to_all | solution.py:21
  107.3 3.5 %all-to-all-start.3 = ((bf16[8,224,128]{2,1,0:T(8,128)(2,1)}), bf16[8,224,128]{2,1,0:T(8,128)(2,1)S(1)}, u32[]{:S(2)}, u32[]{:S(2)}) async-start(bf16[8,224,128]{2,1,0:T(8,128)(2,1)} %shard_map.60), calls=%async_computation.3 | async-start | bytes 917504 | tf_op jit(solution)/shard_map/rotated_z/all_to_all | solution.py:21
  110.9 13.1 %all-gather = bf16[32,16,512]{2,1,0:T(8,128)(2,1)S(1)} all-gather(bf16[8,16,512]{2,1,0:T(8,128)(2,1)S(1)} %add_convert_fusion), channel_id=2, replica_groups=mesh['z'=8,'x'=4,'y'=8,'c'=2] {'x'}, dimensions={0}, use_global_device_ids=true | all-gather | bytes 655360 | tf_op jit(solution)/shard_map/panel_x/all_gather | solution.py:279
  127.8 2.8 %shard_map.61 = f32[4,224,128]{2,1,0:T(8,128)S(1)} custom-call(s32[2]{0:T(128)S(1)} %pad_add_fusion.at_ref, bf16[8,224,128]{2,1,0:T(8,128)(2,1)S(1)} %all-to-all-done.3.left_ref, bf16[4,8,16,512]{3,2,1,0:T(8,128)(2,1)S(1)} %bitcast.15, bf16[4,8,16,512]{3,2,1,0:T(8,128)(2,1)S(1)} %collective-permute-done.11.other_ref), custom_call_target="tpu_custom_call" | custom-call | flops 234881024 | bytes 1048576 | tf_op jit(solution)/shard_map/pallas_call | solution.py:214
  130.7 12.6 %all_to_all.25 = f32[4,224,128]{2,1,0:T(8,128)S(1)} all-to-all(f32[4,224,128]{2,1,0:T(8,128)S(1)} %shard_map.61), channel_id=1, replica_groups=mesh['z'=8,'x'=4,'y'=8,'c'=2] {'x'}, dimensions={0} | all-to-all | bytes 917504 | tf_op jit(solution)/shard_map/out_x/all_to_all | solution.py:21
  (40 shorter events, 18.3 us)
Async XLA Ops:
  0.7 15.7 %copy-start.3 = (bf16[512,128]{1,0:T(8,128)(2,1)S(1)}, bf16[512,128]{1,0:T(8,128)(2,1)}, u32[]{:S(2)}) copy-start(bf16[512,128]{1,0:T(8,128)(2,1)} %param.8) | copy-start | bytes 393220
  3.0 41.5 %copy-start = (bf16[896,896]{1,0:T(8,128)(2,1)S(1)}, bf16[896,896]{1,0:T(8,128)(2,1)}, u32[]{:S(2)}) copy-start(bf16[896,896]{1,0:T(8,128)(2,1)} %basis_ref.3) | copy-start | bytes 4816900
  3.0 39.6 %all-to-all-start = ((bf16[32,16,896]{2,1,0:T(8,128)(2,1)}), bf16[32,16,896]{2,1,0:T(8,128)(2,1)S(1)}, u32[]{:S(2)}, u32[]{:S(2)}) async-start(bf16[32,16,896]{2,1,0:T(8,128)(2,1)} %shard_map.55), calls=%async_computation | async-start | bytes 1835008 | tf_op jit(solution)/shard_map/rows_dp/all_to_all | solution.py:21
  16.3 18.3 %collective-permute-start.1 = (bf16[512,128]{1,0:T(8,128)(2,1)S(1)}, bf16[512,128]{1,0:T(8,128)(2,1)S(1)}, u32[]{:S(2)}, u32[]{:S(2)}) collective-permute-start(bf16[512,128]{1,0:T(8,128)(2,1)S(1)} %copy-done.3), channel_id=1, source_target_pairs={{0,16},{16,0},{32,48},{48,32},{1,17},{17,1},{33,49},{49,33},{2,18}... | collective-permute-start | bytes 393224 | tf_op jit(solution)/shard_map/basis_x/ppermute | solution.py:26
  20.0 14.6 %collective-permute-start.3 = (bf16[512,128]{1,0:T(8,128)(2,1)S(1)}, bf16[512,128]{1,0:T(8,128)(2,1)S(1)}, u32[]{:S(2)}, u32[]{:S(2)}) collective-permute-start(bf16[512,128]{1,0:T(8,128)(2,1)S(1)} %copy-done.3), channel_id=1, source_target_pairs={{0,48},{16,32},{32,16},{48,0},{1,49},{17,33},{33,17},{49,1},{2,50}... | collective-permute-start | bytes 393224 | tf_op jit(solution)/shard_map/basis_x/ppermute | solution.py:26
  24.0 11.8 %collective-permute-start.2 = (bf16[512,128]{1,0:T(8,128)(2,1)S(1)}, bf16[512,128]{1,0:T(8,128)(2,1)S(1)}, u32[]{:S(2)}, u32[]{:S(2)}) collective-permute-start(bf16[512,128]{1,0:T(8,128)(2,1)S(1)} %copy-done.3), channel_id=1, source_target_pairs={{0,32},{16,48},{32,0},{48,16},{1,33},{17,49},{33,1},{49,17},{2,34}... | collective-permute-start | bytes 393224 | tf_op jit(solution)/shard_map/basis_x/ppermute | solution.py:26
  27.3 15.3 %collective-permute-start = (bf16[1,16,1024]{2,1,0:T(8,128)(2,1)S(1)}, bf16[1,16,1024]{2,1,0:T(8,128)(2,1)S(1)}, u32[]{:S(2)}, u32[]{:S(2)}) collective-permute-start(bf16[1,16,1024]{2,1,0:T(8,128)(2,1)S(1)} %maximum_bitcast_fusion), channel_id=1, source_target_pairs={{0,256},{64,320},{128,384},{192,448},{256,0},{320,64},{384,128},{4... | collective-permute-start | bytes 98312 | tf_op jit(solution)/shard_map/slab_z/ppermute | solution.py:26
  35.8 0.7 copy-start.4
  42.6 11.4 %collective-permute-start.4 = (bf16[512,896]{1,0:T(8,128)(2,1)S(1)}, bf16[512,896]{1,0:T(8,128)(2,1)S(1)}, u32[]{:S(2)}, u32[]{:S(2)}) collective-permute-start(bf16[512,896]{1,0:T(8,128)(2,1)S(1)} %bitcast.12), channel_id=1, source_target_pairs={{0,1},{1,0},{2,3},{3,2},{4,5},{5,4},{6,7},{7,6},{8,9},{9,8},{10,11... | collective-permute-start | bytes 2752520 | tf_op jit(solution)/shard_map/rows_c/ppermute | solution.py:26
  46.9 10.7 %collective-permute-start.6 = (bf16[4,512,128]{2,1,0:T(8,128)(2,1)S(1)}, bf16[4,512,128]{2,1,0:T(8,128)(2,1)S(1)}, u32[]{:S(2)}, u32[]{:S(2)}) collective-permute-start(bf16[4,512,128]{2,1,0:T(8,128)(2,1)S(1)} %pad_maximum_fusion.own_ref), channel_id=1, source_target_pairs={{0,1},{1,0},{2,3},{3,2},{4,5},{5,4},{6,7},{7,6},{8,9},{9,8},{10,11... | collective-permute-start | bytes 1572872 | tf_op jit(solution)/shard_map/basis_c/ppermute | solution.py:26
  49.3 8.3 %collective-permute-start.5 = (bf16[2,16,1024]{2,1,0:T(8,128)(2,1)S(1)}, bf16[2,16,1024]{2,1,0:T(8,128)(2,1)S(1)}, u32[]{:S(2)}, u32[]{:S(2)}) collective-permute-start(bf16[2,16,1024]{2,1,0:T(8,128)(2,1)S(1)} %pad_maximum_fusion.3), channel_id=1, source_target_pairs={{0,128},{64,192},{128,0},{192,64},{256,384},{320,448},{384,256},{4... | collective-permute-start | bytes 196616 | tf_op jit(solution)/shard_map/slab_z/ppermute | solution.py:26
  57.6 0.8 copy-start.1
  58.4 29.9 %all-to-all-start.1 = ((bf16[4,224,1024]{2,1,0:T(8,128)(2,1)}), bf16[4,224,1024]{2,1,0:T(8,128)(2,1)S(1)}, u32[]{:S(2)}, u32[]{:S(2)}) async-start(bf16[4,224,1024]{2,1,0:T(8,128)(2,1)} %shard_map.57), calls=%async_computation.1 | async-start | bytes 3670016 | tf_op jit(solution)/shard_map/sum_x/all_to_all | solution.py:21
  63.3 6.9 %collective-permute-start.7 = (bf16[4,16,1024]{2,1,0:T(8,128)(2,1)S(1)}, bf16[4,16,1024]{2,1,0:T(8,128)(2,1)S(1)}, u32[]{:S(2)}, u32[]{:S(2)}) collective-permute-start(bf16[4,16,1024]{2,1,0:T(8,128)(2,1)S(1)} %pad_maximum_fusion.2), channel_id=1, source_target_pairs={{0,64},{64,0},{128,192},{192,128},{256,320},{320,256},{384,448},{4... | collective-permute-start | bytes 393224 | tf_op jit(solution)/shard_map/slab_z/ppermute | solution.py:26
  70.2 1.0 copy-start.2
  72.2 6.9 %collective-permute-start.8 = (bf16[8,16,512]{2,1,0:T(8,128)(2,1)S(1)}, bf16[8,16,512]{2,1,0:T(8,128)(2,1)S(1)}, u32[]{:S(2)}, u32[]{:S(2)}) collective-permute-start(bf16[8,16,512]{2,1,0:T(8,128)(2,1)S(1)} %convert_element_type.21), channel_id=1, source_target_pairs={{0,2},{2,0},{4,6},{6,4},{8,10},{10,8},{12,14},{14,12},{1,3},{3,1},... | collective-permute-start | bytes 393224 | tf_op jit(solution)/shard_map/panel_sum/ppermute | solution.py:26
  79.1 9.2 %collective-permute-start.9 = (bf16[8,16,512]{2,1,0:T(8,128)(2,1)S(1)}, bf16[8,16,512]{2,1,0:T(8,128)(2,1)S(1)}, u32[]{:S(2)}, u32[]{:S(2)}) collective-permute-start(bf16[8,16,512]{2,1,0:T(8,128)(2,1)S(1)} %fusion), channel_id=1, source_target_pairs={{0,4},{2,6},{4,0},{6,2},{8,12},{10,14},{12,8},{14,10},{1,5},{3,7},... | collective-permute-start | bytes 393224 | tf_op jit(solution)/shard_map/panel_sum/ppermute | solution.py:26
  89.5 17.0 %all-to-all-start.2 = ((bf16[8,224,128]{2,1,0:T(8,128)(2,1)}), bf16[8,224,128]{2,1,0:T(8,128)(2,1)S(1)}, u32[]{:S(2)}, u32[]{:S(2)}) async-start(bf16[8,224,128]{2,1,0:T(8,128)(2,1)} %shard_map.59), calls=%async_computation.2 | async-start | bytes 917504 | tf_op jit(solution)/shard_map/sum_z/all_to_all | solution.py:21
  93.0 17.9 %collective-permute-start.10 = (bf16[8,16,512]{2,1,0:T(8,128)(2,1)S(1)}, bf16[8,16,512]{2,1,0:T(8,128)(2,1)S(1)}, u32[]{:S(2)}, u32[]{:S(2)}) collective-permute-start(bf16[8,16,512]{2,1,0:T(8,128)(2,1)S(1)} %convert_element_type.25), channel_id=1, source_target_pairs={{0,8},{2,10},{4,12},{6,14},{8,0},{10,2},{12,4},{14,6},{1,9},{3,11}... | collective-permute-start | bytes 393224 | tf_op jit(solution)/shard_map/panel_sum/ppermute | solution.py:26
  107.3 20.5 %all-to-all-start.3 = ((bf16[8,224,128]{2,1,0:T(8,128)(2,1)}), bf16[8,224,128]{2,1,0:T(8,128)(2,1)S(1)}, u32[]{:S(2)}, u32[]{:S(2)}) async-start(bf16[8,224,128]{2,1,0:T(8,128)(2,1)} %shard_map.60), calls=%async_computation.3 | async-start | bytes 917504 | tf_op jit(solution)/shard_map/rotated_z/all_to_all | solution.py:21
  124.0 3.8 %collective-permute-start.11 = (bf16[4,8,16,512]{3,2,1,0:T(8,128)(2,1)S(1)}, bf16[4,8,16,512]{3,2,1,0:T(8,128)(2,1)S(1)}, u32[]{:S(2)}, u32[]{:S(2)}) collective-permute-start(bf16[4,8,16,512]{3,2,1,0:T(8,128)(2,1)S(1)} %bitcast.14), channel_id=1, source_target_pairs={{0,1},{1,0},{2,3},{3,2},{4,5},{5,4},{6,7},{7,6},{8,9},{9,8},{10,11... | collective-permute-start | bytes 1572872 | tf_op jit(solution)/shard_map/panel_c/ppermute | solution.py:26

commit v8 on v6

v8 whole, which is shorter than its diff:
```python
import functools

import jax
import jax.numpy as jnp
from jax import lax
from jax.experimental import pallas as pl
from jax.experimental.pallas import tpu as pltpu
from jax.sharding import Mesh, PartitionSpec as P

BF = jnp.bfloat16
F32 = jnp.float32
DP = ("z", "x")
TN = ("y", "c")
MIB = 1024 * 1024
PARAMS = pltpu.CompilerParams(vmem_limit_bytes=32 * MIB)
SMEM = pltpu.SMEM
VMEM = pltpu.VMEM


def exchange(blocks, axis):
    return lax.all_to_all(blocks, axis, split_axis=0, concat_axis=0, tiled=True)


def swap(block, axis, bit):
    count = lax.axis_size(axis)
    return lax.ppermute(block, axis, [(i, i ^ bit) for i in range(count)])


def reverse(index, width):
    result = 0
    for k in range(width):
        result = result | (((index >> k) & 1) << (width - 1 - k))
    return result


def add_from(block, axis, bit):
    return block + swap(block.astype(BF), axis, bit).astype(F32)


def cost(flops, moved):
    return pl.CostEstimate(flops=flops, bytes_accessed=moved, transcendentals=0)


def split_kernel(length_ref, grads_ref, out_ref, held, sems):
    parts, half, wide = out_ref.shape
    steps, _, chunk = held.shape
    each = parts // steps
    first = lax.axis_index("c") * half
    copies = [
        pltpu.make_async_copy(
            grads_ref.at[pl.ds(first, half), pl.ds(k * chunk, chunk)], held.at[k], sems.at[k]
        )
        for k in range(steps)
    ]
    for copy in copies:
        copy.start()
    slot = first + lax.broadcasted_iota(jnp.int32, (half, wide), 0)
    live = slot < length_ref[0]
    for k in range(steps):
        copies[k].wait()
        for q in range(each):
            piece = held[k, :, q * wide : (q + 1) * wide]
            out_ref[k * each + q] = jnp.where(live, piece, jnp.zeros_like(piece))


def split_rows(grads, length, half, parts, steps=4):
    wide = grads.shape[1] // parts
    return pl.pallas_call(
        split_kernel,
        out_shape=jax.ShapeDtypeStruct((parts, half, wide), grads.dtype),
        in_specs=[pl.BlockSpec(memory_space=SMEM), pl.BlockSpec(memory_space=pl.ANY)],
        out_specs=pl.BlockSpec(memory_space=VMEM),
        scratch_shapes=[
            VMEM((steps, half, grads.shape[1] // steps), grads.dtype),
            pltpu.SemaphoreType.DMA((steps,)),
        ],
        compiler_params=pltpu.CompilerParams(vmem_limit_bytes=58 * MIB),
        cost_estimate=cost(0, 4 * half * grads.shape[1]),
    )(length, grads)


def rotate_kernel(tokens_ref, basis_ref, *rest):
    out_ref = rest[-1]
    count, slots, wide = tokens_ref.shape
    tokens = tokens_ref[...].reshape(count * slots, wide)
    product = jnp.dot(tokens, basis_ref[...], preferred_element_type=F32)
    pieces = out_ref.shape[0]
    for q in range(pieces):
        rows = [product[k * slots : (k + 1) * slots] for k in range(q, count, pieces)]
        out_ref[q] = jnp.concatenate(rows, axis=0).T.astype(BF)


def rotate(tokens, basis, place, pieces, before=None):
    count, slots, wide = tokens.shape
    columns = basis.shape[1]
    lanes = count * slots // pieces
    in_specs = [
        pl.BlockSpec((count, slots, wide), lambda i: (0, 0, 0)),
        pl.BlockSpec((wide, columns), lambda i: (0, 0)),
    ]
    args = [tokens, basis]
    aliases = {}
    if before is not None:
        in_specs.append(pl.BlockSpec(memory_space=pl.ANY))
        args.append(before)
        aliases = {2: 0}
    return pl.pallas_call(
        rotate_kernel,
        out_shape=jax.ShapeDtypeStruct((pieces, columns, 2 * lanes), BF),
        grid=(1,),
        in_specs=in_specs,
        out_specs=pl.BlockSpec((pieces, columns, lanes), lambda i: (0, 0, place)),
        input_output_aliases=aliases,
        compiler_params=PARAMS,
        cost_estimate=cost(2 * count * slots * wide * columns, 2 * count * slots * (wide + columns)),
    )(*args)


def sum_kernel(scale, parts_ref, out_ref):
    total = parts_ref[0].astype(F32)
    for q in range(1, parts_ref.shape[0]):
        total = total + parts_ref[q].astype(F32)
    if scale is not None:
        total = total * scale
    total = total.astype(out_ref.dtype)
    if len(out_ref.shape) == 2:
        out_ref[...] = total
    else:
        for q in range(out_ref.shape[0]):
            out_ref[q] = total


def sum_parts(parts, copies=None, steps=1, dtype=BF, scale=None):
    count, rows, lanes = parts.shape
    block = (rows // steps, lanes)
    if copies is None:
        shape, out_spec = (rows, lanes), pl.BlockSpec(block, lambda i: (i, 0))
    else:
        shape = (copies, rows, lanes)
        out_spec = pl.BlockSpec((copies,) + block, lambda i: (0, i, 0))
    return pl.pallas_call(
        functools.partial(sum_kernel, scale),
        out_shape=jax.ShapeDtypeStruct(shape, dtype),
        grid=(steps,),
        in_specs=[pl.BlockSpec((count,) + block, lambda i: (0, i, 0))],
        out_specs=out_spec,
        compiler_params=PARAMS,
        cost_estimate=cost(parts.size, 2 * parts.size),
    )(parts)


def panel_kernel(at_ref, slab_ref, *refs):
    *basis_refs, out_ref = refs
    count, slots, _ = out_ref.shape
    cores, deep, lanes = basis_refs[0].shape
    for k, basis_ref in enumerate(basis_refs):
        total = jnp.zeros((count * slots, lanes), F32)
        for r in range(cores):
            left = slab_ref[:, r * deep : (r + 1) * deep]
            total = total + jnp.dot(left, basis_ref[r], preferred_element_type=F32)
        start = pl.multiple_of((k ^ at_ref[0]) * lanes, lanes)
        out_ref[:, :, pl.ds(start, lanes)] = total.reshape(count, slots, lanes)


def panel_part(at, slab, bases):
    count, slots, deep = slab.shape
    columns = len(bases) * bases[0].shape[2]
    return pl.pallas_call(
        panel_kernel,
        out_shape=jax.ShapeDtypeStruct((count, slots, columns), F32),
        in_specs=[pl.BlockSpec(memory_space=SMEM)]
        + [pl.BlockSpec(memory_space=VMEM)] * (1 + len(bases)),
        out_specs=pl.BlockSpec(memory_space=VMEM),
        compiler_params=PARAMS,
        cost_estimate=cost(2 * count * slots * columns * deep, 8 * bases[0].size),
    )(at, slab.reshape(count * slots, deep), *bases)


def example_kernel(at_ref, left_ref, own_ref, other_ref, out_ref):
    rows, lanes = left_ref.shape
    count, slots, columns = own_ref.shape
    places = [reverse(k ^ at_ref[1], 3) for k in range(count)]
    right = jnp.concatenate([own_ref[k] for k in places] + [other_ref[k] for k in places], axis=0)
    tile = 128
    slot = lax.broadcasted_iota(jnp.int32, (tile, lanes), 1)
    owner = (slot % (lanes // 2)) // slots
    wide = out_ref.shape[2]
    for n in range(0, columns, 256):
        weights = right[:, n : n + 256]
        for r in range(0, rows, tile):
            left = left_ref[r : r + tile]
            total = jnp.zeros((tile, 256), F32)
            for j in range(count):
                picked = jnp.where(owner == j, left, jnp.zeros_like(left))
                one = jnp.dot(picked, weights, preferred_element_type=F32)
                total = total + one * one
            total = total.astype(out_ref.dtype)
            for q in range(0, 256, wide):
                out_ref[(n + q) // wide, r : r + tile] = total[:, q : q + wide]


def examples(at, left, own, other, nx):
    rows, lanes = left.shape
    columns = own.shape[-1]
    return pl.pallas_call(
        example_kernel,
        out_shape=jax.ShapeDtypeStruct((nx, rows, columns // nx), BF),
        in_specs=[pl.BlockSpec(memory_space=SMEM)] + [pl.BlockSpec(memory_space=VMEM)] * 3,
        out_specs=pl.BlockSpec(memory_space=VMEM),
        compiler_params=PARAMS,
        cost_estimate=cost(2 * lanes * rows * columns, 4 * own.size),
    )(at, left, own, other)


def per_device(grads_out, inputs, basis_out, basis_in, lengths):
    nz, nx, ny, nc = (lax.axis_size(a) for a in ("z", "x", "y", "c"))
    iz, ix, iy, ic = (lax.axis_index(a) for a in ("z", "x", "y", "c"))
    slots = grads_out.shape[0]
    half = slots // nc
    wide, columns = basis_out.shape
    deep = basis_in.shape[0]
    at = jnp.stack([ix, iz]).astype(jnp.int32)
    tie = lax.optimization_barrier

    blocks = split_rows(grads_out, lengths, half, nz * nx)
    with jax.named_scope("rows_dp"):
        own = exchange(blocks, DP)

    def features(cr):
        start = (iy * nc + (ic ^ cr)) * deep
        return lax.dynamic_slice(inputs, (ic * half, start), (half, deep))

    slab = jnp.concatenate([features(0), features(1)], axis=1)[None]
    with jax.named_scope("slab_z"):
        more_slab = swap(slab, "z", 4)
    with jax.named_scope("basis_cx"):
        pair = jnp.stack([basis_in, swap(basis_in, "c", 1)])
        basis_x = [pair] + [swap(pair, "x", k) for k in range(1, nx)]
    own, more_slab, *basis_x = tie((own, more_slab, *basis_x))
    with jax.named_scope("rows_c"):
        other = swap(own, "c", 1)
    parts = rotate(own, basis_out, 0, nx)
    slab = jnp.concatenate([slab, more_slab], axis=0)
    parts = rotate(other, basis_out, 1, nx, parts)
    parts, slab = tie((parts, slab))
    with jax.named_scope("sum_xz"):
        parts = exchange(parts.reshape(nx * nz, columns // nz, parts.shape[2]), ("x", "z"))

    with jax.named_scope("slab_z"):
        slab = jnp.concatenate([slab, swap(slab, "z", 2)], axis=0)
        slab = jnp.concatenate([slab, swap(slab, "z", 1)], axis=0)
    piece = panel_part(at, slab, basis_x)
    with jax.named_scope("panel_sum"):
        piece = add_from(piece, "y", 1)
        piece = add_from(piece, "y", 4)
    parts, piece = tie((parts, piece))
    with jax.named_scope("panel_sum"):
        piece = add_from(piece, "y", 2).astype(BF)
    with jax.named_scope("panel_c"):
        piece_other = swap(piece, "c", 1)
    rotated = sum_parts(parts, copies=nz)
    with jax.named_scope("rotated_z"):
        rotated = exchange(rotated, "z").reshape(columns, parts.shape[2])

    result = examples(at, rotated, piece, piece_other, nx)
    with jax.named_scope("out_x"):
        result = exchange(result, "x")
    return sum_parts(result, dtype=F32, scale=1.0 / (nz * nx * slots))


def solution(mesh):
    fine = Mesh(mesh.devices.reshape(8, 4, 8, 2), ("z", "x", "y", "c"))
    placed = (P(DP, None), P(DP, None), P(DP, TN), P(TN, DP), P(DP))
    return jax.shard_map(
        per_device, mesh=fine, in_specs=placed, out_specs=P(TN, DP), check_vma=False
    )
```

time: 157 us -> 174 us (1.11)
  waiting for transfers between devices: 49.2 us -> 72.3 us
  between operations: 14.4 us -> 0.89 us
  starting transfers between devices: 64.8 us -> 69.2 us
  blocking collectives: 13 us -> 17.2 us
    ppermute x11 -> x12, waiting for transfers between devices: 38.8 us -> 71.6 us  [swap(): return lax.ppermute(block, axis, [(i, i ^ bit) for i in range(count)])]
    all_to_all x4 -> x3, waiting for transfers between devices: 9.61 us -> 0.75 us  [exchange(): return lax.all_to_all(blocks, axis, split_axis=0, concat_axis=0, tiled=True)]
    all_to_all x1, blocking collectives: 13 us -> 17.2 us  [exchange(): return lax.all_to_all(blocks, axis, split_axis=0, concat_axis=0, tiled=True)]
    all_to_all x4 -> x3, starting transfers between devices: 24.9 us -> 27.9 us  [exchange(): return lax.all_to_all(blocks, axis, split_axis=0, concat_axis=0, tiled=True)]
    unnamed x7 -> x4, local copies, waits for them, and re-layouts: 1.99 us -> 0.01 us
    ppermute x11 -> x12, starting transfers between devices: 39.8 us -> 41.3 us  [swap(): return lax.ppermute(block, axis, [(i, i ^ bit) for i in range(count)])]
  transfers between devices with their start and end apart: 16 -> 15, of which waited for: 9 -> 12; matrix products, arithmetic and copies ran while one was open for 0% -> 1% of each run, Pallas kernels for 4% -> 2%
where the time goes in v8:
time: 174 us
  waiting for transfers between devices  72.3 us (42%)
  starting transfers between devices  69.2 us (40%)
  blocking collectives  17.2 us (10%)
  Pallas kernels  12.9 us (7%)
    ppermute x12, waiting for transfers between devices, swap(): return lax.ppermute(block, axis, [(i, i ^ bit) for i in range(count)])  71.6 us
    ppermute x12, starting transfers between devices, swap(): return lax.ppermute(block, axis, [(i, i ^ bit) for i in range(count)])  41.3 us
    all_to_all x3, starting transfers between devices, exchange(): return lax.all_to_all(blocks, axis, split_axis=0, concat_axis=0, tiled=True)  27.9 us
    all_to_all x1, blocking collectives, exchange(): return lax.all_to_all(blocks, axis, split_axis=0, concat_axis=0, tiled=True)  17.2 us
    pallas_call x2, Pallas kernels, rotate(): pl.pallas_call(rotate_kernel, out_shape=jax.ShapeDtypeStruct((pieces, col...  4.67 us
  transfers between devices with their start and end apart: 15, of which 12 were waited for; matrix products, arithmetic and copies ran while one was open for 1% of the time, Pallas kernels for 2%

profile of v8, /device:TPU:56, one launch (start us, length us, event | category | flops | bytes accessed | tf_op | source)
XLA Modules:
  0.0 173.6 jit_solution(8589416008098127678)
XLA Ops:
  0.7 2.3 %shard_map.55 = bf16[32,16,896]{2,1,0:T(8,128)(2,1)} custom-call(s32[1]{0:T(128)S(6)} %copy.8.length_ref, bf16[32,28672]{1,0:T(8,128)(2,1)} %grads_ref.1), custom_call_target="tpu_custom_call" | custom-call | bytes 1835008 | tf_op jit(solution)/shard_map/pallas_call | solution.py:68
  3.0 13.3 %all-to-all-start = ((bf16[32,16,896]{2,1,0:T(8,128)(2,1)}), bf16[32,16,896]{2,1,0:T(8,128)(2,1)S(1)}, u32[]{:S(2)}, u32[]{:S(2)}) async-start(bf16[32,16,896]{2,1,0:T(8,128)(2,1)} %shard_map.55), calls=%async_computation | async-start | bytes 1835008 | tf_op jit(solution)/shard_map/rows_dp/all_to_all | solution.py:21
  16.3 1.9 %collective-permute-start.1 = (bf16[512,128]{1,0:T(8,128)(2,1)S(1)}, bf16[512,128]{1,0:T(8,128)(2,1)S(1)}, u32[]{:S(2)}, u32[]{:S(2)}) collective-permute-start(bf16[512,128]{1,0:T(8,128)(2,1)S(1)} %copy-done.1), channel_id=1, source_target_pairs={{0,1},{1,0},{2,3},{3,2},{4,5},{5,4},{6,7},{7,6},{8,9},{9,8},{10,11... | collective-permute-start | bytes 393224 | tf_op jit(solution)/shard_map/basis_cx/ppermute | solution.py:26
  19.6 4.9 %collective-permute-start.4 = (bf16[2,512,128]{2,1,0:T(8,128)(2,1)S(1)}, bf16[2,512,128]{2,1,0:T(8,128)(2,1)S(1)}, u32[]{:S(2)}, u32[]{:S(2)}) collective-permute-start(bf16[2,512,128]{2,1,0:T(8,128)(2,1)S(1)} %pad_maximum_fusion.refs_0_), channel_id=1, source_target_pairs={{0,48},{16,32},{32,16},{48,0},{1,49},{17,33},{33,17},{49,1},{2,50}... | collective-permute-start | bytes 786440 | tf_op jit(solution)/shard_map/basis_cx/ppermute | solution.py:26
  24.5 2.8 %collective-permute-start.3 = (bf16[2,512,128]{2,1,0:T(8,128)(2,1)S(1)}, bf16[2,512,128]{2,1,0:T(8,128)(2,1)S(1)}, u32[]{:S(2)}, u32[]{:S(2)}) collective-permute-start(bf16[2,512,128]{2,1,0:T(8,128)(2,1)S(1)} %pad_maximum_fusion.refs_0_), channel_id=1, source_target_pairs={{0,32},{16,48},{32,0},{48,16},{1,33},{17,49},{33,1},{49,17},{2,34}... | collective-permute-start | bytes 786440 | tf_op jit(solution)/shard_map/basis_cx/ppermute | solution.py:26
  27.3 2.1 %collective-permute-start.2 = (bf16[2,512,128]{2,1,0:T(8,128)(2,1)S(1)}, bf16[2,512,128]{2,1,0:T(8,128)(2,1)}, u32[]{:S(2)}, u32[]{:S(2)}) collective-permute-start(bf16[2,512,128]{2,1,0:T(8,128)(2,1)S(1)} %pad_maximum_fusion.refs_0_), channel_id=1, source_target_pairs={{0,16},{16,0},{32,48},{48,32},{1,17},{17,1},{33,49},{49,33},{2,18}... | collective-permute-start | bytes 786440 | tf_op jit(solution)/shard_map/basis_cx/ppermute | solution.py:26
  30.2 7.6 %collective-permute-start = (bf16[1,16,1024]{2,1,0:T(8,128)(2,1)S(1)}, bf16[1,16,1024]{2,1,0:T(8,128)(2,1)S(1)}, u32[]{:S(2)}, u32[]{:S(2)}) collective-permute-start(bf16[1,16,1024]{2,1,0:T(8,128)(2,1)S(1)} %maximum_bitcast_fusion), channel_id=1, source_target_pairs={{0,256},{64,320},{128,384},{192,448},{256,0},{320,64},{384,128},{4... | collective-permute-start | bytes 98312 | tf_op jit(solution)/shard_map/slab_z/ppermute | solution.py:26
  37.8 5.1 %collective-permute-done = bf16[1,16,1024]{2,1,0:T(8,128)(2,1)S(1)} collective-permute-done((bf16[1,16,1024]{2,1,0:T(8,128)(2,1)S(1)}, bf16[1,16,1024]{2,1,0:T(8,128)(2,1)S(1)}, u32[]{:S(2)}, u32[]{:S(2)}) %collective-permute-start) | collective-permute-done | bytes 32800 | tf_op jit(solution)/shard_map/slab_z/ppermute | solution.py:26
  46.0 2.3 %shard_map.56.rest_0_ = bf16[4,896,256]{2,1,0:T(8,128)(2,1)} custom-call(bf16[32,16,896]{2,1,0:T(8,128)(2,1)S(1)} %all-to-all-done.tokens_ref, bf16[896,896]{1,0:T(8,128)(2,1)S(1)} %copy-done), custom_call_target="tpu_custom_call" | custom-call | flops 822083584 | bytes 1835008 | tf_op jit(solution)/shard_map/pallas_call | solution.py:107
  48.5 2.3 %shard_map.57 = bf16[4,896,256]{2,1,0:T(8,128)(2,1)} custom-call(bf16[32,16,896]{2,1,0:T(8,128)(2,1)S(1)} %collective-permute-done.5.tokens_ref, bf16[896,896]{1,0:T(8,128)(2,1)S(1)} %copy-done, bf16[4,896,256]{2,1,0:T(8,128)(2,1)} %shard_map.56.rest_0_), custom_call_target="tpu_custom_call", output_to_operand_aliasing={{}: (2, {})} | custom-call | flops 822083584 | bytes 1835008 | tf_op jit(solution)/shard_map/pallas_call | solution.py:107
  50.8 9.1 %all-to-all-start.1 = ((bf16[32,112,256]{2,1,0:T(8,128)(2,1)}), bf16[32,112,256]{2,1,0:T(8,128)(2,1)S(1)}, u32[]{:S(2)}, u32[]{:S(2)}) async-start(bf16[32,112,256]{2,1,0:T(8,128)(2,1)} %bitcast.5), calls=%async_computation.1 | async-start | bytes 3670016 | tf_op jit(solution)/shard_map/sum_xz/all_to_all | solution.py:21
  59.9 4.6 %collective-permute-start.6 = (bf16[2,16,1024]{2,1,0:T(8,128)(2,1)S(1)}, bf16[2,16,1024]{2,1,0:T(8,128)(2,1)S(1)}, u32[]{:S(2)}, u32[]{:S(2)}) collective-permute-start(bf16[2,16,1024]{2,1,0:T(8,128)(2,1)S(1)} %pad_maximum_fusion.3), channel_id=1, source_target_pairs={{0,128},{64,192},{128,0},{192,64},{256,384},{320,448},{384,256},{4... | collective-permute-start | bytes 196616 | tf_op jit(solution)/shard_map/slab_z/ppermute | solution.py:26
  64.5 41.1 %collective-permute-done.6 = bf16[2,16,1024]{2,1,0:T(8,128)(2,1)S(1)} collective-permute-done((bf16[2,16,1024]{2,1,0:T(8,128)(2,1)S(1)}, bf16[2,16,1024]{2,1,0:T(8,128)(2,1)S(1)}, u32[]{:S(2)}, u32[]{:S(2)}) %collective-permute-start.6) | collective-permute-done | bytes 65568 | tf_op jit(solution)/shard_map/slab_z/ppermute | solution.py:26
  105.7 2.0 %collective-permute-start.7 = (bf16[4,16,1024]{2,1,0:T(8,128)(2,1)S(1)}, bf16[4,16,1024]{2,1,0:T(8,128)(2,1)S(1)}, u32[]{:S(2)}, u32[]{:S(2)}) collective-permute-start(bf16[4,16,1024]{2,1,0:T(8,128)(2,1)S(1)} %pad_maximum_fusion.2), channel_id=1, source_target_pairs={{0,64},{64,0},{128,192},{192,128},{256,320},{320,256},{384,448},{4... | collective-permute-start | bytes 393224 | tf_op jit(solution)/shard_map/slab_z/ppermute | solution.py:26
  107.8 4.8 %collective-permute-done.7 = bf16[4,16,1024]{2,1,0:T(8,128)(2,1)S(1)} collective-permute-done((bf16[4,16,1024]{2,1,0:T(8,128)(2,1)S(1)}, bf16[4,16,1024]{2,1,0:T(8,128)(2,1)S(1)}, u32[]{:S(2)}, u32[]{:S(2)}) %collective-permute-start.7) | collective-permute-done | bytes 131104 | tf_op jit(solution)/shard_map/slab_z/ppermute | solution.py:26
  114.0 3.3 %collective-permute-start.8 = (bf16[8,16,512]{2,1,0:T(8,128)(2,1)S(1)}, bf16[8,16,512]{2,1,0:T(8,128)(2,1)S(1)}, u32[]{:S(2)}, u32[]{:S(2)}) collective-permute-start(bf16[8,16,512]{2,1,0:T(8,128)(2,1)S(1)} %convert_element_type.21), channel_id=1, source_target_pairs={{0,2},{2,0},{4,6},{6,4},{8,10},{10,8},{12,14},{14,12},{1,3},{3,1},... | collective-permute-start | bytes 393224 | tf_op jit(solution)/shard_map/panel_sum/ppermute | solution.py:26
  117.3 3.6 %collective-permute-done.8 = bf16[8,16,512]{2,1,0:T(8,128)(2,1)S(1)} collective-permute-done((bf16[8,16,512]{2,1,0:T(8,128)(2,1)S(1)}, bf16[8,16,512]{2,1,0:T(8,128)(2,1)S(1)}, u32[]{:S(2)}, u32[]{:S(2)}) %collective-permute-start.8) | collective-permute-done | bytes 131104 | tf_op jit(solution)/shard_map/panel_sum/ppermute | solution.py:26
  120.9 4.7 %collective-permute-start.9 = (bf16[8,16,512]{2,1,0:T(8,128)(2,1)S(1)}, bf16[8,16,512]{2,1,0:T(8,128)(2,1)S(1)}, u32[]{:S(2)}, u32[]{:S(2)}) collective-permute-start(bf16[8,16,512]{2,1,0:T(8,128)(2,1)S(1)} %fusion), channel_id=1, source_target_pairs={{0,8},{2,10},{4,12},{6,14},{8,0},{10,2},{12,4},{14,6},{1,9},{3,11}... | collective-permute-start | bytes 393224 | tf_op jit(solution)/shard_map/panel_sum/ppermute | solution.py:26
  125.6 7.5 %collective-permute-done.9 = bf16[8,16,512]{2,1,0:T(8,128)(2,1)S(1)} collective-permute-done((bf16[8,16,512]{2,1,0:T(8,128)(2,1)S(1)}, bf16[8,16,512]{2,1,0:T(8,128)(2,1)S(1)}, u32[]{:S(2)}, u32[]{:S(2)}) %collective-permute-start.9) | collective-permute-done | bytes 131104 | tf_op jit(solution)/shard_map/panel_sum/ppermute | solution.py:26
  134.2 5.5 %all-to-all-start.2 = ((bf16[8,112,256]{2,1,0:T(8,128)(2,1)}), bf16[8,112,256]{2,1,0:T(8,128)(2,1)S(1)}, u32[]{:S(2)}, u32[]{:S(2)}) async-start(bf16[8,112,256]{2,1,0:T(8,128)(2,1)} %shard_map.59), calls=%async_computation.2 | async-start | bytes 917504 | tf_op jit(solution)/shard_map/rotated_z/all_to_all | solution.py:21
  139.6 3.6 %collective-permute-start.10 = (bf16[8,16,512]{2,1,0:T(8,128)(2,1)S(1)}, bf16[8,16,512]{2,1,0:T(8,128)(2,1)S(1)}, u32[]{:S(2)}, u32[]{:S(2)}) collective-permute-start(bf16[8,16,512]{2,1,0:T(8,128)(2,1)S(1)} %convert_element_type.25), channel_id=1, source_target_pairs={{0,4},{2,6},{4,0},{6,2},{8,12},{10,14},{12,8},{14,10},{1,5},{3,7},... | collective-permute-start | bytes 393224 | tf_op jit(solution)/shard_map/panel_sum/ppermute | solution.py:26
  143.2 5.6 %collective-permute-done.10 = bf16[8,16,512]{2,1,0:T(8,128)(2,1)S(1)} collective-permute-done((bf16[8,16,512]{2,1,0:T(8,128)(2,1)S(1)}, bf16[8,16,512]{2,1,0:T(8,128)(2,1)S(1)}, u32[]{:S(2)}, u32[]{:S(2)}) %collective-permute-start.10) | collective-permute-done | bytes 131104 | tf_op jit(solution)/shard_map/panel_sum/ppermute | solution.py:26
  152.8 2.6 %shard_map.60 = bf16[4,896,128]{2,1,0:T(8,128)(2,1)S(1)} custom-call(s32[2]{0:T(128)S(1)} %pad_add_fusion.at_ref, bf16[896,256]{1,0:T(8,128)(2,1)S(1)} %bitcast.9, bf16[8,16,512]{2,1,0:T(8,128)(2,1)S(1)} %add_convert_fusion.own_ref, bf16[8,16,512]{2,1,0:T(8,128)(2,1)S(1)} %collective-permute-done.11.other_ref), custom_call_target="tpu_custom_call" | custom-call | flops 234881024 | bytes 262144 | tf_op jit(solution)/shard_map/pallas_call | solution.py:205
  155.5 17.2 %all_to_all.20.parts_ref = bf16[4,896,128]{2,1,0:T(8,128)(2,1)S(1)} all-to-all(bf16[4,896,128]{2,1,0:T(8,128)(2,1)S(1)} %shard_map.60), channel_id=1, replica_groups=mesh['z'=8,'x'=4,'y'=8,'c'=2] {'x'}, dimensions={0} | all-to-all | bytes 1835008 | tf_op jit(solution)/shard_map/out_x/all_to_all | solution.py:21
  (30 shorter events, 12.8 us)
Async XLA Ops:
  0.7 15.7 %copy-start.1 = (bf16[512,128]{1,0:T(8,128)(2,1)S(1)}, bf16[512,128]{1,0:T(8,128)(2,1)}, u32[]{:S(2)}) copy-start(bf16[512,128]{1,0:T(8,128)(2,1)} %param.8) | copy-start | bytes 393220
  3.0 43.1 %copy-start = (bf16[896,896]{1,0:T(8,128)(2,1)S(1)}, bf16[896,896]{1,0:T(8,128)(2,1)}, u32[]{:S(2)}) copy-start(bf16[896,896]{1,0:T(8,128)(2,1)} %basis_ref.3) | copy-start | bytes 4816900
  3.0 41.1 %all-to-all-start = ((bf16[32,16,896]{2,1,0:T(8,128)(2,1)}), bf16[32,16,896]{2,1,0:T(8,128)(2,1)S(1)}, u32[]{:S(2)}, u32[]{:S(2)}) async-start(bf16[32,16,896]{2,1,0:T(8,128)(2,1)} %shard_map.55), calls=%async_computation | async-start | bytes 1835008 | tf_op jit(solution)/shard_map/rows_dp/all_to_all | solution.py:21
  16.3 3.2 %collective-permute-start.1 = (bf16[512,128]{1,0:T(8,128)(2,1)S(1)}, bf16[512,128]{1,0:T(8,128)(2,1)S(1)}, u32[]{:S(2)}, u32[]{:S(2)}) collective-permute-start(bf16[512,128]{1,0:T(8,128)(2,1)S(1)} %copy-done.1), channel_id=1, source_target_pairs={{0,1},{1,0},{2,3},{3,2},{4,5},{5,4},{6,7},{7,6},{8,9},{9,8},{10,11... | collective-permute-start | bytes 393224 | tf_op jit(solution)/shard_map/basis_cx/ppermute | solution.py:26
  19.6 24.3 %collective-permute-start.4 = (bf16[2,512,128]{2,1,0:T(8,128)(2,1)S(1)}, bf16[2,512,128]{2,1,0:T(8,128)(2,1)S(1)}, u32[]{:S(2)}, u32[]{:S(2)}) collective-permute-start(bf16[2,512,128]{2,1,0:T(8,128)(2,1)S(1)} %pad_maximum_fusion.refs_0_), channel_id=1, source_target_pairs={{0,48},{16,32},{32,16},{48,0},{1,49},{17,33},{33,17},{49,1},{2,50}... | collective-permute-start | bytes 786440 | tf_op jit(solution)/shard_map/basis_cx/ppermute | solution.py:26
  24.5 19.4 %collective-permute-start.3 = (bf16[2,512,128]{2,1,0:T(8,128)(2,1)S(1)}, bf16[2,512,128]{2,1,0:T(8,128)(2,1)S(1)}, u32[]{:S(2)}, u32[]{:S(2)}) collective-permute-start(bf16[2,512,128]{2,1,0:T(8,128)(2,1)S(1)} %pad_maximum_fusion.refs_0_), channel_id=1, source_target_pairs={{0,32},{16,48},{32,0},{48,16},{1,33},{17,49},{33,1},{49,17},{2,34}... | collective-permute-start | bytes 786440 | tf_op jit(solution)/shard_map/basis_cx/ppermute | solution.py:26
  27.3 16.8 %collective-permute-start.2 = (bf16[2,512,128]{2,1,0:T(8,128)(2,1)S(1)}, bf16[2,512,128]{2,1,0:T(8,128)(2,1)}, u32[]{:S(2)}, u32[]{:S(2)}) collective-permute-start(bf16[2,512,128]{2,1,0:T(8,128)(2,1)S(1)} %pad_maximum_fusion.refs_0_), channel_id=1, source_target_pairs={{0,16},{16,0},{32,48},{48,32},{1,17},{17,1},{33,49},{49,33},{2,18}... | collective-permute-start | bytes 786440 | tf_op jit(solution)/shard_map/basis_cx/ppermute | solution.py:26
  30.2 12.8 %collective-permute-start = (bf16[1,16,1024]{2,1,0:T(8,128)(2,1)S(1)}, bf16[1,16,1024]{2,1,0:T(8,128)(2,1)S(1)}, u32[]{:S(2)}, u32[]{:S(2)}) collective-permute-start(bf16[1,16,1024]{2,1,0:T(8,128)(2,1)S(1)} %maximum_bitcast_fusion), channel_id=1, source_target_pairs={{0,256},{64,320},{128,384},{192,448},{256,0},{320,64},{384,128},{4... | collective-permute-start | bytes 98312 | tf_op jit(solution)/shard_map/slab_z/ppermute | solution.py:26
  44.1 4.4 %collective-permute-start.5 = (bf16[32,16,896]{2,1,0:T(8,128)(2,1)S(1)}, bf16[32,16,896]{2,1,0:T(8,128)(2,1)S(1)}, u32[]{:S(2)}, u32[]{:S(2)}) collective-permute-start(bf16[32,16,896]{2,1,0:T(8,128)(2,1)S(1)} %all-to-all-done.tokens_ref), channel_id=1, source_target_pairs={{0,1},{1,0},{2,3},{3,2},{4,5},{5,4},{6,7},{7,6},{8,9},{9,8},{10,11... | collective-permute-start | bytes 2752520 | tf_op jit(solution)/shard_map/rows_c/ppermute | solution.py:26
  50.8 82.3 %all-to-all-start.1 = ((bf16[32,112,256]{2,1,0:T(8,128)(2,1)}), bf16[32,112,256]{2,1,0:T(8,128)(2,1)S(1)}, u32[]{:S(2)}, u32[]{:S(2)}) async-start(bf16[32,112,256]{2,1,0:T(8,128)(2,1)} %bitcast.5), calls=%async_computation.1 | async-start | bytes 3670016 | tf_op jit(solution)/shard_map/sum_xz/all_to_all | solution.py:21
  59.9 45.7 %collective-permute-start.6 = (bf16[2,16,1024]{2,1,0:T(8,128)(2,1)S(1)}, bf16[2,16,1024]{2,1,0:T(8,128)(2,1)S(1)}, u32[]{:S(2)}, u32[]{:S(2)}) collective-permute-start(bf16[2,16,1024]{2,1,0:T(8,128)(2,1)S(1)} %pad_maximum_fusion.3), channel_id=1, source_target_pairs={{0,128},{64,192},{128,0},{192,64},{256,384},{320,448},{384,256},{4... | collective-permute-start | bytes 196616 | tf_op jit(solution)/shard_map/slab_z/ppermute | solution.py:26
  105.7 6.9 %collective-permute-start.7 = (bf16[4,16,1024]{2,1,0:T(8,128)(2,1)S(1)}, bf16[4,16,1024]{2,1,0:T(8,128)(2,1)S(1)}, u32[]{:S(2)}, u32[]{:S(2)}) collective-permute-start(bf16[4,16,1024]{2,1,0:T(8,128)(2,1)S(1)} %pad_maximum_fusion.2), channel_id=1, source_target_pairs={{0,64},{64,0},{128,192},{192,128},{256,320},{320,256},{384,448},{4... | collective-permute-start | bytes 393224 | tf_op jit(solution)/shard_map/slab_z/ppermute | solution.py:26
  114.0 6.9 %collective-permute-start.8 = (bf16[8,16,512]{2,1,0:T(8,128)(2,1)S(1)}, bf16[8,16,512]{2,1,0:T(8,128)(2,1)S(1)}, u32[]{:S(2)}, u32[]{:S(2)}) collective-permute-start(bf16[8,16,512]{2,1,0:T(8,128)(2,1)S(1)} %convert_element_type.21), channel_id=1, source_target_pairs={{0,2},{2,0},{4,6},{6,4},{8,10},{10,8},{12,14},{14,12},{1,3},{3,1},... | collective-permute-start | bytes 393224 | tf_op jit(solution)/shard_map/panel_sum/ppermute | solution.py:26
  120.9 12.2 %collective-permute-start.9 = (bf16[8,16,512]{2,1,0:T(8,128)(2,1)S(1)}, bf16[8,16,512]{2,1,0:T(8,128)(2,1)S(1)}, u32[]{:S(2)}, u32[]{:S(2)}) collective-permute-start(bf16[8,16,512]{2,1,0:T(8,128)(2,1)S(1)} %fusion), channel_id=1, source_target_pairs={{0,8},{2,10},{4,12},{6,14},{8,0},{10,2},{12,4},{14,6},{1,9},{3,11}... | collective-permute-start | bytes 393224 | tf_op jit(solution)/shard_map/panel_sum/ppermute | solution.py:26
  134.2 18.7 %all-to-all-start.2 = ((bf16[8,112,256]{2,1,0:T(8,128)(2,1)}), bf16[8,112,256]{2,1,0:T(8,128)(2,1)S(1)}, u32[]{:S(2)}, u32[]{:S(2)}) async-start(bf16[8,112,256]{2,1,0:T(8,128)(2,1)} %shard_map.59), calls=%async_computation.2 | async-start | bytes 917504 | tf_op jit(solution)/shard_map/rotated_z/all_to_all | solution.py:21
  139.6 9.2 %collective-permute-start.10 = (bf16[8,16,512]{2,1,0:T(8,128)(2,1)S(1)}, bf16[8,16,512]{2,1,0:T(8,128)(2,1)S(1)}, u32[]{:S(2)}, u32[]{:S(2)}) collective-permute-start(bf16[8,16,512]{2,1,0:T(8,128)(2,1)S(1)} %convert_element_type.25), channel_id=1, source_target_pairs={{0,4},{2,6},{4,0},{6,2},{8,12},{10,14},{12,8},{14,10},{1,5},{3,7},... | collective-permute-start | bytes 393224 | tf_op jit(solution)/shard_map/panel_sum/ppermute | solution.py:26
  148.8 3.2 %collective-permute-start.11 = (bf16[8,16,512]{2,1,0:T(8,128)(2,1)S(1)}, bf16[8,16,512]{2,1,0:T(8,128)(2,1)S(1)}, u32[]{:S(2)}, u32[]{:S(2)}) collective-permute-start(bf16[8,16,512]{2,1,0:T(8,128)(2,1)S(1)} %add_convert_fusion.own_ref), channel_id=1, source_target_pairs={{0,1},{1,0},{2,3},{3,2},{4,5},{5,4},{6,7},{7,6},{8,9},{9,8},{10,11... | collective-permute-start | bytes 393224 | tf_op jit(solution)/shard_map/panel_c/ppermute | solution.py:26

commit v9 on v8

--- a/solution.py
+++ b/solution.py
@@ -33,15 +33,15 @@
     return result
 
 
-def add_from(block, axis, bit):
-    return block + swap(block.astype(BF), axis, bit).astype(F32)
+def add_from(block, axis, bit, kind=F32):
+    return block + swap(block.astype(kind), axis, bit).astype(F32)
 
 
 def cost(flops, moved):
     return pl.CostEstimate(flops=flops, bytes_accessed=moved, transcendentals=0)
 
 
-def split_kernel(length_ref, grads_ref, out_ref, held, sems):
+def split_kernel(length_ref, grads_ref, out_ref, held, ready, sems, out_sems):
     parts, half, wide = out_ref.shape
     steps, _, chunk = held.shape
     each = parts // steps
@@ -49,6 +49,12 @@
     copies = [
         pltpu.make_async_copy(
             grads_ref.at[pl.ds(first, half), pl.ds(k * chunk, chunk)], held.at[k], sems.at[k]
+        )
+        for k in range(steps)
+    ]
+    stores = [
+        pltpu.make_async_copy(
+            ready.at[k], out_ref.at[pl.ds(k * each, each)], out_sems.at[k]
         )
         for k in range(steps)
     ]
@@ -60,7 +66,10 @@
         copies[k].wait()
         for q in range(each):
             piece = held[k, :, q * wide : (q + 1) * wide]
-            out_ref[k * each + q] = jnp.where(live, piece, jnp.zeros_like(piece))
+            ready[k, q] = jnp.where(live, piece, jnp.zeros_like(piece))
+        stores[k].start()
+    for store in stores:
+        store.wait()
 
 
 def split_rows(grads, length, half, parts, steps=4):
@@ -69,9 +78,11 @@
         split_kernel,
         out_shape=jax.ShapeDtypeStruct((parts, half, wide), grads.dtype),
         in_specs=[pl.BlockSpec(memory_space=SMEM), pl.BlockSpec(memory_space=pl.ANY)],
-        out_specs=pl.BlockSpec(memory_space=VMEM),
+        out_specs=pl.BlockSpec(memory_space=pl.ANY),
         scratch_shapes=[
             VMEM((steps, half, grads.shape[1] // steps), grads.dtype),
+            VMEM((steps, parts // steps, half, wide), grads.dtype),
+            pltpu.SemaphoreType.DMA((steps,)),
             pltpu.SemaphoreType.DMA((steps,)),
         ],
         compiler_params=pltpu.CompilerParams(vmem_limit_bytes=58 * MIB),
@@ -149,31 +160,29 @@
     )(parts)
 
 
-def panel_kernel(at_ref, slab_ref, *refs):
-    *basis_refs, out_ref = refs
+def panel_kernel(at_ref, slab_ref, other_ref, *refs):
+    *own_refs, out_ref = refs
     count, slots, _ = out_ref.shape
-    cores, deep, lanes = basis_refs[0].shape
-    for k, basis_ref in enumerate(basis_refs):
-        total = jnp.zeros((count * slots, lanes), F32)
-        for r in range(cores):
-            left = slab_ref[:, r * deep : (r + 1) * deep]
-            total = total + jnp.dot(left, basis_ref[r], preferred_element_type=F32)
+    deep, lanes = own_refs[0].shape
+    for k, own_ref in enumerate(own_refs):
+        total = jnp.dot(slab_ref[:, :deep], own_ref[...], preferred_element_type=F32)
+        total = total + jnp.dot(slab_ref[:, deep:], other_ref[k], preferred_element_type=F32)
         start = pl.multiple_of((k ^ at_ref[0]) * lanes, lanes)
         out_ref[:, :, pl.ds(start, lanes)] = total.reshape(count, slots, lanes)
 
 
-def panel_part(at, slab, bases):
+def panel_part(at, slab, other, own):
     count, slots, deep = slab.shape
-    columns = len(bases) * bases[0].shape[2]
+    columns = len(own) * own[0].shape[1]
     return pl.pallas_call(
         panel_kernel,
         out_shape=jax.ShapeDtypeStruct((count, slots, columns), F32),
         in_specs=[pl.BlockSpec(memory_space=SMEM)]
-        + [pl.BlockSpec(memory_space=VMEM)] * (1 + len(bases)),
+        + [pl.BlockSpec(memory_space=VMEM)] * (2 + len(own)),
         out_specs=pl.BlockSpec(memory_space=VMEM),
         compiler_params=PARAMS,
-        cost_estimate=cost(2 * count * slots * columns * deep, 8 * bases[0].size),
-    )(at, slab.reshape(count * slots, deep), *bases)
+        cost_estimate=cost(2 * count * slots * columns * deep, 4 * other.size),
+    )(at, slab.reshape(count * slots, deep), other, *own)
 
 
 def example_kernel(at_ref, left_ref, own_ref, other_ref, out_ref):
@@ -233,28 +242,31 @@
     slab = jnp.concatenate([features(0), features(1)], axis=1)[None]
     with jax.named_scope("slab_z"):
         more_slab = swap(slab, "z", 4)
-    with jax.named_scope("basis_cx"):
-        pair = jnp.stack([basis_in, swap(basis_in, "c", 1)])
-        basis_x = [pair] + [swap(pair, "x", k) for k in range(1, nx)]
+    with jax.named_scope("basis_x"):
+        basis_x = [basis_in] + [swap(basis_in, "x", k) for k in range(1, nx)]
     own, more_slab, *basis_x = tie((own, more_slab, *basis_x))
     with jax.named_scope("rows_c"):
         other = swap(own, "c", 1)
     parts = rotate(own, basis_out, 0, nx)
     slab = jnp.concatenate([slab, more_slab], axis=0)
     parts = rotate(other, basis_out, 1, nx, parts)
-    parts, slab = tie((parts, slab))
-    with jax.named_scope("sum_xz"):
-        parts = exchange(parts.reshape(nx * nz, columns // nz, parts.shape[2]), ("x", "z"))
+    parts, slab, *basis_x = tie((parts, slab, *basis_x))
+    with jax.named_scope("sum_x"):
+        parts = exchange(parts, "x")
 
     with jax.named_scope("slab_z"):
         slab = jnp.concatenate([slab, swap(slab, "z", 2)], axis=0)
         slab = jnp.concatenate([slab, swap(slab, "z", 1)], axis=0)
-    piece = panel_part(at, slab, basis_x)
+    with jax.named_scope("basis_c"):
+        other_basis = swap(jnp.stack(basis_x), "c", 1)
+    piece = panel_part(at, slab, other_basis, basis_x)
+    parts, piece = tie((parts, piece))
+    parts = sum_parts(parts, steps=2).reshape(nz, columns // nz, parts.shape[2])
+    with jax.named_scope("sum_z"):
+        parts = exchange(parts, "z")
     with jax.named_scope("panel_sum"):
-        piece = add_from(piece, "y", 1)
+        piece = add_from(piece, "y", 1, BF)
         piece = add_from(piece, "y", 4)
-    parts, piece = tie((parts, piece))
-    with jax.named_scope("panel_sum"):
         piece = add_from(piece, "y", 2).astype(BF)
     with jax.named_scope("panel_c"):
         piece_other = swap(piece, "c", 1)

time: 174 us -> 147 us (0.84)
  waiting for transfers between devices: 72.3 us -> 48 us
  starting transfers between devices: 69.2 us -> 65.7 us
    ppermute x12, waiting for transfers between devices: 71.6 us -> 39.6 us  [swap(): return lax.ppermute(block, axis, [(i, i ^ bit) for i in range(count)])]
    all_to_all x3 -> x4, waiting for transfers between devices: 0.75 us -> 8.46 us  [exchange(): return lax.all_to_all(blocks, axis, split_axis=0, concat_axis=0, tiled=True)]
    all_to_all x3 -> x4, starting transfers between devices: 27.9 us -> 25.1 us  [exchange(): return lax.all_to_all(blocks, axis, split_axis=0, concat_axis=0, tiled=True)]
  transfers between devices with their start and end apart: 15 -> 16, of which waited for: 12 -> 10; matrix products, arithmetic and copies ran while one was open for 1% -> 1% of each run, Pallas kernels for 2% -> 3%
where the time goes in v9:
time: 147 us
  starting transfers between devices  65.7 us (45%)
  waiting for transfers between devices  48 us (33%)
  blocking collectives  16.7 us (11%)
  Pallas kernels  13.3 us (9%)
    ppermute x12, starting transfers between devices, swap(): return lax.ppermute(block, axis, [(i, i ^ bit) for i in range(count)])  40.6 us
    ppermute x12, waiting for transfers between devices, swap(): return lax.ppermute(block, axis, [(i, i ^ bit) for i in range(count)])  39.6 us
    all_to_all x4, starting transfers between devices, exchange(): return lax.all_to_all(blocks, axis, split_axis=0, concat_axis=0, tiled=True)  25.1 us
    all_to_all x1, blocking collectives, exchange(): return lax.all_to_all(blocks, axis, split_axis=0, concat_axis=0, tiled=True)  16.7 us
    all_to_all x4, waiting for transfers between devices, exchange(): return lax.all_to_all(blocks, axis, split_axis=0, concat_axis=0, tiled=True)  8.46 us
    pallas_call x2, Pallas kernels, rotate(): pl.pallas_call(rotate_kernel, out_shape=jax.ShapeDtypeStruct((pieces, col...  4.7 us
  transfers between devices with their start and end apart: 16, of which 10 were waited for; matrix products, arithmetic and copies ran while one was open for 1% of the time, Pallas kernels for 3%

profile of v9, /device:TPU:56, one launch (start us, length us, event | category | flops | bytes accessed | tf_op | source)
XLA Modules:
  0.0 146.5 jit_solution(11643712916887780231)
XLA Ops:
  2.9 13.2 %all-to-all-start = ((bf16[32,16,896]{2,1,0:T(8,128)(2,1)}), bf16[32,16,896]{2,1,0:T(8,128)(2,1)S(1)}, u32[]{:S(2)}, u32[]{:S(2)}) async-start(bf16[32,16,896]{2,1,0:T(8,128)(2,1)} %shard_map.55), calls=%async_computation | async-start | bytes 1835008 | tf_op jit(solution)/shard_map/rows_dp/all_to_all | solution.py:21
  16.1 5.2 %collective-permute-start.2 = (bf16[512,128]{1,0:T(8,128)(2,1)S(1)}, bf16[512,128]{1,0:T(8,128)(2,1)S(1)}, u32[]{:S(2)}, u32[]{:S(2)}) collective-permute-start(bf16[512,128]{1,0:T(8,128)(2,1)S(1)} %copy-done.1), channel_id=1, source_target_pairs={{0,32},{16,48},{32,0},{48,16},{1,33},{17,49},{33,1},{49,17},{2,34}... | collective-permute-start | bytes 393224 | tf_op jit(solution)/shard_map/basis_x/ppermute | solution.py:26
  21.3 2.5 %collective-permute-start.1 = (bf16[512,128]{1,0:T(8,128)(2,1)S(1)}, bf16[512,128]{1,0:T(8,128)(2,1)S(1)}, u32[]{:S(2)}, u32[]{:S(2)}) collective-permute-start(bf16[512,128]{1,0:T(8,128)(2,1)S(1)} %copy-done.1), channel_id=1, source_target_pairs={{0,16},{16,0},{32,48},{48,32},{1,17},{17,1},{33,49},{49,33},{2,18}... | collective-permute-start | bytes 393224 | tf_op jit(solution)/shard_map/basis_x/ppermute | solution.py:26
  23.8 2.5 %collective-permute-start.3 = (bf16[512,128]{1,0:T(8,128)(2,1)S(1)}, bf16[512,128]{1,0:T(8,128)(2,1)S(1)}, u32[]{:S(2)}, u32[]{:S(2)}) collective-permute-start(bf16[512,128]{1,0:T(8,128)(2,1)S(1)} %copy-done.1), channel_id=1, source_target_pairs={{0,48},{16,32},{32,16},{48,0},{1,49},{17,33},{33,17},{49,1},{2,50}... | collective-permute-start | bytes 393224 | tf_op jit(solution)/shard_map/basis_x/ppermute | solution.py:26
  27.1 7.3 %collective-permute-start = (bf16[1,16,1024]{2,1,0:T(8,128)(2,1)S(1)}, bf16[1,16,1024]{2,1,0:T(8,128)(2,1)S(1)}, u32[]{:S(2)}, u32[]{:S(2)}) collective-permute-start(bf16[1,16,1024]{2,1,0:T(8,128)(2,1)S(1)} %maximum_bitcast_fusion), channel_id=1, source_target_pairs={{0,256},{64,320},{128,384},{192,448},{256,0},{320,64},{384,128},{4... | collective-permute-start | bytes 98312 | tf_op jit(solution)/shard_map/slab_z/ppermute | solution.py:26
  34.3 8.0 %collective-permute-done = bf16[1,16,1024]{2,1,0:T(8,128)(2,1)S(1)} collective-permute-done((bf16[1,16,1024]{2,1,0:T(8,128)(2,1)S(1)}, bf16[1,16,1024]{2,1,0:T(8,128)(2,1)S(1)}, u32[]{:S(2)}, u32[]{:S(2)}) %collective-permute-start) | collective-permute-done | bytes 32800 | tf_op jit(solution)/shard_map/slab_z/ppermute | solution.py:26
  44.3 2.4 %shard_map.56.rest_0_ = bf16[4,896,256]{2,1,0:T(8,128)(2,1)} custom-call(bf16[32,16,896]{2,1,0:T(8,128)(2,1)S(1)} %all-to-all-done.tokens_ref, bf16[896,896]{1,0:T(8,128)(2,1)S(1)} %copy-done), custom_call_target="tpu_custom_call" | custom-call | flops 822083584 | bytes 1835008 | tf_op jit(solution)/shard_map/pallas_call | solution.py:118
  46.7 2.4 %shard_map.57 = bf16[4,896,256]{2,1,0:T(8,128)(2,1)} custom-call(bf16[32,16,896]{2,1,0:T(8,128)(2,1)S(1)} %collective-permute-done.4.tokens_ref, bf16[896,896]{1,0:T(8,128)(2,1)S(1)} %copy-done, bf16[4,896,256]{2,1,0:T(8,128)(2,1)} %shard_map.56.rest_0_), custom_call_target="tpu_custom_call", output_to_operand_aliasing={{}: (2, {})} | custom-call | flops 822083584 | bytes 1835008 | tf_op jit(solution)/shard_map/pallas_call | solution.py:118
  49.1 4.9 %all-to-all-start.1 = ((bf16[4,896,256]{2,1,0:T(8,128)(2,1)}), bf16[4,896,256]{2,1,0:T(8,128)(2,1)S(1)}, u32[]{:S(2)}, u32[]{:S(2)}) async-start(bf16[4,896,256]{2,1,0:T(8,128)(2,1)} %shard_map.57), calls=%async_computation.1 | async-start | bytes 3670016 | tf_op jit(solution)/shard_map/sum_x/all_to_all | solution.py:21
  57.0 3.6 %collective-permute-start.5 = (bf16[2,16,1024]{2,1,0:T(8,128)(2,1)S(1)}, bf16[2,16,1024]{2,1,0:T(8,128)(2,1)S(1)}, u32[]{:S(2)}, u32[]{:S(2)}) collective-permute-start(bf16[2,16,1024]{2,1,0:T(8,128)(2,1)S(1)} %pad_maximum_fusion.3), channel_id=1, source_target_pairs={{0,128},{64,192},{128,0},{192,64},{256,384},{320,448},{384,256},{4... | collective-permute-start | bytes 196616 | tf_op jit(solution)/shard_map/slab_z/ppermute | solution.py:26
  60.5 5.0 %collective-permute-done.5 = bf16[2,16,1024]{2,1,0:T(8,128)(2,1)S(1)} collective-permute-done((bf16[2,16,1024]{2,1,0:T(8,128)(2,1)S(1)}, bf16[2,16,1024]{2,1,0:T(8,128)(2,1)S(1)}, u32[]{:S(2)}, u32[]{:S(2)}) %collective-permute-start.5) | collective-permute-done | bytes 65568 | tf_op jit(solution)/shard_map/slab_z/ppermute | solution.py:26
  67.5 5.3 %collective-permute-done.6 = bf16[4,16,1024]{2,1,0:T(8,128)(2,1)S(1)} collective-permute-done((bf16[4,16,1024]{2,1,0:T(8,128)(2,1)S(1)}, bf16[4,16,1024]{2,1,0:T(8,128)(2,1)S(1)}, u32[]{:S(2)}, u32[]{:S(2)}) %collective-permute-start.6) | collective-permute-done | bytes 131104 | tf_op jit(solution)/shard_map/slab_z/ppermute | solution.py:26
  73.8 4.3 %all-to-all-done.1.parts_ref = bf16[4,896,256]{2,1,0:T(8,128)(2,1)S(1)} async-done(((bf16[4,896,256]{2,1,0:T(8,128)(2,1)}), bf16[4,896,256]{2,1,0:T(8,128)(2,1)S(1)}, u32[]{:S(2)}, u32[]{:S(2)}) %all-to-all-start.1) | async-done | bytes 1835040 | tf_op jit(solution)/shard_map/sum_x/all_to_all | solution.py:21
  79.2 3.5 %all-to-all-start.2 = ((bf16[8,112,256]{2,1,0:T(8,128)(2,1)}), bf16[8,112,256]{2,1,0:T(8,128)(2,1)S(1)}, u32[]{:S(2)}, u32[]{:S(2)}) async-start(bf16[8,112,256]{2,1,0:T(8,128)(2,1)} %bitcast.8), calls=%async_computation.2 | async-start | bytes 917504 | tf_op jit(solution)/shard_map/sum_z/all_to_all | solution.py:21
  82.7 3.3 %collective-permute-start.8 = (bf16[8,16,512]{2,1,0:T(8,128)(2,1)S(1)}, bf16[8,16,512]{2,1,0:T(8,128)(2,1)S(1)}, u32[]{:S(2)}, u32[]{:S(2)}) collective-permute-start(bf16[8,16,512]{2,1,0:T(8,128)(2,1)S(1)} %convert_element_type.9), channel_id=1, source_target_pairs={{0,2},{2,0},{4,6},{6,4},{8,10},{10,8},{12,14},{14,12},{1,3},{3,1},... | collective-permute-start | bytes 393224 | tf_op jit(solution)/shard_map/panel_sum/ppermute | solution.py:26
  86.0 3.6 %collective-permute-done.8 = bf16[8,16,512]{2,1,0:T(8,128)(2,1)S(1)} collective-permute-done((bf16[8,16,512]{2,1,0:T(8,128)(2,1)S(1)}, bf16[8,16,512]{2,1,0:T(8,128)(2,1)S(1)}, u32[]{:S(2)}, u32[]{:S(2)}) %collective-permute-start.8) | collective-permute-done | bytes 131104 | tf_op jit(solution)/shard_map/panel_sum/ppermute | solution.py:26
  89.6 4.7 %collective-permute-start.9 = (f32[8,16,512]{2,1,0:T(8,128)S(1)}, f32[8,16,512]{2,1,0:T(8,128)S(1)}, u32[]{:S(2)}, u32[]{:S(2)}) collective-permute-start(f32[8,16,512]{2,1,0:T(8,128)S(1)} %convert_add_fusion), channel_id=1, source_target_pairs={{0,8},{2,10},{4,12},{6,14},{8,0},{10,2},{12,4},{14,6},{1,9},{3,11}... | collective-permute-start | bytes 786440 | tf_op jit(solution)/shard_map/panel_sum/ppermute | solution.py:26
  94.4 4.1 %all-to-all-done.2.parts_ref = bf16[8,112,256]{2,1,0:T(8,128)(2,1)S(1)} async-done(((bf16[8,112,256]{2,1,0:T(8,128)(2,1)}), bf16[8,112,256]{2,1,0:T(8,128)(2,1)S(1)}, u32[]{:S(2)}, u32[]{:S(2)}) %all-to-all-start.2) | async-done | bytes 458784 | tf_op jit(solution)/shard_map/sum_z/all_to_all | solution.py:21
  99.3 3.5 %all-to-all-start.3 = ((bf16[8,112,256]{2,1,0:T(8,128)(2,1)}), bf16[8,112,256]{2,1,0:T(8,128)(2,1)S(1)}, u32[]{:S(2)}, u32[]{:S(2)}) async-start(bf16[8,112,256]{2,1,0:T(8,128)(2,1)} %shard_map.60), calls=%async_computation.3 | async-start | bytes 917504 | tf_op jit(solution)/shard_map/rotated_z/all_to_all | solution.py:21
  102.8 5.0 %collective-permute-done.9 = f32[8,16,512]{2,1,0:T(8,128)S(1)} collective-permute-done((f32[8,16,512]{2,1,0:T(8,128)S(1)}, f32[8,16,512]{2,1,0:T(8,128)S(1)}, u32[]{:S(2)}, u32[]{:S(2)}) %collective-permute-start.9) | collective-permute-done | bytes 262176 | tf_op jit(solution)/shard_map/panel_sum/ppermute | solution.py:26
  107.8 3.8 %collective-permute-start.10 = (f32[8,16,512]{2,1,0:T(8,128)S(1)}, f32[8,16,512]{2,1,0:T(8,128)S(1)}, u32[]{:S(2)}, u32[]{:S(2)}) collective-permute-start(f32[8,16,512]{2,1,0:T(8,128)S(1)} %add.31), channel_id=1, source_target_pairs={{0,4},{2,6},{4,0},{6,2},{8,12},{10,14},{12,8},{14,10},{1,5},{3,7},... | collective-permute-start | bytes 786440 | tf_op jit(solution)/shard_map/panel_sum/ppermute | solution.py:26
  111.6 11.3 %collective-permute-done.10 = f32[8,16,512]{2,1,0:T(8,128)S(1)} collective-permute-done((f32[8,16,512]{2,1,0:T(8,128)S(1)}, f32[8,16,512]{2,1,0:T(8,128)S(1)}, u32[]{:S(2)}, u32[]{:S(2)}) %collective-permute-start.10) | collective-permute-done | bytes 262176 | tf_op jit(solution)/shard_map/panel_sum/ppermute | solution.py:26
  126.3 2.7 %shard_map.61 = bf16[4,896,128]{2,1,0:T(8,128)(2,1)S(1)} custom-call(s32[2]{0:T(128)S(1)} %pad_add_fusion.at_ref, bf16[896,256]{1,0:T(8,128)(2,1)S(1)} %bitcast.11, bf16[8,16,512]{2,1,0:T(8,128)(2,1)S(1)} %add_convert_fusion.own_ref, bf16[8,16,512]{2,1,0:T(8,128)(2,1)S(1)} %collective-permute-done.11.other_ref), custom_call_target="tpu_custom_call" | custom-call | flops 234881024 | bytes 262144 | tf_op jit(solution)/shard_map/pallas_call | solution.py:214
  128.9 16.7 %all_to_all.25.parts_ref = bf16[4,896,128]{2,1,0:T(8,128)(2,1)S(1)} all-to-all(bf16[4,896,128]{2,1,0:T(8,128)(2,1)S(1)} %shard_map.61), channel_id=1, replica_groups=mesh['z'=8,'x'=4,'y'=8,'c'=2] {'x'}, dimensions={0} | all-to-all | bytes 1835008 | tf_op jit(solution)/shard_map/out_x/all_to_all | solution.py:21
  (32 shorter events, 17.0 us)
Async XLA Ops:
  0.7 15.4 %copy-start.1 = (bf16[512,128]{1,0:T(8,128)(2,1)S(1)}, bf16[512,128]{1,0:T(8,128)(2,1)}, u32[]{:S(2)}) copy-start(bf16[512,128]{1,0:T(8,128)(2,1)} %refs_0_) | copy-start | bytes 393220
  0.7 43.6 %copy-start = (bf16[896,896]{1,0:T(8,128)(2,1)S(1)}, bf16[896,896]{1,0:T(8,128)(2,1)}, u32[]{:S(2)}) copy-start(bf16[896,896]{1,0:T(8,128)(2,1)} %basis_ref.3) | copy-start | bytes 4816900
  2.9 39.5 %all-to-all-start = ((bf16[32,16,896]{2,1,0:T(8,128)(2,1)}), bf16[32,16,896]{2,1,0:T(8,128)(2,1)S(1)}, u32[]{:S(2)}, u32[]{:S(2)}) async-start(bf16[32,16,896]{2,1,0:T(8,128)(2,1)} %shard_map.55), calls=%async_computation | async-start | bytes 1835008 | tf_op jit(solution)/shard_map/rows_dp/all_to_all | solution.py:21
  16.1 26.3 %collective-permute-start.2 = (bf16[512,128]{1,0:T(8,128)(2,1)S(1)}, bf16[512,128]{1,0:T(8,128)(2,1)S(1)}, u32[]{:S(2)}, u32[]{:S(2)}) collective-permute-start(bf16[512,128]{1,0:T(8,128)(2,1)S(1)} %copy-done.1), channel_id=1, source_target_pairs={{0,32},{16,48},{32,0},{48,16},{1,33},{17,49},{33,1},{49,17},{2,34}... | collective-permute-start | bytes 393224 | tf_op jit(solution)/shard_map/basis_x/ppermute | solution.py:26
  21.3 21.1 %collective-permute-start.1 = (bf16[512,128]{1,0:T(8,128)(2,1)S(1)}, bf16[512,128]{1,0:T(8,128)(2,1)S(1)}, u32[]{:S(2)}, u32[]{:S(2)}) collective-permute-start(bf16[512,128]{1,0:T(8,128)(2,1)S(1)} %copy-done.1), channel_id=1, source_target_pairs={{0,16},{16,0},{32,48},{48,32},{1,17},{17,1},{33,49},{49,33},{2,18}... | collective-permute-start | bytes 393224 | tf_op jit(solution)/shard_map/basis_x/ppermute | solution.py:26
  23.8 18.6 %collective-permute-start.3 = (bf16[512,128]{1,0:T(8,128)(2,1)S(1)}, bf16[512,128]{1,0:T(8,128)(2,1)S(1)}, u32[]{:S(2)}, u32[]{:S(2)}) collective-permute-start(bf16[512,128]{1,0:T(8,128)(2,1)S(1)} %copy-done.1), channel_id=1, source_target_pairs={{0,48},{16,32},{32,16},{48,0},{1,49},{17,33},{33,17},{49,1},{2,50}... | collective-permute-start | bytes 393224 | tf_op jit(solution)/shard_map/basis_x/ppermute | solution.py:26
  27.1 15.3 %collective-permute-start = (bf16[1,16,1024]{2,1,0:T(8,128)(2,1)S(1)}, bf16[1,16,1024]{2,1,0:T(8,128)(2,1)S(1)}, u32[]{:S(2)}, u32[]{:S(2)}) collective-permute-start(bf16[1,16,1024]{2,1,0:T(8,128)(2,1)S(1)} %maximum_bitcast_fusion), channel_id=1, source_target_pairs={{0,256},{64,320},{128,384},{192,448},{256,0},{320,64},{384,128},{4... | collective-permute-start | bytes 98312 | tf_op jit(solution)/shard_map/slab_z/ppermute | solution.py:26
  42.4 4.4 %collective-permute-start.4 = (bf16[32,16,896]{2,1,0:T(8,128)(2,1)S(1)}, bf16[32,16,896]{2,1,0:T(8,128)(2,1)S(1)}, u32[]{:S(2)}, u32[]{:S(2)}) collective-permute-start(bf16[32,16,896]{2,1,0:T(8,128)(2,1)S(1)} %all-to-all-done.tokens_ref), channel_id=1, source_target_pairs={{0,1},{1,0},{2,3},{3,2},{4,5},{5,4},{6,7},{7,6},{8,9},{9,8},{10,11... | collective-permute-start | bytes 2752520 | tf_op jit(solution)/shard_map/rows_c/ppermute | solution.py:26
  49.1 29.1 %all-to-all-start.1 = ((bf16[4,896,256]{2,1,0:T(8,128)(2,1)}), bf16[4,896,256]{2,1,0:T(8,128)(2,1)S(1)}, u32[]{:S(2)}, u32[]{:S(2)}) async-start(bf16[4,896,256]{2,1,0:T(8,128)(2,1)} %shard_map.57), calls=%async_computation.1 | async-start | bytes 3670016 | tf_op jit(solution)/shard_map/sum_x/all_to_all | solution.py:21
  54.9 17.9 %collective-permute-start.7 = (bf16[4,512,128]{2,1,0:T(8,128)(2,1)}, bf16[4,512,128]{2,1,0:T(8,128)(2,1)S(1)}, u32[]{:S(2)}, u32[]{:S(2)}) collective-permute-start(bf16[4,512,128]{2,1,0:T(8,128)(2,1)} %pad_maximum_fusion), channel_id=1, source_target_pairs={{0,1},{1,0},{2,3},{3,2},{4,5},{5,4},{6,7},{7,6},{8,9},{9,8},{10,11... | collective-permute-start | bytes 1572872 | tf_op jit(solution)/shard_map/basis_c/ppermute | solution.py:26
  57.0 8.5 %collective-permute-start.5 = (bf16[2,16,1024]{2,1,0:T(8,128)(2,1)S(1)}, bf16[2,16,1024]{2,1,0:T(8,128)(2,1)S(1)}, u32[]{:S(2)}, u32[]{:S(2)}) collective-permute-start(bf16[2,16,1024]{2,1,0:T(8,128)(2,1)S(1)} %pad_maximum_fusion.3), channel_id=1, source_target_pairs={{0,128},{64,192},{128,0},{192,64},{256,384},{320,448},{384,256},{4... | collective-permute-start | bytes 196616 | tf_op jit(solution)/shard_map/slab_z/ppermute | solution.py:26
  65.5 7.3 %collective-permute-start.6 = (bf16[4,16,1024]{2,1,0:T(8,128)(2,1)S(1)}, bf16[4,16,1024]{2,1,0:T(8,128)(2,1)S(1)}, u32[]{:S(2)}, u32[]{:S(2)}) collective-permute-start(bf16[4,16,1024]{2,1,0:T(8,128)(2,1)S(1)} %pad_maximum_fusion.2), channel_id=1, source_target_pairs={{0,64},{64,0},{128,192},{192,128},{256,320},{320,256},{384,448},{4... | collective-permute-start | bytes 393224 | tf_op jit(solution)/shard_map/slab_z/ppermute | solution.py:26
  79.2 19.3 %all-to-all-start.2 = ((bf16[8,112,256]{2,1,0:T(8,128)(2,1)}), bf16[8,112,256]{2,1,0:T(8,128)(2,1)S(1)}, u32[]{:S(2)}, u32[]{:S(2)}) async-start(bf16[8,112,256]{2,1,0:T(8,128)(2,1)} %bitcast.8), calls=%async_computation.2 | async-start | bytes 917504 | tf_op jit(solution)/shard_map/sum_z/all_to_all | solution.py:21
  82.7 6.9 %collective-permute-start.8 = (bf16[8,16,512]{2,1,0:T(8,128)(2,1)S(1)}, bf16[8,16,512]{2,1,0:T(8,128)(2,1)S(1)}, u32[]{:S(2)}, u32[]{:S(2)}) collective-permute-start(bf16[8,16,512]{2,1,0:T(8,128)(2,1)S(1)} %convert_element_type.9), channel_id=1, source_target_pairs={{0,2},{2,0},{4,6},{6,4},{8,10},{10,8},{12,14},{14,12},{1,3},{3,1},... | collective-permute-start | bytes 393224 | tf_op jit(solution)/shard_map/panel_sum/ppermute | solution.py:26
  89.6 18.1 %collective-permute-start.9 = (f32[8,16,512]{2,1,0:T(8,128)S(1)}, f32[8,16,512]{2,1,0:T(8,128)S(1)}, u32[]{:S(2)}, u32[]{:S(2)}) collective-permute-start(f32[8,16,512]{2,1,0:T(8,128)S(1)} %convert_add_fusion), channel_id=1, source_target_pairs={{0,8},{2,10},{4,12},{6,14},{8,0},{10,2},{12,4},{14,6},{1,9},{3,11}... | collective-permute-start | bytes 786440 | tf_op jit(solution)/shard_map/panel_sum/ppermute | solution.py:26
  99.3 27.0 %all-to-all-start.3 = ((bf16[8,112,256]{2,1,0:T(8,128)(2,1)}), bf16[8,112,256]{2,1,0:T(8,128)(2,1)S(1)}, u32[]{:S(2)}, u32[]{:S(2)}) async-start(bf16[8,112,256]{2,1,0:T(8,128)(2,1)} %shard_map.60), calls=%async_computation.3 | async-start | bytes 917504 | tf_op jit(solution)/shard_map/rotated_z/all_to_all | solution.py:21
  107.8 15.2 %collective-permute-start.10 = (f32[8,16,512]{2,1,0:T(8,128)S(1)}, f32[8,16,512]{2,1,0:T(8,128)S(1)}, u32[]{:S(2)}, u32[]{:S(2)}) collective-permute-start(f32[8,16,512]{2,1,0:T(8,128)S(1)} %add.31), channel_id=1, source_target_pairs={{0,4},{2,6},{4,0},{6,2},{8,12},{10,14},{12,8},{14,10},{1,5},{3,7},... | collective-permute-start | bytes 786440 | tf_op jit(solution)/shard_map/panel_sum/ppermute | solution.py:26
  123.0 3.2 %collective-permute-start.11 = (bf16[8,16,512]{2,1,0:T(8,128)(2,1)S(1)}, bf16[8,16,512]{2,1,0:T(8,128)(2,1)S(1)}, u32[]{:S(2)}, u32[]{:S(2)}) collective-permute-start(bf16[8,16,512]{2,1,0:T(8,128)(2,1)S(1)} %add_convert_fusion.own_ref), channel_id=1, source_target_pairs={{0,1},{1,0},{2,3},{3,2},{4,5},{5,4},{6,7},{7,6},{8,9},{9,8},{10,11... | collective-permute-start | bytes 393224 | tf_op jit(solution)/shard_map/panel_c/ppermute | solution.py:26
